TPU v7x, 32 devices: a whole 2x2x4 slice. The times are simulated.
32 devices in a mesh: gx: 2 (over x), gy: 16 (over z, y, core).
Axes of the slice: x: 2, y: 2, z: 4, core: 2. Of those that a mesh axis runs over, the one named last changes fastest.
Arguments:
- node_feats: bfloat16 [8192, 512], P(('gx', 'gy')), may hold values from -6 to 6
- grad_out: bfloat16 [8192, 512], P(('gx', 'gy')), may hold values from -6 to 6
- log_sum_exp: float32 [8, 8192], P(None, ('gx', 'gy')), may hold values from 7.5 to 9
- w_query: bfloat16 [512, 512], replicated, may hold values from -0.25 to 0.25
- w_key: bfloat16 [512, 512], replicated, may hold values from -0.25 to 0.25
- w_value: bfloat16 [512, 512], replicated, may hold values from -0.25 to 0.25
- w_output: bfloat16 [512, 512], replicated, may hold values from -0.25 to 0.25
- partners: int32 [32, 3], replicated, may hold values from 0 to 31, as said below
Outputs:
- grad_nodes: bfloat16 [8192, 512], P(('gx', 'gy'))
- weight_grads: float32 [512, 2048], P('gx', 'gy')
Inputs may be any that keep to these rules, and one draw needn't show every extreme that they name: Row b holds three different blocks, none of them b, and partners[partners[b, j], j] = b for each column j: each column is a perfect matching of the 32 blocks.
All inputs are finite; a program needn't handle non-finite values.
Results may differ from a plain program's by a relative error of at most 0.019.
Values may be sent and summed in bfloat16 or wider, within the bound.
No kernel may reach another device: no remote copies, remote signals or barrier semaphores. Data moves between devices by JAX's collectives and lax.ppermute only.
A program may use at most 64 MiB of HBM per device.

v0:
```python
import jax
import jax.numpy as jnp
from jax import lax
from jax.sharding import PartitionSpec as P


def route_half(payload):
    return lax.all_to_all(
        lax.all_to_all(payload, "gx", split_axis=1, concat_axis=1, tiled=True),
        "gy",
        split_axis=2,
        concat_axis=2,
        tiled=True,
    )


def route_full(payload):
    return lax.all_to_all(
        lax.all_to_all(payload.astype(jnp.bfloat16), "gx", split_axis=1, concat_axis=1, tiled=True),
        "gy",
        split_axis=2,
        concat_axis=2,
        tiled=True,
    ).astype(payload.dtype)


def to_pieces(payload):
    n_outer = lax.axis_size("gx")
    n_inner = lax.axis_size("gy")
    rows = payload.shape[1]
    piece_len = rows // (n_outer * n_inner)
    return payload.reshape(payload.shape[0], n_outer, n_inner, piece_len, payload.shape[2])


def fetch_rows(payload, partners, router):
    lead, rows, cols = payload.shape
    blocks = partners.shape[0]
    piece_len = rows // blocks
    spread = router(to_pieces(payload)).reshape(lead, blocks, piece_len, cols)
    chosen = spread[:, partners.T]
    chosen = chosen.reshape(lead * 3, lax.axis_size("gx"), lax.axis_size("gy"), piece_len, cols)
    back = router(chosen)
    return back.reshape(lead, 3, rows, cols)


def return_terms(terms, partners):
    lead, rows, cols = terms.shape
    blocks = partners.shape[0]
    piece_len = rows // blocks
    spread = route_full(to_pieces(terms)).reshape(lead, blocks, piece_len, cols)
    chosen = jnp.stack([spread[match_idx][partners[:, match_idx]] for match_idx in range(3)])
    chosen = chosen.reshape(lead, lax.axis_size("gx"), lax.axis_size("gy"), piece_len, cols)
    back = route_full(chosen).reshape(lead, rows, cols)
    return jnp.sum(back, axis=0)


def attend(query, key_rows, value_rows, d_out, log_sum_exp, head_size, scaling):
    head_count = log_sum_exp.shape[0]
    grad_q_list, out_list, grad_k_list, grad_v_list, delta_list = ([], [], [], [], [])
    for head_idx in range(head_count):
        lo_col = head_idx * head_size
        hi_col = lo_col + head_size
        query_cols = query[:, lo_col:hi_col]
        key_cols = key_rows[:, lo_col:hi_col]
        value_cols = value_rows[:, lo_col:hi_col]
        dout_cols = d_out[:, lo_col:hi_col]
        scores = jnp.dot(query_cols, key_cols.T, preferred_element_type=jnp.float32) * scaling
        probs = jnp.exp(jnp.minimum(scores - log_sum_exp[head_idx][:, None], 0.0))
        probs_low = probs.astype(jnp.bfloat16)
        out_cols = jnp.dot(probs_low, value_cols, preferred_element_type=jnp.float32).astype(
            jnp.bfloat16
        )
        row_delta = jnp.sum(dout_cols.astype(jnp.float32) * out_cols.astype(jnp.float32), axis=-1)
        grad_probs = jnp.dot(dout_cols, value_cols.T, preferred_element_type=jnp.float32)
        grad_scores = (probs * (grad_probs - row_delta[:, None]) * scaling).astype(jnp.bfloat16)
        grad_q_list.append(
            jnp.dot(grad_scores, key_cols, preferred_element_type=jnp.float32).astype(jnp.bfloat16)
        )
        out_list.append(out_cols)
        grad_k_list.append(jnp.dot(grad_scores.T, query_cols, preferred_element_type=jnp.float32))
        grad_v_list.append(jnp.dot(probs_low.T, dout_cols, preferred_element_type=jnp.float32))
        delta_list.append(row_delta)
    return (
        jnp.concatenate(grad_q_list, axis=1),
        jnp.concatenate(out_list, axis=1),
        jnp.concatenate(grad_k_list, axis=1),
        jnp.concatenate(grad_v_list, axis=1),
        jnp.stack(delta_list),
    )


def on_device(node_feats, grad_out, log_sum_exp, w_query, w_key, w_value, w_output, partners):
    block_len, width = node_feats.shape
    head_count = log_sum_exp.shape[0]
    head_size = width // head_count
    scaling = head_size ** (-0.5)
    query = jnp.dot(node_feats, w_query, preferred_element_type=jnp.float32).astype(jnp.bfloat16)
    key_own = jnp.dot(node_feats, w_key, preferred_element_type=jnp.float32).astype(jnp.bfloat16)
    value_own = jnp.dot(node_feats, w_value, preferred_element_type=jnp.float32).astype(
        jnp.bfloat16
    )
    d_out = jnp.dot(grad_out, w_output.T, preferred_element_type=jnp.float32).astype(jnp.bfloat16)
    payload = jnp.concatenate([key_own, value_own], axis=1)[None]
    fetched = fetch_rows(payload, partners, route_half)[0]
    key_far = fetched[:, :, :width].reshape(3 * block_len, width)
    value_far = fetched[:, :, width : 2 * width].reshape(3 * block_len, width)
    key_rows = jnp.concatenate([key_own, key_far], axis=0)
    value_rows = jnp.concatenate([value_own, value_far], axis=0)
    grad_query, out_rows, grad_key_all, grad_value_all, row_delta = attend(
        query, key_rows, value_rows, d_out, log_sum_exp, head_size, scaling
    )
    terms = jnp.concatenate(
        [
            grad_key_all[block_len:].reshape(3, block_len, width),
            grad_value_all[block_len:].reshape(3, block_len, width),
        ],
        axis=2,
    )
    returned = return_terms(terms, partners)
    key_total = grad_key_all[:block_len] + returned[:, :width]
    value_total = grad_value_all[:block_len] + returned[:, width:]
    grad_key = key_total.astype(jnp.bfloat16)
    grad_value = value_total.astype(jnp.bfloat16)
    local_weights = jnp.concatenate(
        [
            jnp.dot(node_feats.T, grad_query, preferred_element_type=jnp.float32),
            jnp.dot(node_feats.T, grad_key, preferred_element_type=jnp.float32),
            jnp.dot(node_feats.T, grad_value, preferred_element_type=jnp.float32),
            jnp.dot(out_rows.T, grad_out, preferred_element_type=jnp.float32),
        ],
        axis=1,
    )
    partial_cols = lax.psum_scatter(
        local_weights.astype(jnp.bfloat16), "gy", scatter_dimension=1, tiled=True
    )
    weight_grads = lax.psum_scatter(partial_cols, "gx", scatter_dimension=0, tiled=True).astype(
        jnp.float32
    )
    total = jnp.dot(grad_query, w_query.T, preferred_element_type=jnp.float32)
    total = total + jnp.dot(grad_key, w_key.T, preferred_element_type=jnp.float32)
    total = total + jnp.dot(grad_value, w_value.T, preferred_element_type=jnp.float32)
    return (total.astype(jnp.bfloat16), weight_grads)


def solution(mesh):
    return jax.shard_map(
        on_device,
        mesh=mesh,
        in_specs=(
            P(("gx", "gy"), None),
            P(("gx", "gy"), None),
            P(None, ("gx", "gy")),
            P(),
            P(),
            P(),
            P(),
            P(),
        ),
        out_specs=(P(("gx", "gy"), None), P("gx", "gy")),
        check_vma=False,
    )
```

profile of v0, /device:TPU:0, one launch (start us, length us, event | category | flops | bytes accessed | tf_op | source)
XLA Modules:
  0.0 374.2 jit_solution(6133223120870284922)
XLA Ops:
  7.2 1.5 convolution_convert_fusion.5
  8.7 1.4 convolution_convert_fusion.6
  10.2 12.0 %all_to_all.40 = bf16[1,2,16,8,1024]{4,3,2,0,1:T(8,128)(2,1)S(1)} all-to-all(bf16[1,2,16,8,1024]{4,3,2,0,1:T(8,128)(2,1)S(1)} %bitcast.126), channel_id=1, replica_groups=mesh['gx'=2,'gy'=16] {'gx'}, dimensions={1} | all-to-all | bytes 1048576 | tf_op jit(solution)/shard_map/all_to_all | solution.py:9
  22.1 0.8 copy.86
  23.0 6.1 %all-to-all-start.1 = ((bf16[1,2,16,8,1024]{4,3,1,0,2:T(8,128)(2,1)}), bf16[1,2,16,8,1024]{4,3,1,0,2:T(8,128)(2,1)S(1)}, u32[]{:S(2)}, u32[]{:S(2)}) async-start(bf16[1,2,16,8,1024]{4,3,1,0,2:T(8,128)(2,1)} %copy.86), calls=%async_computation.1 | async-start | bytes 1048576 | tf_op jit(solution)/shard_map/all_to_all | solution.py:8
  29.2 14.4 %all-to-all-done.1 = bf16[1,2,16,8,1024]{4,3,1,0,2:T(8,128)(2,1)S(1)} async-done(((bf16[1,2,16,8,1024]{4,3,1,0,2:T(8,128)(2,1)}), bf16[1,2,16,8,1024]{4,3,1,0,2:T(8,128)(2,1)S(1)}, u32[]{:S(2)}, u32[]{:S(2)}) %all-to-all-start.1) | async-done | bytes 524320 | tf_op jit(solution)/shard_map/all_to_all | solution.py:8
  43.6 1.9 gather_fusion
  45.5 1.6 copy.88
  47.1 22.2 %all_to_all.41 = bf16[3,2,16,8,1024]{4,3,2,0,1:T(8,128)(2,1)S(1)} all-to-all(bf16[3,2,16,8,1024]{4,3,2,0,1:T(8,128)(2,1)S(1)} %copy.88), channel_id=1, replica_groups=mesh['gx'=2,'gy'=16] {'gx'}, dimensions={1} | all-to-all | bytes 3145728 | tf_op jit(solution)/shard_map/all_to_all | solution.py:9
  69.3 1.3 copy.89
  70.6 4.6 %all-to-all-start.3 = ((bf16[3,2,16,8,1024]{4,3,1,0,2:T(8,128)(2,1)}), bf16[3,2,16,8,1024]{4,3,1,0,2:T(8,128)(2,1)}, u32[]{:S(2)}, u32[]{:S(2)}) async-start(bf16[3,2,16,8,1024]{4,3,1,0,2:T(8,128)(2,1)} %copy.89), calls=%async_computation.3 | async-start | bytes 3145728 | tf_op jit(solution)/shard_map/all_to_all | solution.py:8
  75.2 1.0 convolution_convert_fusion.7
  76.5 30.6 %all-to-all-done.3 = bf16[3,2,16,8,1024]{4,3,1,0,2:T(8,128)(2,1)} async-done(((bf16[3,2,16,8,1024]{4,3,1,0,2:T(8,128)(2,1)}), bf16[3,2,16,8,1024]{4,3,1,0,2:T(8,128)(2,1)}, u32[]{:S(2)}, u32[]{:S(2)}) %all-to-all-start.3) | async-done | bytes 1572896 | tf_op jit(solution)/shard_map/all_to_all | solution.py:8
  107.2 1.5 copy.90
  109.1 1.3 fusion.39
  110.7 1.3 fusion.34
  112.4 1.2 fusion.29
  113.9 1.3 fusion.24
  115.6 1.2 fusion.19
  117.1 1.3 fusion.14
  118.8 1.2 fusion.9
  121.4 1.0 multiply_reduce_fusion
  122.5 1.1 fusion.40
  123.6 1.3 fusion.41
  124.8 1.2 fusion.42
  126.0 1.2 fusion.43
  127.2 1.1 fusion.44
  128.3 1.2 fusion.45
  129.8 1.1 fusion.47
  133.0 1.3 copy-done.26
  134.3 1.0 slice.507
  135.3 2.4 copy.100
  137.7 1.4 convolution_dynamic-update-slice_fusion.15
  139.1 1.3 convolution_dynamic-update-slice_fusion.14
  140.4 1.3 convolution_dynamic-update-slice_fusion.13
  143.3 1.3 copy-done.25
  144.7 1.2 copy.99
  145.9 1.3 pad_maximum_fusion.1
  147.4 22.9 %all_to_all.42 = bf16[3,2,16,8,1024]{4,3,2,0,1:T(8,128)(2,1)S(1)} all-to-all(bf16[3,2,16,8,1024]{4,3,2,0,1:T(8,128)(2,1)S(1)} %copy.101), channel_id=1, replica_groups=mesh['gx'=2,'gy'=16] {'gx'}, dimensions={1} | all-to-all | bytes 3145728 | tf_op jit(solution)/shard_map/all_to_all | solution.py:19
  170.3 1.3 copy.102
  171.7 8.6 %all-to-all-start.5 = ((bf16[3,2,16,8,1024]{4,3,1,0,2:T(8,128)(2,1)}), bf16[3,2,16,8,1024]{4,3,1,0,2:T(8,128)(2,1)S(1)}, u32[]{:S(2)}, u32[]{:S(2)}) async-start(bf16[3,2,16,8,1024]{4,3,1,0,2:T(8,128)(2,1)} %copy.102), calls=%async_computation.5 | async-start | bytes 3145728 | tf_op jit(solution)/shard_map/all_to_all | solution.py:18
  180.3 31.9 %all-to-all-done.5 = bf16[3,2,16,8,1024]{4,3,1,0,2:T(8,128)(2,1)S(1)} async-done(((bf16[3,2,16,8,1024]{4,3,1,0,2:T(8,128)(2,1)}), bf16[3,2,16,8,1024]{4,3,1,0,2:T(8,128)(2,1)S(1)}, u32[]{:S(2)}, u32[]{:S(2)}) %all-to-all-start.5) | async-done | bytes 1572896 | tf_op jit(solution)/shard_map/all_to_all | solution.py:18
  212.6 1.4 gather_fusion.3
  214.0 1.4 gather_fusion.2
  215.4 0.6 gather_fusion.1
  215.9 1.2 pad_maximum_fusion.2
  217.2 22.9 %all_to_all.43 = bf16[3,2,16,8,1024]{4,3,2,0,1:T(8,128)(2,1)S(1)} all-to-all(bf16[3,2,16,8,1024]{4,3,2,0,1:T(8,128)(2,1)S(1)} %pad_maximum_fusion.2), channel_id=1, replica_groups=mesh['gx'=2,'gy'=16] {'gx'}, dimensions={1} | all-to-all | bytes 3145728 | tf_op jit(solution)/shard_map/all_to_all | solution.py:19
  240.1 1.3 copy.109
  241.4 8.8 %all-to-all-start.7 = ((bf16[3,2,16,8,1024]{4,3,1,0,2:T(8,128)(2,1)}), bf16[3,2,16,8,1024]{4,3,1,0,2:T(8,128)(2,1)}, u32[]{:S(2)}, u32[]{:S(2)}) async-start(bf16[3,2,16,8,1024]{4,3,1,0,2:T(8,128)(2,1)} %copy.109), calls=%async_computation.7 | async-start | bytes 3145728 | tf_op jit(solution)/shard_map/all_to_all | solution.py:18
  250.3 1.9 concatenate.45
  252.5 0.4 fusion.58
  253.3 0.4 fusion.56
  254.1 0.4 fusion.54
  255.9 1.1 fusion.48
  257.0 25.3 %all-to-all-done.7 = bf16[3,2,16,8,1024]{4,3,1,0,2:T(8,128)(2,1)} async-done(((bf16[3,2,16,8,1024]{4,3,1,0,2:T(8,128)(2,1)}), bf16[3,2,16,8,1024]{4,3,1,0,2:T(8,128)(2,1)}, u32[]{:S(2)}, u32[]{:S(2)}) %all-to-all-start.7) | async-done | bytes 1572896 | tf_op jit(solution)/shard_map/all_to_all | solution.py:18
  282.3 1.9 convert_reduce_fusion
  284.5 1.1 fusion.61
  285.8 1.1 fusion.60
  287.5 1.5 pad_maximum_fusion
  289.1 0.9 copy-done.24
  290.7 63.6 %reduce-scatter.3.cloned.1.call-done = bf16[512,128]{0,1:T(8,128)(2,1)} async-done(((bf16[512,2048]{0,1:T(8,128)(2,1)}), bf16[512,128]{0,1:T(8,128)(2,1)}) %reduce-scatter.3.cloned.1.call-update) | async-done | bytes 131088 | tf_op jit(solution)/shard_map/reduce_scatter | solution.py:133
  354.3 1.1 fusion.51
  355.3 10.5 %reduce-scatter.5.cloned.1.call-done = bf16[256,128]{0,1:T(8,128)(2,1)} async-done(((bf16[512,128]{0,1:T(8,128)(2,1)}), bf16[256,128]{0,1:T(8,128)(2,1)}) %reduce-scatter.5.cloned.1.call-update) | async-done | bytes 65552 | tf_op jit(solution)/shard_map/reduce_scatter | solution.py:136
  365.8 1.6 copy.113
  (132 shorter events, 12.8 us)
Async XLA Ops:
  7.2 68.0 %copy-start = (bf16[512,512]{1,0:T(8,128)(2,1)S(1)}, bf16[512,512]{1,0:T(8,128)(2,1)}, u32[]{:S(2)}) copy-start(bf16[512,512]{1,0:T(8,128)(2,1)} %param.11) | copy-start | bytes 1572868
  10.1 19.0 %copy-start.37 = (s32[32,3]{0,1:T(4,128)S(1)}, s32[32,3]{0,1:T(4,128)}, u32[]{:S(2)}) copy-start(s32[32,3]{0,1:T(4,128)} %param.15) | copy-start | bytes 1156
  23.0 20.5 %all-to-all-start.1 = ((bf16[1,2,16,8,1024]{4,3,1,0,2:T(8,128)(2,1)}), bf16[1,2,16,8,1024]{4,3,1,0,2:T(8,128)(2,1)S(1)}, u32[]{:S(2)}, u32[]{:S(2)}) async-start(bf16[1,2,16,8,1024]{4,3,1,0,2:T(8,128)(2,1)} %copy.86), calls=%async_computation.1 | async-start | bytes 1048576 | tf_op jit(solution)/shard_map/all_to_all | solution.py:8
  70.6 4.6 %copy-start.36 = (f32[8,256]{1,0:T(8,128)S(1)}, f32[8,256]{1,0:T(8,128)}, u32[]{:S(2)}) copy-start(f32[8,256]{1,0:T(8,128)} %param.10) | copy-start | bytes 24580
  70.6 4.6 %copy-start.1 = (bf16[256,512]{1,0:T(8,128)(2,1)S(1)}, bf16[256,512]{1,0:T(8,128)(2,1)}, u32[]{:S(2)}) copy-start(bf16[256,512]{1,0:T(8,128)(2,1)} %param.8) | copy-start | bytes 786436
  70.6 5.6 %copy-start.28 = (bf16[256,512]{1,0:T(8,128)(2,1)S(1)}, bf16[256,512]{1,0:T(8,128)(2,1)}, u32[]{:S(2)}) copy-start(bf16[256,512]{1,0:T(8,128)(2,1)} %param.9) | copy-start | bytes 786436
  70.6 5.6 %copy-start.35 = (bf16[512,512]{1,0:T(8,128)(2,1)S(1)}, bf16[512,512]{1,0:T(8,128)(2,1)}, u32[]{:S(2)}) copy-start(bf16[512,512]{1,0:T(8,128)(2,1)} %param.14) | copy-start | bytes 1572868
  70.6 36.6 %all-to-all-start.3 = ((bf16[3,2,16,8,1024]{4,3,1,0,2:T(8,128)(2,1)}), bf16[3,2,16,8,1024]{4,3,1,0,2:T(8,128)(2,1)}, u32[]{:S(2)}, u32[]{:S(2)}) async-start(bf16[3,2,16,8,1024]{4,3,1,0,2:T(8,128)(2,1)} %copy.89), calls=%async_computation.3 | async-start | bytes 3145728 | tf_op jit(solution)/shard_map/all_to_all | solution.py:8
  109.1 11.5 %copy-start.17 = (bf16[1024,64]{1,0:T(8,128)(2,1)}, bf16[1024,64]{1,0:T(8,128)(2,1)S(1)}, u32[]{:S(2)}) copy-start(bf16[1024,64]{1,0:T(8,128)(2,1)S(1)} %pad_maximum_fusion.5) | copy-start | bytes 393220
  113.9 7.5 %copy-start.30 = (bf16[256,64]{1,0:T(8,128)(2,1)}, bf16[256,64]{1,0:T(8,128)(2,1)S(1)}, u32[]{:S(2)}) copy-start(bf16[256,64]{1,0:T(8,128)(2,1)S(1)} %convolution_convert_fusion.13) | copy-start | bytes 98308
  115.6 5.8 %copy-start.31 = (bf16[256,64]{1,0:T(8,128)(2,1)}, bf16[256,64]{1,0:T(8,128)(2,1)S(1)}, u32[]{:S(2)}) copy-start(bf16[256,64]{1,0:T(8,128)(2,1)S(1)} %convolution_convert_fusion.12) | copy-start | bytes 98308
  117.1 4.3 %copy-start.32 = (bf16[256,64]{1,0:T(8,128)(2,1)}, bf16[256,64]{1,0:T(8,128)(2,1)S(1)}, u32[]{:S(2)}) copy-start(bf16[256,64]{1,0:T(8,128)(2,1)S(1)} %convolution_convert_fusion.11) | copy-start | bytes 98308
  118.8 2.6 copy-start.33
  120.0 1.0 copy-start.2
  120.3 2.1 copy-start.34
  129.8 12.9 %copy-start.3 = (bf16[256,1024]{1,0:T(8,128)(2,1)}, bf16[256,1024]{1,0:T(8,128)(2,1)S(1)}, u32[]{:S(2)}) copy-start(bf16[256,1024]{1,0:T(8,128)(2,1)S(1)} %fusion.46) | copy-start | bytes 1572868
  133.0 1.3 copy-start.26
  135.3 6.8 %copy-start.9 = (bf16[256,1024]{1,0:T(8,128)(2,1)S(1)}, bf16[256,1024]{1,0:T(8,128)(2,1)}, u32[]{:S(2)}) copy-start(bf16[256,1024]{1,0:T(8,128)(2,1)} %fusion.44) | copy-start | bytes 1572868
  137.7 4.1 %copy-start.11 = (bf16[256,1024]{1,0:T(8,128)(2,1)S(1)}, bf16[256,1024]{1,0:T(8,128)(2,1)}, u32[]{:S(2)}) copy-start(bf16[256,1024]{1,0:T(8,128)(2,1)} %fusion.43) | copy-start | bytes 1572868
  137.7 4.7 %copy-start.7 = (bf16[256,1024]{1,0:T(8,128)(2,1)S(1)}, bf16[256,1024]{1,0:T(8,128)(2,1)}, u32[]{:S(2)}) copy-start(bf16[256,1024]{1,0:T(8,128)(2,1)} %fusion.45) | copy-start | bytes 1572868
  140.4 2.5 copy-start.5
  143.0 2.9 copy-start.16
  143.3 1.3 copy-start.25
  171.7 40.6 %all-to-all-start.5 = ((bf16[3,2,16,8,1024]{4,3,1,0,2:T(8,128)(2,1)}), bf16[3,2,16,8,1024]{4,3,1,0,2:T(8,128)(2,1)S(1)}, u32[]{:S(2)}, u32[]{:S(2)}) async-start(bf16[3,2,16,8,1024]{4,3,1,0,2:T(8,128)(2,1)} %copy.102), calls=%async_computation.5 | async-start | bytes 3145728 | tf_op jit(solution)/shard_map/all_to_all | solution.py:18
  214.0 2.0 copy-start.21
  241.4 10.8 %copy-start.13 = (bf16[256,1024]{1,0:T(8,128)(2,1)S(1)}, bf16[256,1024]{1,0:T(8,128)(2,1)}, u32[]{:S(2)}) copy-start(bf16[256,1024]{1,0:T(8,128)(2,1)} %fusion.40) | copy-start | bytes 1572868
  241.4 11.1 %copy-start.15 = (bf16[256,1024]{1,0:T(8,128)(2,1)S(1)}, bf16[256,1024]{1,0:T(8,128)(2,1)}, u32[]{:S(2)}) copy-start(bf16[256,1024]{1,0:T(8,128)(2,1)} %fusion.41) | copy-start | bytes 1572868
  241.4 40.9 %all-to-all-start.7 = ((bf16[3,2,16,8,1024]{4,3,1,0,2:T(8,128)(2,1)}), bf16[3,2,16,8,1024]{4,3,1,0,2:T(8,128)(2,1)}, u32[]{:S(2)}, u32[]{:S(2)}) async-start(bf16[3,2,16,8,1024]{4,3,1,0,2:T(8,128)(2,1)} %copy.109), calls=%async_computation.7 | async-start | bytes 3145728 | tf_op jit(solution)/shard_map/all_to_all | solution.py:18
  250.2 2.7 copy-start.14
  250.2 104.0 %reduce-scatter.3.cloned.1.call-start = ((), (), s32[]{:S(2)}) async-start(), calls=%async_computation.10 | async-start | bytes 2228224 | tf_op jit(solution)/shard_map/reduce_scatter | solution.py:133
  252.2 1.0 copy-start.12
  252.5 1.2 copy-start.10
  253.0 1.1 copy-start.8
  253.3 1.3 copy-start.4
  253.7 1.1 copy-start.6
  253.7 1.2 copy-start.18
  254.1 1.1 copy-start.27
  254.1 1.1 copy-start.29
  255.2 0.7 copy-start.23
  285.6 1.9 copy-start.22
  289.0 0.9 copy-start.24
  289.0 1.3 copy-start.19
  289.0 65.2 %copy-start.20 = (bf16[512,512]{1,0:T(8,128)(2,1)S(1)}, bf16[512,512]{1,0:T(8,128)(2,1)}, u32[]{:S(2)}) copy-start(bf16[512,512]{1,0:T(8,128)(2,1)} %param.13) | copy-start | bytes 1572868
  289.0 76.7 %reduce-scatter.5.cloned.1.call-start = ((), (), s32[]{:S(2)}) async-start(), calls=%async_computation.11 | async-start | bytes 196608 | tf_op jit(solution)/shard_map/reduce_scatter | solution.py:136
Sparse Core Ops, SparseCore 0:
  289.1 65.0 reduce-scatter.2
  356.5 9.2 reduce-scatter.4
where the time goes:
time: 376 us; the launch traced here: 374 us
  waiting for transfers between devices  176 us (47%)
  blocking collectives  80 us (21%)
  matrix products  39.4 us (10%)
  starting transfers between devices  28.2 us (8%)
  local copies, waits for them, and re-layouts  27 us (7%)
  between operations  14.9 us (4%)
  other arithmetic  8.42 us (2%)
    reduce_scatter x1, waiting for transfers between devices, on_device(): lax.psum_scatter(local_weights.astype(jnp.bfloat16), 'gy', scatter_dimens...  63.6 us
    all_to_all x2, waiting for transfers between devices, route_full(): lax.all_to_all(lax.all_to_all(payload.astype(jnp.bfloat16), 'gx', split_a...  57.2 us
    all_to_all x2, blocking collectives, route_full(): lax.all_to_all(payload.astype(jnp.bfloat16), 'gx', split_axis=1, concat_a...  45.9 us
    all_to_all x2, waiting for transfers between devices, route_half(): lax.all_to_all(lax.all_to_all(payload, 'gx', split_axis=1, concat_axis=1,...  45 us
    all_to_all x2, blocking collectives, route_half(): lax.all_to_all(payload, 'gx', split_axis=1, concat_axis=1, tiled=True)  34.2 us
    all_to_all x2, starting transfers between devices, route_full(): lax.all_to_all(lax.all_to_all(payload.astype(jnp.bfloat16), 'gx', split_a...  17.5 us
    all_to_all x2, starting transfers between devices, route_half(): lax.all_to_all(lax.all_to_all(payload, 'gx', split_axis=1, concat_axis=1,...  10.6 us
    reduce_scatter x1, waiting for transfers between devices, on_device(): lax.psum_scatter(partial_cols, 'gx', scatter_dimension=0, tiled=True)  10.5 us
  transfers between devices with their start and end apart: 6, of which 6 were waited for; matrix products, arithmetic and copies ran while one was open for 2% of the time, Pallas kernels for 0%

commit v1 on v0

v1 whole, which is shorter than its diff:
```python
import functools
import math

import jax
import jax.numpy as jnp
from jax import lax
from jax.experimental import pallas as pl
from jax.experimental.pallas import tpu as pltpu
from jax.sharding import PartitionSpec as P

AXES = ("gx", "gy")
LOW = jnp.bfloat16
WIDE = jnp.float32


def dot(left, right):
    return jnp.dot(left, right, preferred_element_type=WIDE)


def dot_nt(left, right):
    return lax.dot_general(left, right, (((1,), (1,)), ((), ())), preferred_element_type=WIDE)


def exchange(pieces):
    return lax.all_to_all(pieces, AXES, split_axis=0, concat_axis=0, tiled=True)


def attention_kernel(
    head_size,
    group,
    far_ref,
    key_own_ref,
    value_own_ref,
    key_own_t_ref,
    value_own_t_ref,
    query_t_ref,
    d_out_t_ref,
    query_ref,
    d_out_ref,
    lse_ref,
    w_key_ref,
    w_value_ref,
    w_key_t_ref,
    w_value_t_ref,
    w_query_t_ref,
    terms_ref,
    own_ref,
    grad_query_t_ref,
    out_t_ref,
    grad_key_ref,
    grad_value_ref,
    key_ref,
    value_ref,
    key_t_ref,
    value_t_ref,
):
    heads = lse_ref.shape[0]
    block = query_ref.shape[0]
    scaling = head_size ** (-0.5)
    log2e = math.log2(math.e)
    far = far_ref[...]
    key_ref[:block] = key_own_ref[...]
    value_ref[:block] = value_own_ref[...]
    key_t_ref[:, :block] = key_own_t_ref[...]
    value_t_ref[:, :block] = value_own_t_ref[...]
    key_ref[block:] = dot(far, w_key_ref[...]).astype(LOW)
    value_ref[block:] = dot(far, w_value_ref[...]).astype(LOW)
    key_t_ref[:, block:] = dot_nt(w_key_t_ref[...], far).astype(LOW)
    value_t_ref[:, block:] = dot_nt(w_value_t_ref[...], far).astype(LOW)
    span = group * head_size
    for first in range(0, heads, group):
        cols = slice(first * head_size, first * head_size + span)
        key = key_ref[:, cols]
        value = value_ref[:, cols]
        row = lax.broadcasted_iota(jnp.int32, (span, block), 0) // head_size
        col = lax.broadcasted_iota(jnp.int32, (block, span), 1) // head_size
        query_t = query_t_ref[cols, :]
        d_out_t = d_out_t_ref[cols, :]
        query = query_ref[:, cols]
        d_out = d_out_ref[:, cols]
        zero_t = jnp.zeros_like(query_t)
        zero = jnp.zeros_like(query)
        grad_key = None
        grad_value = None
        for inner in range(group):
            head = first + inner
            rows = slice(head * head_size, (head + 1) * head_size)
            score = dot(key, jnp.where(row == inner, query_t, zero_t))
            shift = lse_ref[head : head + 1, :] * log2e
            prob = jnp.exp2(jnp.minimum(score * (scaling * log2e) - shift, 0.0))
            prob_low = prob.astype(LOW)
            out_t = dot(value_t_ref[rows, :], prob_low).astype(LOW)
            out_t_ref[rows, :] = out_t
            d_rows = d_out_t_ref[rows, :]
            delta = jnp.sum(d_rows.astype(WIDE) * out_t.astype(WIDE), axis=0, keepdims=True) * scaling
            grad_prob = dot(value, jnp.where(row == inner, d_out_t * scaling, zero_t))
            grad_score = (prob * (grad_prob - delta)).astype(LOW)
            grad_query_t_ref[rows, :] = dot(key_t_ref[rows, :], grad_score).astype(LOW)
            part_key = dot(grad_score, jnp.where(col == inner, query, zero))
            part_value = dot(prob_low, jnp.where(col == inner, d_out, zero))
            grad_key = part_key if grad_key is None else grad_key + part_key
            grad_value = part_value if grad_value is None else grad_value + part_value
        grad_key_ref[:, cols] = grad_key.astype(LOW)
        grad_value_ref[:, cols] = grad_value.astype(LOW)
    total = dot(grad_key_ref[...], w_key_t_ref[...]) + dot(grad_value_ref[...], w_value_t_ref[...])
    terms_ref[...] = total[block:].astype(LOW)
    own_ref[...] = total[:block] + lax.dot_general(
        grad_query_t_ref[...],
        w_query_t_ref[...],
        (((0,), (0,)), ((), ())),
        preferred_element_type=WIDE,
    )


def attention(head_size, block, width, heads, *operands):
    members = 4 * block
    group = max(1, 128 // head_size)
    return pl.pallas_call(
        functools.partial(attention_kernel, head_size, group),
        out_shape=(
            jax.ShapeDtypeStruct((3 * block, width), LOW),
            jax.ShapeDtypeStruct((block, width), WIDE),
            jax.ShapeDtypeStruct((width, block), LOW),
            jax.ShapeDtypeStruct((width, block), LOW),
            jax.ShapeDtypeStruct((members, width), LOW),
            jax.ShapeDtypeStruct((members, width), LOW),
        ),
        in_specs=[pl.BlockSpec(memory_space=pltpu.VMEM)] * len(operands),
        out_specs=(pl.BlockSpec(memory_space=pltpu.VMEM),) * 6,
        scratch_shapes=[
            pltpu.VMEM((members, width), LOW),
            pltpu.VMEM((members, width), LOW),
            pltpu.VMEM((width, members), LOW),
            pltpu.VMEM((width, members), LOW),
        ],
        compiler_params=pltpu.CompilerParams(vmem_limit_bytes=48 * 1024 * 1024),
        cost_estimate=pl.CostEstimate(
            flops=12 * block * members * width + 8 * members * width * width,
            bytes_accessed=16 * members * width,
            transcendentals=heads * block * members,
        ),
    )(*operands)


def bits_of(count):
    return [1 << position for position in range(count.bit_length() - 1)]


def halve(parts, axis, mask, me, devices):
    mine = jnp.where((me & mask) != 0, 1, 0)
    send = lax.dynamic_index_in_dim(parts, 1 - mine, axis, keepdims=False)
    keep = lax.dynamic_index_in_dim(parts, mine, axis, keepdims=False)
    got = lax.ppermute(send, AXES, [(device, device ^ mask) for device in range(devices)])
    return (keep.astype(WIDE) + got.astype(WIDE)).astype(LOW)


def scatter_sum(partial):
    n_outer = lax.axis_size("gx")
    n_inner = lax.axis_size("gy")
    devices = n_outer * n_inner
    me = lax.axis_index("gx") * n_inner + lax.axis_index("gy")
    rows, cols = partial.shape
    outer = [mask * n_inner for mask in bits_of(n_outer)]
    inner = bits_of(n_inner)
    blocks = partial.reshape(n_outer, rows // n_outer, n_inner, cols // n_inner)
    blocks = blocks.transpose(0, 2, 1, 3)
    high_first = outer[::-1] + inner[::-1]
    half = rows // n_outer // 2
    orders = (
        inner[:1] + outer + inner[1:2] + inner[2:],
        inner[:1] + inner[1:2] + outer + inner[2:],
    )
    results = []
    for part, order in enumerate(orders):
        piece = blocks[:, :, part * half : (part + 1) * half]
        piece = piece.reshape((2,) * len(high_first) + (half, cols // n_inner))
        left = list(high_first)
        for mask in order:
            piece = halve(piece, left.index(mask), mask, me, devices)
            left.remove(mask)
        results.append(piece)
    return jnp.concatenate(results, axis=0).astype(WIDE)


def on_device(node_feats, grad_out, log_sum_exp, w_query, w_key, w_value, w_output, partners):
    block, width = node_feats.shape
    heads = log_sum_exp.shape[0]
    head_size = width // heads
    devices = partners.shape[0]
    piece = block // devices
    spread = exchange(node_feats.reshape(devices, piece, width))
    chosen = spread[partners]
    arrived = exchange(chosen)
    far = arrived.transpose(1, 0, 2, 3).reshape(3 * block, width)

    w_query_t, w_key_t, w_value_t = w_query.T, w_key.T, w_value.T
    query = dot(node_feats, w_query).astype(LOW)
    query_t = dot_nt(w_query_t, node_feats).astype(LOW)
    key_own = dot(node_feats, w_key).astype(LOW)
    key_own_t = dot_nt(w_key_t, node_feats).astype(LOW)
    value_own = dot(node_feats, w_value).astype(LOW)
    value_own_t = dot_nt(w_value_t, node_feats).astype(LOW)
    d_out = dot_nt(grad_out, w_output).astype(LOW)
    d_out_t = dot_nt(w_output, grad_out).astype(LOW)

    terms, own, grad_query_t, out_t, grad_key, grad_value = attention(
        head_size,
        block,
        width,
        heads,
        far,
        key_own,
        value_own,
        key_own_t,
        value_own_t,
        query_t,
        d_out_t,
        query,
        d_out,
        log_sum_exp,
        w_key,
        w_value,
        w_key_t,
        w_value_t,
        w_query_t,
    )

    returned = exchange(terms.reshape(3, devices, piece, width).transpose(1, 0, 2, 3))
    summed = sum(returned[partners[:, match], match].astype(WIDE) for match in range(3))
    back = exchange(summed.astype(LOW)).reshape(block, width)
    grad_nodes = (own + back.astype(WIDE)).astype(LOW)

    feats_all = jnp.concatenate([node_feats, far], axis=0)
    partial = jnp.concatenate(
        [
            dot_nt(node_feats.T, grad_query_t),
            dot(feats_all.T, grad_key),
            dot(feats_all.T, grad_value),
            dot(out_t, grad_out),
        ],
        axis=1,
    ).astype(LOW)
    return grad_nodes, scatter_sum(partial)


def solution(mesh):
    return jax.shard_map(
        on_device,
        mesh=mesh,
        in_specs=(
            P(AXES, None),
            P(AXES, None),
            P(None, AXES),
            P(),
            P(),
            P(),
            P(),
            P(),
        ),
        out_specs=(P(AXES, None), P("gx", "gy")),
        check_vma=False,
    )
```

time: 376 us -> 138 us (0.37)
  waiting for transfers between devices: 176 us -> 42.4 us
  blocking collectives: 80 us -> 0 us
  matrix products: 39.4 us -> 13.3 us
  between operations: 14.9 us -> 1.03 us
  Pallas kernels: 0 us -> 13.5 us
    all_to_all x4 -> x0, blocking collectives: 80 us -> none  [the longest x2 45.9 us: route_full(): lax.all_to_all(payload.astype(jnp.bfloat16), 'gx', split_axis=1, concat_a...]
    all_to_all x4, waiting for transfers between devices: 102 us -> 28 us  [exchange(): return lax.all_to_all(pieces, AXES, split_axis=0, concat_axis=0, tiled=True)]
    reduce_scatter x2 -> x0, waiting for transfers between devices: 74 us -> none  [the longest x1 63.6 us: on_device(): lax.psum_scatter(local_weights.astype(jnp.bfloat16), 'gy', scatter_dimens...]
    dot_general x59 -> x12, matrix products: 39.4 us -> 13.3 us  [the longest x6 7.77 us: dot(): return jnp.dot(left, right, preferred_element_type=WIDE)]
    ppermute x0 -> x10, waiting for transfers between devices: none -> 14.4 us  [halve(): lax.ppermute(send, AXES, [(device, device ^ mask) for device in range(dev...]
    pallas_call x0 -> x1, Pallas kernels: none -> 13.5 us  [attention(): pl.pallas_call(functools.partial(attention_kernel, head_size, group), out...]
    ppermute x0 -> x10, starting transfers between devices: none -> 13.4 us  [halve(): lax.ppermute(send, AXES, [(device, device ^ mask) for device in range(dev...]
    all_to_all x4, starting transfers between devices: 28.1 us -> 17 us  [exchange(): return lax.all_to_all(pieces, AXES, split_axis=0, concat_axis=0, tiled=True)]
  transfers between devices with their start and end apart: 6 -> 14, of which waited for: 6 -> 6; matrix products, arithmetic and copies ran while one was open for 2% -> 17% of each run, Pallas kernels for 0% -> 0%
where the time goes in v1:
time: 138 us; the launch traced here: 137 us
  waiting for transfers between devices  42.4 us (31%)
  starting transfers between devices  30.4 us (22%)
  local copies, waits for them, and re-layouts  30.2 us (22%)
  Pallas kernels  13.5 us (10%)
  matrix products  13.3 us (10%)
  other arithmetic  5.75 us (4%)
    all_to_all x4, waiting for transfers between devices, exchange(): return lax.all_to_all(pieces, AXES, split_axis=0, concat_axis=0, tiled=True)  28 us
    all_to_all x4, starting transfers between devices, exchange(): return lax.all_to_all(pieces, AXES, split_axis=0, concat_axis=0, tiled=True)  17 us
    ppermute x10, waiting for transfers between devices, halve(): lax.ppermute(send, AXES, [(device, device ^ mask) for device in range(dev...  14.4 us
    pallas_call x1, Pallas kernels, attention(): pl.pallas_call(functools.partial(attention_kernel, head_size, group), out...  13.5 us
    ppermute x10, starting transfers between devices, halve(): lax.ppermute(send, AXES, [(device, device ^ mask) for device in range(dev...  13.4 us
    unnamed x47, local copies, waits for them, and re-layouts  11.3 us
    dot_general x6, matrix products, dot(): return jnp.dot(left, right, preferred_element_type=WIDE)  7.77 us
    convert_element_type x2, local copies, waits for them, and re-layouts, on_device(): partial = jnp.concatenate([dot_nt(node_feats.T, grad_query_t), dot(feats_...  6.92 us
  transfers between devices with their start and end apart: 14, of which 6 were waited for; matrix products, arithmetic and copies ran while one was open for 17% of the time, Pallas kernels for 0%

profile of v1, /device:TPU:0, one launch (start us, length us, event | category | flops | bytes accessed | tf_op | source)
XLA Modules:
  0.0 136.7 jit_solution(3084680715751185289)
XLA Ops:
  0.6 7.3 %all-to-all-start = ((bf16[32,8,512]{2,1,0:T(8,128)(2,1)}), bf16[32,8,512]{2,1,0:T(8,128)(2,1)S(1)}, u32[]{:S(2)}, u32[]{:S(2)}) async-start(bf16[32,8,512]{2,1,0:T(8,128)(2,1)} %bitcast.105), calls=%async_computation | async-start | bytes 524288 | tf_op jit(solution)/shard_map/all_to_all | solution.py:25
  8.0 0.7 compare_select_fusion
  8.9 1.5 %convolution_convert_fusion.10.value_own_ref = bf16[256,512]{1,0:T(8,128)(2,1)S(1)} fusion(bf16[256,512]{1,0:T(8,128)(2,1)} %param.8, bf16[512,512]{1,0:T(8,128)(2,1)} %w_value_ref.1), kind=kOutput, calls=%fused_computation.16 | convolution fusion | flops 134348800 | bytes 1048576 | tf_op jit(solution)/shard_map/dot_general | solution.py:17
  10.4 7.9 %all-to-all-done = bf16[32,8,512]{2,1,0:T(8,128)(2,1)S(1)} async-done(((bf16[32,8,512]{2,1,0:T(8,128)(2,1)}), bf16[32,8,512]{2,1,0:T(8,128)(2,1)S(1)}, u32[]{:S(2)}, u32[]{:S(2)}) %all-to-all-start) | async-done | bytes 262176 | tf_op jit(solution)/shard_map/all_to_all | solution.py:25
  18.2 1.5 %gather_fusion = bf16[96,8,512]{2,1,0:T(8,128)(2,1)} fusion(bf16[32,8,512]{2,1,0:T(8,128)(2,1)S(1)} %all-to-all-done, s32[1024]{0:T(1024)S(1)} %pad_clamp_fusion), kind=kCustom, calls=%fused_computation | custom fusion | bytes 1573248 | tf_op jit(solution)/shard_map/gather | solution.py:192
  19.8 3.5 %all-to-all-start.1 = ((bf16[32,3,8,512]{3,2,1,0:T(8,128)(2,1)}), bf16[32,3,8,512]{3,2,1,0:T(8,128)(2,1)}, u32[]{:S(2)}, u32[]{:S(2)}) async-start(bf16[32,3,8,512]{3,2,1,0:T(8,128)(2,1)} %bitcast.1), calls=%async_computation.1 | async-start | bytes 1572864 | tf_op jit(solution)/shard_map/all_to_all | solution.py:25
  23.3 1.0 convolution_convert_fusion.11.key_own_ref
  24.3 0.2 copy.24
  24.5 0.2 copy.25
  24.7 2.0 %copy.26 = bf16[512,512]{0,1:T(8,128)(2,1)} copy(bf16[512,512]{1,0:T(8,128)(2,1)} %param.11) | data formatting | bytes 1048576 | tf_op args[3]
  26.8 2.1 %convolution_convert_fusion.5.query_ref = bf16[256,512]{1,0:T(8,128)(2,1)} fusion(bf16[256,512]{1,0:T(8,128)(2,1)S(1)} %copy-done.12, bf16[512,512]{1,0:T(8,128)(2,1)} %param.11), kind=kOutput, calls=%fused_computation.11 | convolution fusion | flops 134348800 | bytes 1048576 | tf_op jit(solution)/shard_map/dot_general | solution.py:17
  28.9 1.0 convolution_convert_fusion.4.d_out_ref
  29.9 1.1 convolution_convert_fusion.6.d_out_t_ref
  31.0 1.1 convolution_convert_fusion.7.query_t_ref
  32.0 1.1 convolution_convert_fusion.8.value_own_t_ref
  33.1 1.1 convolution_convert_fusion.9.key_own_t_ref
  34.2 10.6 %all-to-all-done.1 = bf16[32,3,8,512]{3,2,1,0:T(8,128)(2,1)} async-done(((bf16[32,3,8,512]{3,2,1,0:T(8,128)(2,1)}), bf16[32,3,8,512]{3,2,1,0:T(8,128)(2,1)}, u32[]{:S(2)}, u32[]{:S(2)}) %all-to-all-start.1) | async-done | bytes 786464 | tf_op jit(solution)/shard_map/all_to_all | solution.py:25
  44.7 2.1 %copy.23 = bf16[3,32,8,512]{3,2,1,0:T(8,128)(2,1)} copy(bf16[3,32,8,512]{3,2,0,1:T(8,128)(2,1)} %bitcast.2) | data formatting | bytes 1572864 | tf_op jit(solution)/shard_map/transpose | solution.py:194
  46.8 1.0 copy-done.3
  47.9 0.9 copy-done.4
  48.8 0.9 copy-done.5
  49.8 0.9 copy-done.6
  50.7 0.9 copy-done.7
  51.7 0.9 copy-done.8
  52.6 0.9 copy-done.9
  53.6 0.9 copy-done.10
  54.5 13.5 %shard_map.95 = (bf16[768,512]{1,0:T(8,128)(2,1)}, f32[256,512]{1,0:T(8,128)S(1)}, bf16[512,256]{1,0:T(8,128)(2,1)S(1)}, bf16[512,256]{1,0:T(8,128)(2,1)S(1)}, b...) custom-call(bf16[768,512]{1,0:T(8,128)(2,1)} %bitcast.112, bf16[256,512]{1,0:T(8,128)(2,1)S(1)} %copy-done.4, ...), custom_call_target="tpu_custom_call" | custom-call | flops 3758096384 | bytes 8388608 | tf_op jit(solution)/shard_map/pallas_call | solution.py:118
  68.1 2.1 %convolution_convert_fusion.2 = bf16[512,512]{0,1:T(8,128)(2,1)S(1)} fusion(bf16[1024,512]{1,0:T(8,128)(2,1)} %get-tuple-element.12, bf16[768,512]{1,0:T(8,128)(2,1)S(1)} %bitcast.113, bf16[256,512]{1,0:T(8,128)(2,1)S(1)} %copy-done.13), kind=kOutput, calls=%fused_computation.7 | convolution fusion | flops 539230208 | bytes 2621440 | tf_op jit(solution)/shard_map/dot_general | solution.py:17
  70.2 0.8 convolution_convert_fusion.3
  70.9 0.2 copy-done.18
  71.1 0.3 convolution_convert_fusion
  71.5 0.3 fusion
  71.8 0.1 pad_maximum_fusion
  71.9 2.1 %convert_element_type.188 = bf16[2,256,16,128]{1,0,3,2:T(2,128)(2,1)} reshape(bf16[512,2048]{0,1:T(8,128)(2,1)S(1)} %pad_maximum_fusion) | data formatting | bytes 4194304 | tf_op jit(solution)/shard_map/convert_element_type | solution.py:242
  74.0 4.9 %copy.28 = bf16[2,256,16,128]{3,1,2,0:T(8,128)(2,1)S(1)} copy(bf16[2,256,16,128]{1,0,3,2:T(2,128)(2,1)} %convert_element_type.188) | data formatting | bytes 4194304 | tf_op jit(solution)/shard_map/convert_element_type | solution.py:242
  78.8 1.1 fusion.25
  79.9 0.9 copy-done.15
  80.9 0.8 dynamic-slice_bitcast_fusion
  81.7 1.3 constant_dynamic-slice_fusion.1
  83.0 0.8 copy.38
  83.8 0.5 collective-permute-start.5
  84.4 2.1 %copy.37 = bf16[3,32,8,512]{3,2,0,1:T(8,128)(2,1)} copy(bf16[3,32,8,512]{3,2,1,0:T(8,128)(2,1)} %bitcast.111) | data formatting | bytes 1572864 | tf_op jit(solution)/shard_map/reshape | solution.py:228
  86.5 2.6 %all-to-all-start.2 = ((bf16[32,3,8,512]{3,2,1,0:T(8,128)(2,1)}), bf16[32,3,8,512]{3,2,1,0:T(8,128)(2,1)S(1)}, u32[]{:S(2)}, u32[]{:S(2)}) async-start(bf16[32,3,8,512]{3,2,1,0:T(8,128)(2,1)} %bitcast.110), calls=%async_computation.2 | async-start | bytes 1572864 | tf_op jit(solution)/shard_map/all_to_all | solution.py:25
  89.1 1.2 fusion.2
  90.3 1.7 %collective-permute-start.1 = (bf16[2,2,2,128,128]{4,3,2,1,0:T(8,128)(2,1)S(1)}, bf16[2,2,2,128,128]{4,3,2,1,0:T(8,128)(2,1)S(1)}, u32[]{:S(2)}, u32[]{:S(2)}) collective-permute-start(bf16[2,2,2,128,128]{4,3,2,1,0:T(8,128)(2,1)S(1)} %dynamic-slice_bitcast_fusion.2), channel_id=1, source_target_pairs={{0,16},{1,17},{2,18},{3,19},{4,20},{5,21},{6,22},{7,23},{8,24},{9,... | collective-permute-start | bytes 786440 | tf_op jit(solution)/shard_map/ppermute | solution.py:153
  92.0 1.2 fusion.1
  93.3 1.6 %collective-permute-start.6 = (bf16[2,2,2,128,128]{4,3,1,2,0:T(8,128)(2,1)S(1)}, bf16[2,2,2,128,128]{4,3,1,2,0:T(8,128)(2,1)S(1)}, u32[]{:S(2)}, u32[]{:S(2)}) collective-permute-start(bf16[2,2,2,128,128]{4,3,1,2,0:T(8,128)(2,1)S(1)} %dynamic-slice_bitcast_fusion.1), channel_id=1, source_target_pairs={{0,2},{1,3},{2,0},{3,1},{4,6},{5,7},{6,4},{7,5},{8,10},{9,11},{10,... | collective-permute-start | bytes 786440 | tf_op jit(solution)/shard_map/ppermute | solution.py:153
  94.8 9.1 %collective-permute-done.1 = bf16[2,2,2,128,128]{4,3,2,1,0:T(8,128)(2,1)S(1)} collective-permute-done((bf16[2,2,2,128,128]{4,3,2,1,0:T(8,128)(2,1)S(1)}, bf16[2,2,2,128,128]{4,3,2,1,0:T(8,128)(2,1)S(1)}, u32[]{:S(2)}, u32[]{:S(2)}) %collective-permute-start.1) | collective-permute-done | bytes 262176 | tf_op jit(solution)/shard_map/ppermute | solution.py:153
  104.0 1.7 %collective-permute-start.2 = (bf16[2,2,128,128]{3,2,1,0:T(8,128)(2,1)S(1)}, bf16[2,2,128,128]{3,2,1,0:T(8,128)(2,1)S(1)}, u32[]{:S(2)}, u32[]{:S(2)}) collective-permute-start(bf16[2,2,128,128]{3,2,1,0:T(8,128)(2,1)S(1)} %dynamic-slice_bitcast_fusion.4), channel_id=1, source_target_pairs={{0,2},{1,3},{2,0},{3,1},{4,6},{5,7},{6,4},{7,5},{8,10},{9,11},{10,... | collective-permute-start | bytes 393224 | tf_op jit(solution)/shard_map/ppermute | solution.py:153
  105.8 0.6 collective-permute-start.7
  106.4 3.9 %collective-permute-done.2 = bf16[2,2,128,128]{3,2,1,0:T(8,128)(2,1)S(1)} collective-permute-done((bf16[2,2,128,128]{3,2,1,0:T(8,128)(2,1)S(1)}, bf16[2,2,128,128]{3,2,1,0:T(8,128)(2,1)S(1)}, u32[]{:S(2)}, u32[]{:S(2)}) %collective-permute-start.2) | collective-permute-done | bytes 131104 | tf_op jit(solution)/shard_map/ppermute | solution.py:153
  110.4 1.6 %collective-permute-start.3 = (bf16[2,128,128]{2,1,0:T(8,128)(2,1)S(1)}, bf16[2,128,128]{2,1,0:T(8,128)(2,1)S(1)}, u32[]{:S(2)}, u32[]{:S(2)}) collective-permute-start(bf16[2,128,128]{2,1,0:T(8,128)(2,1)S(1)} %dynamic-slice_bitcast_fusion.6), channel_id=1, source_target_pairs={{0,4},{1,5},{2,6},{3,7},{4,0},{5,1},{6,2},{7,3},{8,12},{9,13},{10,... | collective-permute-start | bytes 196616 | tf_op jit(solution)/shard_map/ppermute | solution.py:153
  112.0 1.3 collective-permute-start.8
  113.4 1.4 %collective-permute-done.3 = bf16[2,128,128]{2,1,0:T(8,128)(2,1)S(1)} collective-permute-done((bf16[2,128,128]{2,1,0:T(8,128)(2,1)S(1)}, bf16[2,128,128]{2,1,0:T(8,128)(2,1)S(1)}, u32[]{:S(2)}, u32[]{:S(2)}) %collective-permute-start.3) | collective-permute-done | bytes 65568 | tf_op jit(solution)/shard_map/ppermute | solution.py:153
  114.8 3.2 %collective-permute-start.4 = (bf16[128,128]{1,0:T(8,128)(2,1)S(1)}, bf16[128,128]{1,0:T(8,128)(2,1)S(1)}, u32[]{:S(2)}, u32[]{:S(2)}) collective-permute-start(bf16[128,128]{1,0:T(8,128)(2,1)S(1)} %dynamic-slice_bitcast_fusion.8), channel_id=1, source_target_pairs={{0,8},{1,9},{2,10},{3,11},{4,12},{5,13},{6,14},{7,15},{8,0},{9,1},... | collective-permute-start | bytes 98312 | tf_op jit(solution)/shard_map/ppermute | solution.py:153
  118.0 1.3 collective-permute-start.9
  119.3 0.6 gather_fusion.1
  119.9 0.6 gather_fusion.2
  120.6 0.6 gather_fusion.3
  121.2 0.8 add_convert_fusion
  122.0 3.6 %all-to-all-start.3 = ((bf16[32,8,512]{2,1,0:T(8,128)(2,1)}), bf16[32,8,512]{2,1,0:T(8,128)(2,1)S(1)}, u32[]{:S(2)}, u32[]{:S(2)}) async-start(bf16[32,8,512]{2,1,0:T(8,128)(2,1)} %add_convert_fusion), calls=%async_computation.3 | async-start | bytes 524288 | tf_op jit(solution)/shard_map/all_to_all | solution.py:25
  125.7 0.7 maximum_convert_fusion
  126.4 9.5 %all-to-all-done.3 = bf16[32,8,512]{2,1,0:T(8,128)(2,1)S(1)} async-done(((bf16[32,8,512]{2,1,0:T(8,128)(2,1)}), bf16[32,8,512]{2,1,0:T(8,128)(2,1)S(1)}, u32[]{:S(2)}, u32[]{:S(2)}) %all-to-all-start.3) | async-done | bytes 262176 | tf_op jit(solution)/shard_map/all_to_all | solution.py:25
  135.9 0.8 fusion.5
  (63 shorter events, 0.8 us)
Async XLA Ops:
  0.6 28.3 %copy-start = (bf16[512,512]{1,0:T(8,128)(2,1)S(1)}, bf16[512,512]{1,0:T(8,128)(2,1)}, u32[]{:S(2)}) copy-start(bf16[512,512]{1,0:T(8,128)(2,1)} %param.14) | copy-start | bytes 1572868
  0.6 17.6 %all-to-all-start = ((bf16[32,8,512]{2,1,0:T(8,128)(2,1)}), bf16[32,8,512]{2,1,0:T(8,128)(2,1)S(1)}, u32[]{:S(2)}, u32[]{:S(2)}) async-start(bf16[32,8,512]{2,1,0:T(8,128)(2,1)} %bitcast.105), calls=%async_computation | async-start | bytes 524288 | tf_op jit(solution)/shard_map/all_to_all | solution.py:25
  8.9 14.4 %copy-start.1 = (bf16[512,512]{1,0:T(8,128)(2,1)S(1)}, bf16[512,512]{1,0:T(8,128)(2,1)}, u32[]{:S(2)}) copy-start(bf16[512,512]{1,0:T(8,128)(2,1)} %w_key_ref.1) | copy-start | bytes 1572868
  8.9 14.4 %copy-start.12 = (bf16[256,512]{1,0:T(8,128)(2,1)S(1)}, bf16[256,512]{1,0:T(8,128)(2,1)}, u32[]{:S(2)}) copy-start(bf16[256,512]{1,0:T(8,128)(2,1)} %param.8) | copy-start | bytes 786436
  19.8 4.7 %copy-start.2 = (bf16[512,512]{1,0:T(8,128)(2,1)S(1)}, bf16[512,512]{1,0:T(8,128)(2,1)}, u32[]{:S(2)}) copy-start(bf16[512,512]{1,0:T(8,128)(2,1)} %w_value_ref.1) | copy-start | bytes 1572868
  19.8 25.0 %all-to-all-start.1 = ((bf16[32,3,8,512]{3,2,1,0:T(8,128)(2,1)}), bf16[32,3,8,512]{3,2,1,0:T(8,128)(2,1)}, u32[]{:S(2)}, u32[]{:S(2)}) async-start(bf16[32,3,8,512]{3,2,1,0:T(8,128)(2,1)} %bitcast.1), calls=%async_computation.1 | async-start | bytes 1572864 | tf_op jit(solution)/shard_map/all_to_all | solution.py:25
  24.3 4.6 %copy-start.17 = (bf16[256,512]{1,0:T(8,128)(2,1)S(1)}, bf16[256,512]{1,0:T(8,128)(2,1)}, u32[]{:S(2)}) copy-start(bf16[256,512]{1,0:T(8,128)(2,1)} %param.9) | copy-start | bytes 786436
  26.8 4.2 %copy-start.14 = (bf16[512,512]{1,0:T(8,128)(2,1)S(1)}, bf16[512,512]{1,0:T(8,128)(2,1)}, u32[]{:S(2)}) copy-start(bf16[512,512]{1,0:T(8,128)(2,1)} %param.11) | copy-start | bytes 1572868
  32.0 14.8 %copy-start.11 = (f32[8,256]{1,0:T(8,128)S(1)}, f32[8,256]{1,0:T(8,128)}, u32[]{:S(2)}) copy-start(f32[8,256]{1,0:T(8,128)} %lse_ref.1) | copy-start | bytes 24580
  46.8 1.0 copy-start.3
  47.9 0.9 copy-start.4
  48.8 0.9 copy-start.5
  49.8 0.9 copy-start.6
  50.7 0.9 copy-start.7
  51.7 0.9 copy-start.8
  52.6 0.9 copy-start.9
  53.6 0.9 copy-start.10
  54.5 13.5 %copy-start.13 = (bf16[256,512]{1,0:T(8,128)(2,1)S(1)}, bf16[256,512]{1,0:T(8,128)(2,1)}, u32[]{:S(2)}) copy-start(bf16[256,512]{1,0:T(8,128)(2,1)} %param.8) | copy-start | bytes 786436
  54.5 13.5 %copy-start.19 = (bf16[3,32,8,512]{3,2,1,0:T(8,128)(2,1)S(1)}, bf16[3,32,8,512]{3,2,1,0:T(8,128)(2,1)}, u32[]{:S(2)}) copy-start(bf16[3,32,8,512]{3,2,1,0:T(8,128)(2,1)} %copy.23) | copy-start | bytes 2359300
  68.1 2.1 %copy-start.21 = (bf16[1024,512]{1,0:T(8,128)(2,1)S(1)}, bf16[1024,512]{1,0:T(8,128)(2,1)}, u32[]{:S(2)}) copy-start(bf16[1024,512]{1,0:T(8,128)(2,1)} %get-tuple-element.11) | copy-start | bytes 3145732
  70.2 1.0 copy-start.18
  79.9 0.9 copy-start.15
  80.9 3.5 %copy-start.20 = (s32[32,3]{0,1:T(4,128)S(1)}, s32[32,3]{0,1:T(4,128)}, u32[]{:S(2)}) copy-start(s32[32,3]{0,1:T(4,128)} %param.15) | copy-start | bytes 1156
  81.7 7.4 %collective-permute-start = (bf16[2,2,2,2,128,128]{5,4,3,2,1,0:T(8,128)(2,1)}, bf16[2,2,2,2,128,128]{5,4,3,2,1,0:T(8,128)(2,1)}, u32[]{:S(2)}, u32[]{:S(2)}) collective-permute-start(bf16[2,2,2,2,128,128]{5,4,3,2,1,0:T(8,128)(2,1)} %dynamic-slice_bitcast_fusion), channel_id=1, source_target_pairs={{0,1},{1,0},{2,3},{3,2},{4,5},{5,4},{6,7},{7,6},{8,9},{9,8},{10,11... | collective-permute-start | bytes 1572872 | tf_op jit(solution)/shard_map/ppermute | solution.py:153
  83.0 6.1 %copy-start.16 = (bf16[2,16,128,128]{3,2,1,0:T(8,128)(2,1)S(1)}, bf16[2,16,128,128]{3,2,1,0:T(8,128)(2,1)}, u32[]{:S(2)}) copy-start(bf16[2,16,128,128]{3,2,1,0:T(8,128)(2,1)} %copy-done.15) | copy-start | bytes 3145732
  83.8 8.2 %collective-permute-start.5 = (bf16[2,2,2,2,128,128]{5,4,1,2,0,3:T(8,128)(2,1)}, bf16[2,2,2,2,128,128]{5,4,1,2,0,3:T(8,128)(2,1)}, u32[]{:S(2)}, u32[]{:S(2)}) collective-permute-start(bf16[2,2,2,2,128,128]{5,4,1,2,0,3:T(8,128)(2,1)} %bitcast.101), channel_id=1, source_target_pairs={{0,1},{1,0},{2,3},{3,2},{4,5},{5,4},{6,7},{7,6},{8,9},{9,8},{10,11... | collective-permute-start | bytes 1572872 | tf_op jit(solution)/shard_map/ppermute | solution.py:153
  86.5 32.8 %all-to-all-start.2 = ((bf16[32,3,8,512]{3,2,1,0:T(8,128)(2,1)}), bf16[32,3,8,512]{3,2,1,0:T(8,128)(2,1)S(1)}, u32[]{:S(2)}, u32[]{:S(2)}) async-start(bf16[32,3,8,512]{3,2,1,0:T(8,128)(2,1)} %bitcast.110), calls=%async_computation.2 | async-start | bytes 1572864 | tf_op jit(solution)/shard_map/all_to_all | solution.py:25
  90.3 13.6 %collective-permute-start.1 = (bf16[2,2,2,128,128]{4,3,2,1,0:T(8,128)(2,1)S(1)}, bf16[2,2,2,128,128]{4,3,2,1,0:T(8,128)(2,1)S(1)}, u32[]{:S(2)}, u32[]{:S(2)}) collective-permute-start(bf16[2,2,2,128,128]{4,3,2,1,0:T(8,128)(2,1)S(1)} %dynamic-slice_bitcast_fusion.2), channel_id=1, source_target_pairs={{0,16},{1,17},{2,18},{3,19},{4,20},{5,21},{6,22},{7,23},{8,24},{9,... | collective-permute-start | bytes 786440 | tf_op jit(solution)/shard_map/ppermute | solution.py:153
  93.3 12.4 %collective-permute-start.6 = (bf16[2,2,2,128,128]{4,3,1,2,0:T(8,128)(2,1)S(1)}, bf16[2,2,2,128,128]{4,3,1,2,0:T(8,128)(2,1)S(1)}, u32[]{:S(2)}, u32[]{:S(2)}) collective-permute-start(bf16[2,2,2,128,128]{4,3,1,2,0:T(8,128)(2,1)S(1)} %dynamic-slice_bitcast_fusion.1), channel_id=1, source_target_pairs={{0,2},{1,3},{2,0},{3,1},{4,6},{5,7},{6,4},{7,5},{8,10},{9,11},{10,... | collective-permute-start | bytes 786440 | tf_op jit(solution)/shard_map/ppermute | solution.py:153
  104.0 6.3 %collective-permute-start.2 = (bf16[2,2,128,128]{3,2,1,0:T(8,128)(2,1)S(1)}, bf16[2,2,128,128]{3,2,1,0:T(8,128)(2,1)S(1)}, u32[]{:S(2)}, u32[]{:S(2)}) collective-permute-start(bf16[2,2,128,128]{3,2,1,0:T(8,128)(2,1)S(1)} %dynamic-slice_bitcast_fusion.4), channel_id=1, source_target_pairs={{0,2},{1,3},{2,0},{3,1},{4,6},{5,7},{6,4},{7,5},{8,10},{9,11},{10,... | collective-permute-start | bytes 393224 | tf_op jit(solution)/shard_map/ppermute | solution.py:153
  105.8 6.2 %collective-permute-start.7 = (bf16[2,2,128,128]{3,2,0,1:T(8,128)(2,1)S(1)}, bf16[2,2,128,128]{3,2,0,1:T(8,128)(2,1)S(1)}, u32[]{:S(2)}, u32[]{:S(2)}) collective-permute-start(bf16[2,2,128,128]{3,2,0,1:T(8,128)(2,1)S(1)} %dynamic-slice_bitcast_fusion.3), channel_id=1, source_target_pairs={{0,16},{1,17},{2,18},{3,19},{4,20},{5,21},{6,22},{7,23},{8,24},{9,... | collective-permute-start | bytes 393224 | tf_op jit(solution)/shard_map/ppermute | solution.py:153
  110.4 4.3 %collective-permute-start.3 = (bf16[2,128,128]{2,1,0:T(8,128)(2,1)S(1)}, bf16[2,128,128]{2,1,0:T(8,128)(2,1)S(1)}, u32[]{:S(2)}, u32[]{:S(2)}) collective-permute-start(bf16[2,128,128]{2,1,0:T(8,128)(2,1)S(1)} %dynamic-slice_bitcast_fusion.6), channel_id=1, source_target_pairs={{0,4},{1,5},{2,6},{3,7},{4,0},{5,1},{6,2},{7,3},{8,12},{9,13},{10,... | collective-permute-start | bytes 196616 | tf_op jit(solution)/shard_map/ppermute | solution.py:153
  112.0 5.9 %collective-permute-start.8 = (bf16[2,128,128]{2,1,0:T(8,128)(2,1)S(1)}, bf16[2,128,128]{2,1,0:T(8,128)(2,1)S(1)}, u32[]{:S(2)}, u32[]{:S(2)}) collective-permute-start(bf16[2,128,128]{2,1,0:T(8,128)(2,1)S(1)} %dynamic-slice_bitcast_fusion.5), channel_id=1, source_target_pairs={{0,4},{1,5},{2,6},{3,7},{4,0},{5,1},{6,2},{7,3},{8,12},{9,13},{10,... | collective-permute-start | bytes 196616 | tf_op jit(solution)/shard_map/ppermute | solution.py:153
  114.8 10.8 %collective-permute-start.4 = (bf16[128,128]{1,0:T(8,128)(2,1)S(1)}, bf16[128,128]{1,0:T(8,128)(2,1)S(1)}, u32[]{:S(2)}, u32[]{:S(2)}) collective-permute-start(bf16[128,128]{1,0:T(8,128)(2,1)S(1)} %dynamic-slice_bitcast_fusion.8), channel_id=1, source_target_pairs={{0,8},{1,9},{2,10},{3,11},{4,12},{5,13},{6,14},{7,15},{8,0},{9,1},... | collective-permute-start | bytes 98312 | tf_op jit(solution)/shard_map/ppermute | solution.py:153
  118.0 7.6 %collective-permute-start.9 = (bf16[128,128]{1,0:T(8,128)(2,1)S(1)}, bf16[128,128]{1,0:T(8,128)(2,1)S(1)}, u32[]{:S(2)}, u32[]{:S(2)}) collective-permute-start(bf16[128,128]{1,0:T(8,128)(2,1)S(1)} %dynamic-slice_bitcast_fusion.7), channel_id=1, source_target_pairs={{0,8},{1,9},{2,10},{3,11},{4,12},{5,13},{6,14},{7,15},{8,0},{9,1},... | collective-permute-start | bytes 98312 | tf_op jit(solution)/shard_map/ppermute | solution.py:153
  122.0 13.9 %all-to-all-start.3 = ((bf16[32,8,512]{2,1,0:T(8,128)(2,1)}), bf16[32,8,512]{2,1,0:T(8,128)(2,1)S(1)}, u32[]{:S(2)}, u32[]{:S(2)}) async-start(bf16[32,8,512]{2,1,0:T(8,128)(2,1)} %add_convert_fusion), calls=%async_computation.3 | async-start | bytes 524288 | tf_op jit(solution)/shard_map/all_to_all | solution.py:25

commit v2 on v1

v2 whole, which is shorter than its diff:
```python
import functools
import math

import jax
import jax.numpy as jnp
from jax import lax
from jax.experimental import pallas as pl
from jax.experimental.pallas import tpu as pltpu
from jax.sharding import PartitionSpec as P

AXES = ("gx", "gy")
LOW = jnp.bfloat16
WIDE = jnp.float32


def dot(left, right):
    return jnp.dot(left, right, preferred_element_type=WIDE)


def dot_nt(left, right):
    return lax.dot_general(left, right, (((1,), (1,)), ((), ())), preferred_element_type=WIDE)


def exchange(pieces):
    return lax.all_to_all(pieces, AXES, split_axis=0, concat_axis=0, tiled=True)


VMEM = pl.BlockSpec(memory_space=pltpu.VMEM)
ANY = pl.BlockSpec(memory_space=pl.ANY)
FULL_VMEM = 56 * 1024 * 1024


def shaped(shape, dtype=LOW):
    return jax.ShapeDtypeStruct(shape, dtype)


def project_kernel(
    feats_ref,
    grad_out_ref,
    w_query_ref,
    w_key_ref,
    w_value_ref,
    w_output_ref,
    query_ref,
    query_t_ref,
    d_out_ref,
    d_out_t_ref,
    key_ref,
    key_t_ref,
    value_ref,
    value_t_ref,
    w_query_t_ref,
    w_key_t_ref,
    w_value_t_ref,
    feats_t_ref,
):
    feats = feats_ref[...]
    feats_t_ref[...] = feats.T
    for w_ref, w_t_ref, plain_ref, turned_ref in (
        (w_query_ref, w_query_t_ref, query_ref, query_t_ref),
        (w_key_ref, w_key_t_ref, key_ref, key_t_ref),
        (w_value_ref, w_value_t_ref, value_ref, value_t_ref),
    ):
        w_t = w_ref[...].T
        w_t_ref[...] = w_t
        plain_ref[...] = dot(feats, w_ref[...]).astype(LOW)
        turned_ref[...] = dot_nt(w_t, feats).astype(LOW)
    d_out_ref[...] = dot_nt(grad_out_ref[...], w_output_ref[...]).astype(LOW)
    d_out_t_ref[...] = dot_nt(w_output_ref[...], grad_out_ref[...]).astype(LOW)


def project(node_feats, grad_out, *weights):
    block, width = node_feats.shape
    plain, turned, square = shaped((block, width)), shaped((width, block)), shaped((width, width))
    return pl.pallas_call(
        project_kernel,
        out_shape=(plain, turned) * 4 + (square,) * 3 + (turned,),
        in_specs=[VMEM] * 6,
        out_specs=(VMEM,) * 12,
        compiler_params=pltpu.CompilerParams(vmem_limit_bytes=FULL_VMEM),
        cost_estimate=pl.CostEstimate(
            flops=16 * block * width * width,
            bytes_accessed=2 * (10 * block * width + 7 * width * width),
            transcendentals=0,
        ),
    )(node_feats, grad_out, *weights)


def attention_kernel(
    head_size,
    group,
    stages,
    n_inner,
    me_ref,
    lse_ref,
    arrived_hbm,
    query_hbm,
    query_t_hbm,
    d_out_hbm,
    d_out_t_hbm,
    key_own_hbm,
    key_own_t_hbm,
    value_own_hbm,
    value_own_t_hbm,
    w_query_t_hbm,
    w_key_t_hbm,
    w_value_t_hbm,
    feats_t_hbm,
    grad_out_hbm,
    terms_hbm,
    own_hbm,
    keep_hbm,
    send_hbm,
    arrived_ref,
    query_ref,
    query_t_ref,
    d_out_ref,
    d_out_t_ref,
    w_query_t_ref,
    w_key_t_ref,
    w_value_t_ref,
    feats_t_ref,
    grad_out_ref,
    key_ref,
    value_ref,
    key_t_ref,
    value_t_ref,
    terms_ref,
    own_ref,
    grad_query_t_ref,
    out_t_ref,
    grad_key_ref,
    grad_value_ref,
    keep_ref,
    send_ref,
    in_sem,
    out_sem,
):
    heads = lse_ref.shape[0]
    block, width = query_ref.shape
    scaling = head_size ** (-0.5)
    log2e = math.log2(math.e)

    def by_match(ref, match):
        return ref.at[:, match] if len(ref.shape) == 4 else ref.at[match]

    loads = []

    def load(source, target):
        copy = pltpu.make_async_copy(source, target, in_sem.at[len(loads)])
        copy.start()
        loads.append(copy)
        return copy

    stores = []

    def store(source, target):
        copy = pltpu.make_async_copy(source, target, out_sem.at[len(stores)])
        copy.start()
        stores.append(copy)

    first_need = load(by_match(arrived_hbm, 0), arrived_ref.at[0])
    key_need = load(w_key_t_hbm, w_key_t_ref)
    value_need = load(w_value_t_hbm, w_value_t_ref)
    far_needs = [load(by_match(arrived_hbm, match), arrived_ref.at[match]) for match in (1, 2)]
    own = pl.ds(0, block)
    head_needs = [
        load(key_own_hbm, key_ref.at[own]),
        load(value_own_hbm, value_ref.at[own]),
        load(key_own_t_hbm, key_t_ref.at[:, own]),
        load(value_own_t_hbm, value_t_ref.at[:, own]),
        load(query_t_hbm, query_t_ref),
        load(d_out_t_hbm, d_out_t_ref),
        load(query_hbm, query_ref),
        load(d_out_hbm, d_out_ref),
    ]
    last_needs = [
        load(w_query_t_hbm, w_query_t_ref),
        load(feats_t_hbm, feats_t_ref),
        load(grad_out_hbm, grad_out_ref),
    ]
    first_need.wait()
    key_need.wait()
    for match in range(3):
        here = slice((match + 1) * block, (match + 2) * block)
        if match > 0:
            far_needs[match - 1].wait()
        far = arrived_ref[match].reshape(block, width)
        key_ref[here] = dot_nt(far, w_key_t_ref[...]).astype(LOW)
        key_t_ref[:, here] = dot_nt(w_key_t_ref[...], far).astype(LOW)
        if match == 0:
            value_need.wait()
        value_ref[here] = dot_nt(far, w_value_t_ref[...]).astype(LOW)
        value_t_ref[:, here] = dot_nt(w_value_t_ref[...], far).astype(LOW)
    for copy in head_needs:
        copy.wait()
    span = group * head_size
    for first in range(0, heads, group):
        cols = slice(first * head_size, first * head_size + span)
        key = key_ref[:, cols]
        value = value_ref[:, cols]
        row = lax.broadcasted_iota(jnp.int32, (span, block), 0) // head_size
        col = lax.broadcasted_iota(jnp.int32, (block, span), 1) // head_size
        query_t = query_t_ref[cols, :]
        d_out_t = d_out_t_ref[cols, :]
        query = query_ref[:, cols]
        d_out = d_out_ref[:, cols]
        zero_t = jnp.zeros_like(query_t)
        zero = jnp.zeros_like(query)
        grad_key = None
        grad_value = None
        for inner in range(group):
            head = first + inner
            rows = slice(head * head_size, (head + 1) * head_size)
            score = dot(key, jnp.where(row == inner, query_t, zero_t))
            shift = lse_ref[head : head + 1, :] * log2e
            prob = jnp.exp2(jnp.minimum(score * (scaling * log2e) - shift, 0.0))
            prob_low = prob.astype(LOW)
            out_t = dot(value_t_ref[rows, :], prob_low).astype(LOW)
            out_t_ref[rows, :] = out_t
            d_rows = d_out_t_ref[rows, :]
            delta = jnp.sum(d_rows.astype(WIDE) * out_t.astype(WIDE), axis=0, keepdims=True) * scaling
            grad_prob = dot(value, jnp.where(row == inner, d_out_t * scaling, zero_t))
            grad_score = (prob * (grad_prob - delta)).astype(LOW)
            grad_query_t_ref[rows, :] = dot(key_t_ref[rows, :], grad_score).astype(LOW)
            part_key = dot(grad_score, jnp.where(col == inner, query, zero))
            part_value = dot(prob_low, jnp.where(col == inner, d_out, zero))
            grad_key = part_key if grad_key is None else grad_key + part_key
            grad_value = part_value if grad_value is None else grad_value + part_value
        grad_key_ref[:, cols] = grad_key.astype(LOW)
        grad_value_ref[:, cols] = grad_value.astype(LOW)
    for copy in last_needs:
        copy.wait()

    _, rows, cols = keep_ref.shape
    n_outer = width // rows
    me = me_ref[0]
    odd = me % 2 == 1

    def place(matrix, total):
        low = total.astype(LOW)
        for start in range(0, width, 2 * cols):
            inner = (matrix * width + start) // cols
            for outer in range(n_outer):
                differ = me ^ (outer * n_inner + inner)
                slot = 0
                for masks in stages:
                    for mask in masks:
                        slot = slot * 2 + jnp.where((differ & mask) != 0, 1, 0)
                here = slice(outer * rows, (outer + 1) * rows)
                left = low[here, start : start + cols]
                right = low[here, start + cols : start + 2 * cols]
                keep_ref[slot] = jnp.where(odd, right, left)
                send_ref[slot] = jnp.where(odd, left, right)

    feats_t = feats_t_ref[...]
    far_t = [arrived_ref[match].reshape(block, width).T for match in range(3)]
    place(3, dot(out_t_ref[...], grad_out_ref[...]))
    place(0, dot_nt(feats_t, grad_query_t_ref[...]))
    for matrix, ref in ((1, grad_key_ref), (2, grad_value_ref)):
        total = dot(feats_t, ref[:block])
        for match in range(3):
            total = total + dot(far_t[match], ref[(match + 1) * block : (match + 2) * block])
        place(matrix, total)
    store(send_ref, send_hbm)
    store(keep_ref, keep_hbm)
    for member in range(4):
        here = slice(member * block, (member + 1) * block)
        total = dot(grad_key_ref[here], w_key_t_ref[...])
        total = total + dot(grad_value_ref[here], w_value_t_ref[...])
        if member == 0:
            own_ref[...] = total + lax.dot_general(
                grad_query_t_ref[...],
                w_query_t_ref[...],
                (((0,), (0,)), ((), ())),
                preferred_element_type=WIDE,
            )
            store(own_ref, own_hbm)
        else:
            terms_ref[member - 1] = total.astype(LOW).reshape(terms_ref.shape[1:])
            store(terms_ref.at[member - 1], by_match(terms_hbm, member - 1))
    for copy in stores:
        copy.wait()


def attention(me, stages, arrived, projections, grad_out, log_sum_exp):
    n_outer, n_inner = lax.axis_size("gx"), lax.axis_size("gy")
    block, width = grad_out.shape
    heads = log_sum_exp.shape[0]
    head_size = width // heads
    members = 4 * block
    group = max(1, 128 // head_size)
    devices, _, piece, _ = arrived.shape
    whole_tiles = piece % 8 == 0
    if not whole_tiles:
        arrived = arrived.transpose(1, 0, 2, 3).reshape(3, block, width)
    staged = (3, devices, piece, width) if whole_tiles else (3, block, width)
    half = (devices // 2, width // n_outer, 4 * width // n_inner)
    plain, turned, square = (
        pltpu.VMEM((block, width), LOW),
        pltpu.VMEM((width, block), LOW),
        pltpu.VMEM((width, width), LOW),
    )
    long, long_t = pltpu.VMEM((members, width), LOW), pltpu.VMEM((width, members), LOW)
    terms, own, keep, send = pl.pallas_call(
        functools.partial(attention_kernel, head_size, group, stages, n_inner),
        out_shape=(shaped(arrived.shape), shaped((block, width), WIDE), shaped(half), shaped(half)),
        in_specs=[pl.BlockSpec(memory_space=pltpu.SMEM), VMEM] + [ANY] * 14,
        out_specs=(ANY,) * 4,
        scratch_shapes=[
            pltpu.VMEM(staged, LOW),
            plain,
            turned,
            plain,
            turned,
            square,
            square,
            square,
            turned,
            plain,
            long,
            long,
            long_t,
            long_t,
            pltpu.VMEM(staged, LOW),
            pltpu.VMEM((block, width), WIDE),
            turned,
            turned,
            long,
            long,
            pltpu.VMEM(half, LOW),
            pltpu.VMEM(half, LOW),
            pltpu.SemaphoreType.DMA((16,)),
            pltpu.SemaphoreType.DMA((6,)),
        ],
        compiler_params=pltpu.CompilerParams(vmem_limit_bytes=FULL_VMEM),
        cost_estimate=pl.CostEstimate(
            flops=12 * block * members * width + 32 * members * width * width,
            bytes_accessed=16 * members * width,
            transcendentals=heads * block * members,
        ),
    )(me.reshape(1), log_sum_exp, arrived, *projections, grad_out)
    if not whole_tiles:
        terms = terms.reshape(3, devices, piece, width).transpose(1, 0, 2, 3)
    return terms, own, keep, send


def bits_of(count):
    return [1 << position for position in range(count.bit_length() - 1)]


def stages_of(n_outer, n_inner):
    outer = [mask * n_inner for mask in bits_of(n_outer)]
    inner = bits_of(n_inner)[1:]
    order = []
    for position in range(max(len(outer), len(inner))):
        order += inner[position : position + 1] + outer[position : position + 1]
    return [order[start : start + 2] for start in range(0, len(order), 2)]


def add_up(first, *others):
    total = first.astype(WIDE)
    for other in others:
        total = total + other.astype(WIDE)
    return total


def swap(value, mask, devices):
    return lax.ppermute(value, AXES, [(device, device ^ mask) for device in range(devices)])


def stage_sum(parts, masks, devices):
    got = []
    for index in range(1, len(parts)):
        mask = 0
        for position, each in enumerate(masks):
            if index >> (len(masks) - 1 - position) & 1:
                mask |= each
        got.append(swap(parts[index], mask, devices))
    return parts[0], got


def collect_kernel(partners_ref, returned_ref, summed_ref):
    for node in range(summed_ref.shape[0]):
        total = None
        for match in range(3):
            term = returned_ref[partners_ref[node, match], match].astype(WIDE)
            total = term if total is None else total + term
        summed_ref[node] = total.astype(LOW)


def collect_pieces(returned, partners):
    devices, _, piece, width = returned.shape
    if piece % 8:
        return sum(returned[partners[:, match], match].astype(WIDE) for match in range(3)).astype(LOW)
    return pl.pallas_call(
        collect_kernel,
        out_shape=shaped((devices, piece, width)),
        in_specs=[pl.BlockSpec(memory_space=pltpu.SMEM), VMEM],
        out_specs=VMEM,
        compiler_params=pltpu.CompilerParams(vmem_limit_bytes=FULL_VMEM),
    )(partners, returned)


def on_device(node_feats, grad_out, log_sum_exp, w_query, w_key, w_value, w_output, partners):
    block, width = node_feats.shape
    n_outer, n_inner = lax.axis_size("gx"), lax.axis_size("gy")
    devices = n_outer * n_inner
    piece = block // devices
    me = lax.axis_index("gx") * n_inner + lax.axis_index("gy")
    stages = stages_of(n_outer, n_inner)

    spread = exchange(node_feats.reshape(devices, piece, width))
    arrived = exchange(spread[partners])
    projections = project(node_feats, grad_out, w_query, w_key, w_value, w_output)
    terms, own, keep, send = attention(me, stages, arrived, projections, grad_out, log_sum_exp)
    returned = exchange(terms)
    got = [swap(send, 1, devices)]
    summed = None
    for number, masks in enumerate(stages):
        count = 2 ** len(masks)
        keep = keep.reshape((count, -1) + keep.shape[1:])
        got = [each.reshape(keep.shape) for each in got]
        parts = [
            add_up(keep[index], *(each[index] for each in got)).astype(LOW) for index in range(count)
        ]
        if number == len(stages) - 1:
            summed = collect_pieces(returned, partners)
            *parts, summed = lax.optimization_barrier((*parts, summed))
        keep, got = stage_sum(parts, masks, devices)
    back = exchange(summed).reshape(block, width)
    grad_nodes = (own + back.astype(WIDE)).astype(LOW)
    weight_grads = add_up(keep, *got)[0]
    return grad_nodes, weight_grads


def solution(mesh):
    return jax.shard_map(
        on_device,
        mesh=mesh,
        in_specs=(
            P(AXES, None),
            P(AXES, None),
            P(None, AXES),
            P(),
            P(),
            P(),
            P(),
            P(),
        ),
        out_specs=(P(AXES, None), P("gx", "gy")),
        check_vma=False,
    )
```

time: 138 us -> 111 us (0.80)
  local copies, waits for them, and re-layouts: 30.2 us -> 4.17 us
  matrix products: 13.3 us -> 0 us
  waiting for transfers between devices: 42.4 us -> 55.3 us
  Pallas kernels: 13.5 us -> 23.2 us
  starting transfers between devices: 30.4 us -> 24.6 us
  other arithmetic: 5.75 us -> 2.7 us
    ppermute x10 -> x7, waiting for transfers between devices: 14.4 us -> 27.8 us  [swap(): lax.ppermute(value, AXES, [(device, device ^ mask) for device in range(de...]
    dot_general x12 -> x0, matrix products: 13.3 us -> none  [the longest x6 7.77 us: dot(): return jnp.dot(left, right, preferred_element_type=WIDE)]
    pallas_call x1 -> x3, Pallas kernels: 13.5 us -> 23.2 us  [the longest x1 17.3 us: attention(): pl.pallas_call(functools.partial(attention_kernel, head_size, group, stag...]
    unnamed x47 -> x11, local copies, waits for them, and re-layouts: 11.3 us -> 2.46 us
    convert_element_type x2 -> x0, local copies, waits for them, and re-layouts: 6.92 us -> none  [on_device(): partial = jnp.concatenate([dot_nt(node_feats.T, grad_query_t), dot(feats_...]
    ppermute x10 -> x7, starting transfers between devices: 13.4 us -> 8.01 us  [swap(): lax.ppermute(value, AXES, [(device, device ^ mask) for device in range(de...]
    convert_element_type x12 -> x2, other arithmetic: 4.14 us -> 1.23 us  [on_device(): add_up(keep[index], *(each[index] for each in got)).astype(LOW)]
    dynamic_slice x2 -> x0, local copies, waits for them, and re-layouts: 2.1 us -> none  [the longest x1 1.27 us: halve(): keep = lax.dynamic_index_in_dim(parts, mine, axis, keepdims=False)]
  transfers between devices with their start and end apart: 14 -> 11, of which waited for: 6 -> 7; matrix products, arithmetic and copies ran while one was open for 17% -> 3% of each run, Pallas kernels for 0% -> 4%
where the time goes in v2:
time: 111 us
  waiting for transfers between devices  55.3 us (50%)
  starting transfers between devices  24.6 us (22%)
  Pallas kernels  23.2 us (21%)
  local copies, waits for them, and re-layouts  4.17 us (4%)
  other arithmetic  2.7 us (2%)
    ppermute x7, waiting for transfers between devices, swap(): lax.ppermute(value, AXES, [(device, device ^ mask) for device in range(de...  27.8 us
    all_to_all x4, waiting for transfers between devices, exchange(): return lax.all_to_all(pieces, AXES, split_axis=0, concat_axis=0, tiled=True)  27.6 us
    pallas_call x1, Pallas kernels, attention(): pl.pallas_call(functools.partial(attention_kernel, head_size, group, stag...  17.3 us
    all_to_all x4, starting transfers between devices, exchange(): return lax.all_to_all(pieces, AXES, split_axis=0, concat_axis=0, tiled=True)  16.6 us
    ppermute x7, starting transfers between devices, swap(): lax.ppermute(value, AXES, [(device, device ^ mask) for device in range(de...  8.01 us
    pallas_call x1, Pallas kernels, project(): pl.pallas_call(project_kernel, out_shape=(plain, turned) * 4 + (square,)...  4 us
    unnamed x11, local copies, waits for them, and re-layouts  2.46 us
  transfers between devices with their start and end apart: 11, of which 7 were waited for; matrix products, arithmetic and copies ran while one was open for 3% of the time, Pallas kernels for 4%

profile of v2, /device:TPU:0, one launch (start us, length us, event | category | flops | bytes accessed | tf_op | source)
XLA Modules:
  0.0 110.8 jit_solution(18235488297746218481)
XLA Ops:
  0.6 0.0 copy-start.4
  0.6 7.3 %all-to-all-start = ((bf16[32,8,512]{2,1,0:T(8,128)(2,1)}), bf16[32,8,512]{2,1,0:T(8,128)(2,1)S(1)}, u32[]{:S(2)}, u32[]{:S(2)}) async-start(bf16[32,8,512]{2,1,0:T(8,128)(2,1)} %bitcast.8), calls=%async_computation | async-start | bytes 524288 | tf_op jit(solution)/shard_map/all_to_all | solution.py:25
  8.0 0.0 copy-done.4
  8.0 0.1 copy.12
  8.1 0.1 reshape.120
  8.2 10.1 %all-to-all-done = bf16[32,8,512]{2,1,0:T(8,128)(2,1)S(1)} async-done(((bf16[32,8,512]{2,1,0:T(8,128)(2,1)}), bf16[32,8,512]{2,1,0:T(8,128)(2,1)S(1)}, u32[]{:S(2)}, u32[]{:S(2)}) %all-to-all-start) | async-done | bytes 262176 | tf_op jit(solution)/shard_map/all_to_all | solution.py:25
  18.2 1.5 %gather_fusion = bf16[96,8,512]{2,1,0:T(8,128)(2,1)} fusion(bf16[32,8,512]{2,1,0:T(8,128)(2,1)S(1)} %all-to-all-done, s32[1024]{0:T(1024)S(1)} %pad_clamp_fusion), kind=kCustom, calls=%fused_computation | custom fusion | bytes 1573248 | tf_op jit(solution)/shard_map/gather | solution.py:414
  19.8 2.6 %all-to-all-start.1 = ((bf16[32,3,8,512]{3,2,1,0:T(8,128)(2,1)}), bf16[32,3,8,512]{3,2,1,0:T(8,128)(2,1)S(1)}, u32[]{:S(2)}, u32[]{:S(2)}) async-start(bf16[32,3,8,512]{3,2,1,0:T(8,128)(2,1)} %bitcast.2), calls=%async_computation.1 | async-start | bytes 1572864 | tf_op jit(solution)/shard_map/all_to_all | solution.py:25
  22.4 4.0 %shard_map.95 = (bf16[256,512]{1,0:T(8,128)(2,1)}, bf16[512,256]{1,0:T(8,128)(2,1)}, bf16[256,512]{1,0:T(8,128)(2,1)}, bf16[512,256]{1,0:T(8,128)(2,1)}, bf16[25...) custom-call(bf16[256,512]{1,0:T(8,128)(2,1)} %feats_ref.1, ...), custom_call_target="tpu_custom_call" | custom-call | flops 1073741824 | bytes 6291456 | tf_op jit(solution)/shard_map/pallas_call | solution.py:75
  26.4 17.5 %all-to-all-done.1.arrived_hbm = bf16[32,3,8,512]{3,2,1,0:T(8,128)(2,1)S(1)} async-done(((bf16[32,3,8,512]{3,2,1,0:T(8,128)(2,1)}), bf16[32,3,8,512]{3,2,1,0:T(8,128)(2,1)S(1)}, u32[]{:S(2)}, u32[]{:S(2)}) %all-to-all-start.1) | async-done | bytes 786464 | tf_op jit(solution)/shard_map/all_to_all | solution.py:25
  43.9 0.0 copy-start.2
  43.9 0.9 copy-done.2
  44.8 17.3 %shard_map.96 = (bf16[32,3,8,512]{3,2,1,0:T(8,128)(2,1)}, f32[256,512]{1,0:T(8,128)}, bf16[16,256,128]{2,1,0:T(8,128)(2,1)}, bf16[16,256,128]{2,1,0:T(8,128)(2,1)}) custom-call(s32[1]{0:T(128)} %bitcast.me_ref, f32[8,256]{1,0:T(8,128)} %lse_ref.1, bf16[32,3,8,512]{3,2,1,0:T(8,128)(2,1)} %copy-done.2, bf16[256,512]{1,0:T(8,128)(2,1)} %get-tuple-element.23.query_hbm, ...), custom_call_target="tpu_custom_call" | custom-call | flops 10200547328 | bytes 8388608 | tf_op jit(solution)/shard_map/pallas_call | solution.py:305
  62.1 0.0 copy-start.1
  62.1 0.1 collective-permute-start
  62.1 2.8 %all-to-all-start.2 = ((bf16[32,3,8,512]{3,2,1,0:T(8,128)(2,1)}), bf16[32,3,8,512]{3,2,1,0:T(8,128)(2,1)S(1)}, u32[]{:S(2)}, u32[]{:S(2)}) async-start(bf16[32,3,8,512]{3,2,1,0:T(8,128)(2,1)} %get-tuple-element.38), calls=%async_computation.2 | async-start | bytes 1572864 | tf_op jit(solution)/shard_map/all_to_all | solution.py:25
  64.9 0.1 collective-permute-done
  65.0 0.0 copy-done.1
  65.0 1.1 add_convert_fusion.3
  66.1 1.6 %collective-permute-start.1 = (bf16[4,256,128]{2,1,0:T(8,128)(2,1)}, bf16[4,256,128]{2,1,0:T(8,128)(2,1)S(1)}, u32[]{:S(2)}, u32[]{:S(2)}) collective-permute-start(bf16[4,256,128]{2,1,0:T(8,128)(2,1)} %get-tuple-element.47), channel_id=1, source_target_pairs={{0,16},{1,17},{2,18},{3,19},{4,20},{5,21},{6,22},{7,23},{8,24},{9,... | collective-permute-start | bytes 786440 | tf_op jit(solution)/shard_map/ppermute | solution.py:369
  67.7 1.5 %collective-permute-start.2 = (bf16[4,256,128]{2,1,0:T(8,128)(2,1)}, bf16[4,256,128]{2,1,0:T(8,128)(2,1)S(1)}, u32[]{:S(2)}, u32[]{:S(2)}) collective-permute-start(bf16[4,256,128]{2,1,0:T(8,128)(2,1)} %get-tuple-element.46), channel_id=1, source_target_pairs={{0,2},{1,3},{2,0},{3,1},{4,6},{5,7},{6,4},{7,5},{8,10},{9,11},{10,... | collective-permute-start | bytes 786440 | tf_op jit(solution)/shard_map/ppermute | solution.py:369
  69.2 0.4 collective-permute-start.3
  69.6 0.7 copy.13.partners_ref
  70.3 10.2 %collective-permute-done.1 = bf16[4,256,128]{2,1,0:T(8,128)(2,1)S(1)} collective-permute-done((bf16[4,256,128]{2,1,0:T(8,128)(2,1)}, bf16[4,256,128]{2,1,0:T(8,128)(2,1)S(1)}, u32[]{:S(2)}, u32[]{:S(2)}) %collective-permute-start.1) | collective-permute-done | bytes 262176 | tf_op jit(solution)/shard_map/ppermute | solution.py:369
  80.5 2.8 %collective-permute-done.2 = bf16[4,256,128]{2,1,0:T(8,128)(2,1)S(1)} collective-permute-done((bf16[4,256,128]{2,1,0:T(8,128)(2,1)}, bf16[4,256,128]{2,1,0:T(8,128)(2,1)S(1)}, u32[]{:S(2)}, u32[]{:S(2)}) %collective-permute-start.2) | collective-permute-done | bytes 262176 | tf_op jit(solution)/shard_map/ppermute | solution.py:369
  83.4 5.0 %collective-permute-done.3 = bf16[4,256,128]{2,1,0:T(8,128)(2,1)S(1)} collective-permute-done((bf16[4,256,128]{2,1,0:T(8,128)(2,1)S(1)}, bf16[4,256,128]{2,1,0:T(8,128)(2,1)S(1)}, u32[]{:S(2)}, u32[]{:S(2)}) %collective-permute-start.3) | collective-permute-done | bytes 262176 | tf_op jit(solution)/shard_map/ppermute | solution.py:369
  88.4 0.1 add_convert_fusion.4
  88.5 0.0 all-to-all-done.2.returned_ref
  88.5 0.0 copy-start
  88.5 0.9 copy-done
  89.4 2.0 %shard_map.97 = bf16[32,8,512]{2,1,0:T(8,128)(2,1)} custom-call(s32[32,3]{1,0:T(8,128)} %copy.13.partners_ref, bf16[32,3,8,512]{3,2,1,0:T(8,128)(2,1)} %copy-done), custom_call_target="tpu_custom_call" | custom-call | tf_op jit(solution)/shard_map/pallas_call | solution.py:396
  91.4 0.0 copy-start.3
  91.4 3.9 %all-to-all-start.3 = ((bf16[32,8,512]{2,1,0:T(8,128)(2,1)}), bf16[32,8,512]{2,1,0:T(8,128)(2,1)S(1)}, u32[]{:S(2)}, u32[]{:S(2)}) async-start(bf16[32,8,512]{2,1,0:T(8,128)(2,1)} %shard_map.97), calls=%async_computation.3 | async-start | bytes 524288 | tf_op jit(solution)/shard_map/all_to_all | solution.py:25
  95.3 2.7 %collective-permute-start.4 = (bf16[1,256,128]{2,1,0:T(8,128)(2,1)S(1)}, bf16[1,256,128]{2,1,0:T(8,128)(2,1)S(1)}, u32[]{:S(2)}, u32[]{:S(2)}) collective-permute-start(bf16[1,256,128]{2,1,0:T(8,128)(2,1)S(1)} %get-tuple-element.41), channel_id=1, source_target_pairs={{0,8},{1,9},{2,10},{3,11},{4,12},{5,13},{6,14},{7,15},{8,0},{9,1},... | collective-permute-start | bytes 196616 | tf_op jit(solution)/shard_map/ppermute | solution.py:369
  98.0 1.5 %collective-permute-start.5 = (bf16[1,256,128]{2,1,0:T(8,128)(2,1)S(1)}, bf16[1,256,128]{2,1,0:T(8,128)(2,1)S(1)}, u32[]{:S(2)}, u32[]{:S(2)}) collective-permute-start(bf16[1,256,128]{2,1,0:T(8,128)(2,1)S(1)} %get-tuple-element.42), channel_id=1, source_target_pairs={{0,4},{1,5},{2,6},{3,7},{4,0},{5,1},{6,2},{7,3},{8,12},{9,13},{10,... | collective-permute-start | bytes 196616 | tf_op jit(solution)/shard_map/ppermute | solution.py:369
  99.5 0.2 collective-permute-start.6
  99.7 9.6 %collective-permute-done.4 = bf16[1,256,128]{2,1,0:T(8,128)(2,1)S(1)} collective-permute-done((bf16[1,256,128]{2,1,0:T(8,128)(2,1)S(1)}, bf16[1,256,128]{2,1,0:T(8,128)(2,1)S(1)}, u32[]{:S(2)}, u32[]{:S(2)}) %collective-permute-start.4) | collective-permute-done | bytes 65568 | tf_op jit(solution)/shard_map/ppermute | solution.py:369
  109.3 0.0 collective-permute-done.5
  109.3 0.0 collective-permute-done.6
  109.4 0.7 add_bitcast_fusion
  110.0 0.0 all-to-all-done.3
  110.0 0.0 copy-done.3
  110.0 0.8 fusion
  (2 shorter events, 0.0 us)
Async XLA Ops:
  0.6 7.3 %copy-start.4 = (s32[32,3]{0,1:T(4,128)S(1)}, s32[32,3]{0,1:T(4,128)}, u32[]{:S(2)}) copy-start(s32[32,3]{0,1:T(4,128)} %param.15) | copy-start | bytes 1156
  0.6 17.6 %all-to-all-start = ((bf16[32,8,512]{2,1,0:T(8,128)(2,1)}), bf16[32,8,512]{2,1,0:T(8,128)(2,1)S(1)}, u32[]{:S(2)}, u32[]{:S(2)}) async-start(bf16[32,8,512]{2,1,0:T(8,128)(2,1)} %bitcast.8), calls=%async_computation | async-start | bytes 524288 | tf_op jit(solution)/shard_map/all_to_all | solution.py:25
  19.8 24.1 %all-to-all-start.1 = ((bf16[32,3,8,512]{3,2,1,0:T(8,128)(2,1)}), bf16[32,3,8,512]{3,2,1,0:T(8,128)(2,1)S(1)}, u32[]{:S(2)}, u32[]{:S(2)}) async-start(bf16[32,3,8,512]{3,2,1,0:T(8,128)(2,1)} %bitcast.2), calls=%async_computation.1 | async-start | bytes 1572864 | tf_op jit(solution)/shard_map/all_to_all | solution.py:25
  43.9 0.9 copy-start.2
  62.1 2.9 %copy-start.1 = (bf16[16,256,128]{2,1,0:T(8,128)(2,1)S(1)}, bf16[16,256,128]{2,1,0:T(8,128)(2,1)}, u32[]{:S(2)}) copy-start(bf16[16,256,128]{2,1,0:T(8,128)(2,1)} %get-tuple-element.36) | copy-start | bytes 3145732
  62.1 2.9 %collective-permute-start = (bf16[16,256,128]{2,1,0:T(8,128)(2,1)}, bf16[16,256,128]{2,1,0:T(8,128)(2,1)S(1)}, u32[]{:S(2)}, u32[]{:S(2)}) collective-permute-start(bf16[16,256,128]{2,1,0:T(8,128)(2,1)} %get-tuple-element.37), channel_id=1, source_target_pairs={{0,1},{1,0},{2,3},{3,2},{4,5},{5,4},{6,7},{7,6},{8,9},{9,8},{10,11... | collective-permute-start | bytes 3145736 | tf_op jit(solution)/shard_map/ppermute | solution.py:369
  62.1 26.4 %all-to-all-start.2 = ((bf16[32,3,8,512]{3,2,1,0:T(8,128)(2,1)}), bf16[32,3,8,512]{3,2,1,0:T(8,128)(2,1)S(1)}, u32[]{:S(2)}, u32[]{:S(2)}) async-start(bf16[32,3,8,512]{3,2,1,0:T(8,128)(2,1)} %get-tuple-element.38), calls=%async_computation.2 | async-start | bytes 1572864 | tf_op jit(solution)/shard_map/all_to_all | solution.py:25
  66.1 14.4 %collective-permute-start.1 = (bf16[4,256,128]{2,1,0:T(8,128)(2,1)}, bf16[4,256,128]{2,1,0:T(8,128)(2,1)S(1)}, u32[]{:S(2)}, u32[]{:S(2)}) collective-permute-start(bf16[4,256,128]{2,1,0:T(8,128)(2,1)} %get-tuple-element.47), channel_id=1, source_target_pairs={{0,16},{1,17},{2,18},{3,19},{4,20},{5,21},{6,22},{7,23},{8,24},{9,... | collective-permute-start | bytes 786440 | tf_op jit(solution)/shard_map/ppermute | solution.py:369
  67.7 15.7 %collective-permute-start.2 = (bf16[4,256,128]{2,1,0:T(8,128)(2,1)}, bf16[4,256,128]{2,1,0:T(8,128)(2,1)S(1)}, u32[]{:S(2)}, u32[]{:S(2)}) collective-permute-start(bf16[4,256,128]{2,1,0:T(8,128)(2,1)} %get-tuple-element.46), channel_id=1, source_target_pairs={{0,2},{1,3},{2,0},{3,1},{4,6},{5,7},{6,4},{7,5},{8,10},{9,11},{10,... | collective-permute-start | bytes 786440 | tf_op jit(solution)/shard_map/ppermute | solution.py:369
  69.2 19.2 %collective-permute-start.3 = (bf16[4,256,128]{2,1,0:T(8,128)(2,1)S(1)}, bf16[4,256,128]{2,1,0:T(8,128)(2,1)S(1)}, u32[]{:S(2)}, u32[]{:S(2)}) collective-permute-start(bf16[4,256,128]{2,1,0:T(8,128)(2,1)S(1)} %get-tuple-element.45), channel_id=1, source_target_pairs={{0,18},{1,19},{2,16},{3,17},{4,22},{5,23},{6,20},{7,21},{8,26},{9,... | collective-permute-start | bytes 786440 | tf_op jit(solution)/shard_map/ppermute | solution.py:369
  88.5 0.9 copy-start
  91.4 18.7 %copy-start.3 = (f32[256,512]{1,0:T(8,128)S(1)}, f32[256,512]{1,0:T(8,128)}, u32[]{:S(2)}) copy-start(f32[256,512]{1,0:T(8,128)} %get-tuple-element.35) | copy-start | bytes 1572868
  91.4 18.7 %all-to-all-start.3 = ((bf16[32,8,512]{2,1,0:T(8,128)(2,1)}), bf16[32,8,512]{2,1,0:T(8,128)(2,1)S(1)}, u32[]{:S(2)}, u32[]{:S(2)}) async-start(bf16[32,8,512]{2,1,0:T(8,128)(2,1)} %shard_map.97), calls=%async_computation.3 | async-start | bytes 524288 | tf_op jit(solution)/shard_map/all_to_all | solution.py:25
  95.3 14.1 %collective-permute-start.4 = (bf16[1,256,128]{2,1,0:T(8,128)(2,1)S(1)}, bf16[1,256,128]{2,1,0:T(8,128)(2,1)S(1)}, u32[]{:S(2)}, u32[]{:S(2)}) collective-permute-start(bf16[1,256,128]{2,1,0:T(8,128)(2,1)S(1)} %get-tuple-element.41), channel_id=1, source_target_pairs={{0,8},{1,9},{2,10},{3,11},{4,12},{5,13},{6,14},{7,15},{8,0},{9,1},... | collective-permute-start | bytes 196616 | tf_op jit(solution)/shard_map/ppermute | solution.py:369
  98.0 11.3 %collective-permute-start.5 = (bf16[1,256,128]{2,1,0:T(8,128)(2,1)S(1)}, bf16[1,256,128]{2,1,0:T(8,128)(2,1)S(1)}, u32[]{:S(2)}, u32[]{:S(2)}) collective-permute-start(bf16[1,256,128]{2,1,0:T(8,128)(2,1)S(1)} %get-tuple-element.42), channel_id=1, source_target_pairs={{0,4},{1,5},{2,6},{3,7},{4,0},{5,1},{6,2},{7,3},{8,12},{9,13},{10,... | collective-permute-start | bytes 196616 | tf_op jit(solution)/shard_map/ppermute | solution.py:369
  99.5 9.8 %collective-permute-start.6 = (bf16[1,256,128]{2,1,0:T(8,128)(2,1)S(1)}, bf16[1,256,128]{2,1,0:T(8,128)(2,1)S(1)}, u32[]{:S(2)}, u32[]{:S(2)}) collective-permute-start(bf16[1,256,128]{2,1,0:T(8,128)(2,1)S(1)} %get-tuple-element.43), channel_id=1, source_target_pairs={{0,12},{1,13},{2,14},{3,15},{4,8},{5,9},{6,10},{7,11},{8,4},{9,5},... | collective-permute-start | bytes 196616 | tf_op jit(solution)/shard_map/ppermute | solution.py:369

commit v3 on v2

--- a/solution.py
+++ b/solution.py
@@ -28,6 +28,7 @@
 VMEM = pl.BlockSpec(memory_space=pltpu.VMEM)
 ANY = pl.BlockSpec(memory_space=pl.ANY)
 FULL_VMEM = 56 * 1024 * 1024
+LITTLE_VMEM = 8 * 1024 * 1024
 
 
 def shaped(shape, dtype=LOW):
@@ -89,6 +90,7 @@
 def attention_kernel(
     head_size,
     group,
+    chunk,
     stages,
     n_inner,
     me_ref,
@@ -117,8 +119,7 @@
     d_out_ref,
     d_out_t_ref,
     w_query_t_ref,
-    w_key_t_ref,
-    w_value_t_ref,
+    w_both_t_ref,
     feats_t_ref,
     grad_out_ref,
     key_ref,
@@ -129,15 +130,17 @@
     own_ref,
     grad_query_t_ref,
     out_t_ref,
-    grad_key_ref,
-    grad_value_ref,
+    grad_both_ref,
     keep_ref,
     send_ref,
+    prob_ref,
+    grad_score_ref,
     in_sem,
     out_sem,
 ):
     heads = lse_ref.shape[0]
     block, width = query_ref.shape
+    members = 4 * block
     scaling = head_size ** (-0.5)
     log2e = math.log2(math.e)
 
@@ -159,115 +162,117 @@
         copy.start()
         stores.append(copy)
 
-    first_need = load(by_match(arrived_hbm, 0), arrived_ref.at[0])
-    key_need = load(w_key_t_hbm, w_key_t_ref)
-    value_need = load(w_value_t_hbm, w_value_t_ref)
+    own = pl.ds(0, block)
+    first_needs = [
+        load(by_match(arrived_hbm, 0), arrived_ref.at[0]),
+        load(w_key_t_hbm, w_both_t_ref.at[pl.ds(0, width)]),
+    ]
     far_needs = [load(by_match(arrived_hbm, match), arrived_ref.at[match]) for match in (1, 2)]
-    own = pl.ds(0, block)
+    value_need = load(w_value_t_hbm, w_both_t_ref.at[pl.ds(width, width)])
     head_needs = [
         load(key_own_hbm, key_ref.at[own]),
+        load(query_t_hbm, query_t_ref),
+        load(value_own_t_hbm, value_t_ref.at[:, own]),
         load(value_own_hbm, value_ref.at[own]),
+        load(d_out_t_hbm, d_out_t_ref),
         load(key_own_t_hbm, key_t_ref.at[:, own]),
-        load(value_own_t_hbm, value_t_ref.at[:, own]),
-        load(query_t_hbm, query_t_ref),
-        load(d_out_t_hbm, d_out_t_ref),
         load(query_hbm, query_ref),
         load(d_out_hbm, d_out_ref),
     ]
     last_needs = [
+        load(feats_t_hbm, feats_t_ref.at[:, own]),
+        load(grad_out_hbm, grad_out_ref),
         load(w_query_t_hbm, w_query_t_ref),
-        load(feats_t_hbm, feats_t_ref),
-        load(grad_out_hbm, grad_out_ref),
     ]
-    first_need.wait()
-    key_need.wait()
+    for copy in first_needs:
+        copy.wait()
     for match in range(3):
         here = slice((match + 1) * block, (match + 2) * block)
         if match > 0:
             far_needs[match - 1].wait()
         far = arrived_ref[match].reshape(block, width)
-        key_ref[here] = dot_nt(far, w_key_t_ref[...]).astype(LOW)
-        key_t_ref[:, here] = dot_nt(w_key_t_ref[...], far).astype(LOW)
+        key_ref[here] = dot_nt(far, w_both_t_ref[:width]).astype(LOW)
+        key_t_ref[:, here] = dot_nt(w_both_t_ref[:width], far).astype(LOW)
         if match == 0:
             value_need.wait()
-        value_ref[here] = dot_nt(far, w_value_t_ref[...]).astype(LOW)
-        value_t_ref[:, here] = dot_nt(w_value_t_ref[...], far).astype(LOW)
+        value_ref[here] = dot_nt(far, w_both_t_ref[width:]).astype(LOW)
+        value_t_ref[:, here] = dot_nt(w_both_t_ref[width:], far).astype(LOW)
+        feats_t_ref[:, here] = far.T
     for copy in head_needs:
         copy.wait()
     span = group * head_size
+    row = lax.broadcasted_iota(jnp.int32, (span, block), 0) // head_size
+    col = lax.broadcasted_iota(jnp.int32, (block, span), 1) // head_size
     for first in range(0, heads, group):
         cols = slice(first * head_size, first * head_size + span)
-        key = key_ref[:, cols]
-        value = value_ref[:, cols]
-        row = lax.broadcasted_iota(jnp.int32, (span, block), 0) // head_size
-        col = lax.broadcasted_iota(jnp.int32, (block, span), 1) // head_size
         query_t = query_t_ref[cols, :]
-        d_out_t = d_out_t_ref[cols, :]
+        d_out_t = d_out_t_ref[cols, :] * scaling
         query = query_ref[:, cols]
         d_out = d_out_ref[:, cols]
         zero_t = jnp.zeros_like(query_t)
         zero = jnp.zeros_like(query)
-        grad_key = None
-        grad_value = None
         for inner in range(group):
             head = first + inner
             rows = slice(head * head_size, (head + 1) * head_size)
-            score = dot(key, jnp.where(row == inner, query_t, zero_t))
+            lanes = slice(inner * block, (inner + 1) * block)
             shift = lse_ref[head : head + 1, :] * log2e
-            prob = jnp.exp2(jnp.minimum(score * (scaling * log2e) - shift, 0.0))
-            prob_low = prob.astype(LOW)
-            out_t = dot(value_t_ref[rows, :], prob_low).astype(LOW)
+            query_one = jnp.where(row == inner, query_t, zero_t)
+            for start in range(0, members, chunk):
+                here = slice(start, start + chunk)
+                score = dot(key_ref[here, cols], query_one)
+                prob = jnp.exp2(jnp.minimum(score * (scaling * log2e) - shift, 0.0))
+                prob_ref[here, lanes] = prob.astype(LOW)
+            out_t = dot(value_t_ref[rows, :], prob_ref[:, lanes]).astype(LOW)
             out_t_ref[rows, :] = out_t
             d_rows = d_out_t_ref[rows, :]
             delta = jnp.sum(d_rows.astype(WIDE) * out_t.astype(WIDE), axis=0, keepdims=True) * scaling
-            grad_prob = dot(value, jnp.where(row == inner, d_out_t * scaling, zero_t))
-            grad_score = (prob * (grad_prob - delta)).astype(LOW)
-            grad_query_t_ref[rows, :] = dot(key_t_ref[rows, :], grad_score).astype(LOW)
-            part_key = dot(grad_score, jnp.where(col == inner, query, zero))
-            part_value = dot(prob_low, jnp.where(col == inner, d_out, zero))
-            grad_key = part_key if grad_key is None else grad_key + part_key
-            grad_value = part_value if grad_value is None else grad_value + part_value
-        grad_key_ref[:, cols] = grad_key.astype(LOW)
-        grad_value_ref[:, cols] = grad_value.astype(LOW)
+            d_out_one = jnp.where(row == inner, d_out_t, zero_t)
+            for start in range(0, members, chunk):
+                here = slice(start, start + chunk)
+                grad_prob = dot(value_ref[here, cols], d_out_one)
+                grad_score = prob_ref[here, lanes].astype(WIDE) * (grad_prob - delta)
+                grad_score_ref[here, lanes] = grad_score.astype(LOW)
+            grad_query_t_ref[rows, :] = dot(key_t_ref[rows, :], grad_score_ref[:, lanes]).astype(LOW)
+        queries = jnp.concatenate([jnp.where(col == inner, query, zero) for inner in range(group)], axis=0)
+        d_outs = jnp.concatenate([jnp.where(col == inner, d_out, zero) for inner in range(group)], axis=0)
+        for start in range(0, members, chunk):
+            here = slice(start, start + chunk)
+            grad_both_ref[here, cols] = dot(grad_score_ref[here, :], queries).astype(LOW)
+            later = slice(width + cols.start, width + cols.stop)
+            grad_both_ref[here, later] = dot(prob_ref[here, :], d_outs).astype(LOW)
     for copy in last_needs:
         copy.wait()
 
-    _, rows, cols = keep_ref.shape
-    n_outer = width // rows
+    _, tall, wide = keep_ref.shape
+    n_outer = width // tall
     me = me_ref[0]
     odd = me % 2 == 1
 
-    def place(matrix, total):
+    def place(start, total):
         low = total.astype(LOW)
-        for start in range(0, width, 2 * cols):
-            inner = (matrix * width + start) // cols
+        for offset in range(0, total.shape[1], 2 * wide):
+            inner = (start + offset) // wide
             for outer in range(n_outer):
                 differ = me ^ (outer * n_inner + inner)
                 slot = 0
                 for masks in stages:
                     for mask in masks:
                         slot = slot * 2 + jnp.where((differ & mask) != 0, 1, 0)
-                here = slice(outer * rows, (outer + 1) * rows)
-                left = low[here, start : start + cols]
-                right = low[here, start + cols : start + 2 * cols]
+                here = slice(outer * tall, (outer + 1) * tall)
+                left = low[here, offset : offset + wide]
+                right = low[here, offset + wide : offset + 2 * wide]
                 keep_ref[slot] = jnp.where(odd, right, left)
                 send_ref[slot] = jnp.where(odd, left, right)
 
-    feats_t = feats_t_ref[...]
-    far_t = [arrived_ref[match].reshape(block, width).T for match in range(3)]
-    place(3, dot(out_t_ref[...], grad_out_ref[...]))
-    place(0, dot_nt(feats_t, grad_query_t_ref[...]))
-    for matrix, ref in ((1, grad_key_ref), (2, grad_value_ref)):
-        total = dot(feats_t, ref[:block])
-        for match in range(3):
-            total = total + dot(far_t[match], ref[(match + 1) * block : (match + 2) * block])
-        place(matrix, total)
+    place(3 * width, dot(out_t_ref[...], grad_out_ref[...]))
+    place(0, dot_nt(feats_t_ref[:, :block], grad_query_t_ref[...]))
+    for start in range(0, 2 * width, block):
+        place(width + start, dot(feats_t_ref[...], grad_both_ref[:, start : start + block]))
     store(send_ref, send_hbm)
     store(keep_ref, keep_hbm)
     for member in range(4):
         here = slice(member * block, (member + 1) * block)
-        total = dot(grad_key_ref[here], w_key_t_ref[...])
-        total = total + dot(grad_value_ref[here], w_value_t_ref[...])
+        total = dot(grad_both_ref[here], w_both_t_ref[...])
         if member == 0:
             own_ref[...] = total + lax.dot_general(
                 grad_query_t_ref[...],
@@ -303,7 +308,7 @@
     )
     long, long_t = pltpu.VMEM((members, width), LOW), pltpu.VMEM((width, members), LOW)
     terms, own, keep, send = pl.pallas_call(
-        functools.partial(attention_kernel, head_size, group, stages, n_inner),
+        functools.partial(attention_kernel, head_size, group, 2 * block, stages, n_inner),
         out_shape=(shaped(arrived.shape), shaped((block, width), WIDE), shaped(half), shaped(half)),
         in_specs=[pl.BlockSpec(memory_space=pltpu.SMEM), VMEM] + [ANY] * 14,
         out_specs=(ANY,) * 4,
@@ -314,9 +319,8 @@
             plain,
             turned,
             square,
-            square,
-            square,
-            turned,
+            pltpu.VMEM((2 * width, width), LOW),
+            long_t,
             plain,
             long,
             long,
@@ -326,10 +330,11 @@
             pltpu.VMEM((block, width), WIDE),
             turned,
             turned,
-            long,
-            long,
+            pltpu.VMEM((members, 2 * width), LOW),
             pltpu.VMEM(half, LOW),
             pltpu.VMEM(half, LOW),
+            pltpu.VMEM((members, group * block), LOW),
+            pltpu.VMEM((members, group * block), LOW),
             pltpu.SemaphoreType.DMA((16,)),
             pltpu.SemaphoreType.DMA((6,)),
         ],
@@ -398,7 +403,7 @@
         out_shape=shaped((devices, piece, width)),
         in_specs=[pl.BlockSpec(memory_space=pltpu.SMEM), VMEM],
         out_specs=VMEM,
-        compiler_params=pltpu.CompilerParams(vmem_limit_bytes=FULL_VMEM),
+        compiler_params=pltpu.CompilerParams(vmem_limit_bytes=LITTLE_VMEM),
     )(partners, returned)
 
 
@@ -426,7 +431,6 @@
         ]
         if number == len(stages) - 1:
             summed = collect_pieces(returned, partners)
-            *parts, summed = lax.optimization_barrier((*parts, summed))
         keep, got = stage_sum(parts, masks, devices)
     back = exchange(summed).reshape(block, width)
     grad_nodes = (own + back.astype(WIDE)).astype(LOW)

time: 111 us -> 106 us (0.955)
  local copies, waits for them, and re-layouts: 4.17 us -> 2.7 us
  Pallas kernels: 23.2 us -> 21.9 us
  starting transfers between devices: 24.6 us -> 23.3 us
  waiting for transfers between devices: 55.3 us -> 54 us
    ppermute x7, waiting for transfers between devices: 27.8 us -> 9.53 us  [swap(): lax.ppermute(value, AXES, [(device, device ^ mask) for device in range(de...]
    all_to_all x4, waiting for transfers between devices: 27.6 us -> 44.4 us  [exchange(): return lax.all_to_all(pieces, AXES, split_axis=0, concat_axis=0, tiled=True)]
    unnamed x11 -> x9, local copies, waits for them, and re-layouts: 2.46 us -> 0.98 us
    all_to_all x4, starting transfers between devices: 16.6 us -> 15.3 us  [exchange(): return lax.all_to_all(pieces, AXES, split_axis=0, concat_axis=0, tiled=True)]
  transfers between devices with their start and end apart: 11 -> 11, of which waited for: 7 -> 5; matrix products, arithmetic and copies ran while one was open for 3% -> 2% of each run, Pallas kernels for 4% -> 5%
where the time goes in v3:
time: 106 us; the launch traced here: 105 us
  waiting for transfers between devices  54 us (51%)
  starting transfers between devices  23.3 us (22%)
  Pallas kernels  21.9 us (21%)
  local copies, waits for them, and re-layouts  2.7 us (3%)
  other arithmetic  2.7 us (3%)
    all_to_all x4, waiting for transfers between devices, exchange(): return lax.all_to_all(pieces, AXES, split_axis=0, concat_axis=0, tiled=True)  44.4 us
    pallas_call x1, Pallas kernels, attention(): pl.pallas_call(functools.partial(attention_kernel, head_size, group, 2 *...  16.3 us
    all_to_all x4, starting transfers between devices, exchange(): return lax.all_to_all(pieces, AXES, split_axis=0, concat_axis=0, tiled=True)  15.3 us
    ppermute x7, waiting for transfers between devices, swap(): lax.ppermute(value, AXES, [(device, device ^ mask) for device in range(de...  9.53 us
    ppermute x7, starting transfers between devices, swap(): lax.ppermute(value, AXES, [(device, device ^ mask) for device in range(de...  8.01 us
    pallas_call x1, Pallas kernels, project(): pl.pallas_call(project_kernel, out_shape=(plain, turned) * 4 + (square,)...  4 us
  transfers between devices with their start and end apart: 11, of which 5 were waited for; matrix products, arithmetic and copies ran while one was open for 2% of the time, Pallas kernels for 5%

profile of v3, /device:TPU:0, one launch (start us, length us, event | category | flops | bytes accessed | tf_op | source)
XLA Modules:
  0.0 105.3 jit_solution(4020110270162433983)
XLA Ops:
  0.6 0.0 copy-start.3
  0.6 7.3 %all-to-all-start = ((bf16[32,8,512]{2,1,0:T(8,128)(2,1)}), bf16[32,8,512]{2,1,0:T(8,128)(2,1)S(1)}, u32[]{:S(2)}, u32[]{:S(2)}) async-start(bf16[32,8,512]{2,1,0:T(8,128)(2,1)} %bitcast.8), calls=%async_computation | async-start | bytes 524288 | tf_op jit(solution)/shard_map/all_to_all | solution.py:25
  8.0 0.0 copy-done.3
  8.0 0.1 copy.12
  8.1 0.1 reshape.121
  8.2 10.1 %all-to-all-done = bf16[32,8,512]{2,1,0:T(8,128)(2,1)S(1)} async-done(((bf16[32,8,512]{2,1,0:T(8,128)(2,1)}), bf16[32,8,512]{2,1,0:T(8,128)(2,1)S(1)}, u32[]{:S(2)}, u32[]{:S(2)}) %all-to-all-start) | async-done | bytes 262176 | tf_op jit(solution)/shard_map/all_to_all | solution.py:25
  18.2 1.5 %gather_fusion = bf16[96,8,512]{2,1,0:T(8,128)(2,1)} fusion(bf16[32,8,512]{2,1,0:T(8,128)(2,1)S(1)} %all-to-all-done, s32[1024]{0:T(1024)S(1)} %pad_clamp_fusion), kind=kCustom, calls=%fused_computation | custom fusion | bytes 1573248 | tf_op jit(solution)/shard_map/gather | solution.py:419
  19.8 2.6 %all-to-all-start.1 = ((bf16[32,3,8,512]{3,2,1,0:T(8,128)(2,1)}), bf16[32,3,8,512]{3,2,1,0:T(8,128)(2,1)S(1)}, u32[]{:S(2)}, u32[]{:S(2)}) async-start(bf16[32,3,8,512]{3,2,1,0:T(8,128)(2,1)} %bitcast.2), calls=%async_computation.1 | async-start | bytes 1572864 | tf_op jit(solution)/shard_map/all_to_all | solution.py:25
  22.4 4.0 %shard_map.95 = (bf16[256,512]{1,0:T(8,128)(2,1)}, bf16[512,256]{1,0:T(8,128)(2,1)}, bf16[256,512]{1,0:T(8,128)(2,1)}, bf16[512,256]{1,0:T(8,128)(2,1)}, bf16[25...) custom-call(bf16[256,512]{1,0:T(8,128)(2,1)} %feats_ref.1, ...), custom_call_target="tpu_custom_call" | custom-call | flops 1073741824 | bytes 6291456 | tf_op jit(solution)/shard_map/pallas_call | solution.py:76
  26.4 17.5 %all-to-all-done.1.arrived_hbm = bf16[32,3,8,512]{3,2,1,0:T(8,128)(2,1)S(1)} async-done(((bf16[32,3,8,512]{3,2,1,0:T(8,128)(2,1)}), bf16[32,3,8,512]{3,2,1,0:T(8,128)(2,1)S(1)}, u32[]{:S(2)}, u32[]{:S(2)}) %all-to-all-start.1) | async-done | bytes 786464 | tf_op jit(solution)/shard_map/all_to_all | solution.py:25
  43.9 0.0 copy-start.1
  43.9 0.9 copy-done.1
  44.8 16.3 %shard_map.96 = (bf16[32,3,8,512]{3,2,1,0:T(8,128)(2,1)}, f32[256,512]{1,0:T(8,128)}, bf16[16,256,128]{2,1,0:T(8,128)(2,1)}, bf16[16,256,128]{2,1,0:T(8,128)(2,1)}) custom-call(s32[1]{0:T(128)} %bitcast.me_ref, f32[8,256]{1,0:T(8,128)} %lse_ref.1, bf16[32,3,8,512]{3,2,1,0:T(8,128)(2,1)} %copy-done.1, bf16[256,512]{1,0:T(8,128)(2,1)} %get-tuple-element.18.query_hbm, ...), custom_call_target="tpu_custom_call" | custom-call | flops 10200547328 | bytes 8388608 | tf_op jit(solution)/shard_map/pallas_call | solution.py:310
  61.1 0.0 copy-start
  61.1 0.1 collective-permute-start
  61.2 2.8 %all-to-all-start.2 = ((bf16[32,3,8,512]{3,2,1,0:T(8,128)(2,1)}), bf16[32,3,8,512]{3,2,1,0:T(8,128)(2,1)S(1)}, u32[]{:S(2)}, u32[]{:S(2)}) async-start(bf16[32,3,8,512]{3,2,1,0:T(8,128)(2,1)} %get-tuple-element.31), calls=%async_computation.2 | async-start | bytes 1572864 | tf_op jit(solution)/shard_map/all_to_all | solution.py:25
  64.0 0.1 collective-permute-done
  64.0 0.0 copy-done
  64.0 1.1 %add_convert_fusion.3 = (bf16[4,256,128]{2,1,0:T(8,128)(2,1)S(1)}, bf16[4,256,128]{2,1,0:T(8,128)(2,1)S(1)}, bf16[4,256,128]{2,1,0:T(8,128)(2,1)}, bf16[4,256,128]{2,1,0:T(8,128)(2,1)}) fusion(bf16[16,256,128]{2,1,0:T(8,128)(2,1)S(1)} %collective-permute-done, bf16[16,256,128]{2,1,0:T(8,128)(2,1)S(1)} %copy-done), kind=kLoop, calls=%fused_computation.6 | loop fusion | flops 2097152 | bytes 3145728 | tf_op jit(solution)/shard_map/convert_element_type | solution.py:430
  65.1 1.6 %collective-permute-start.1 = (bf16[4,256,128]{2,1,0:T(8,128)(2,1)}, bf16[4,256,128]{2,1,0:T(8,128)(2,1)S(1)}, u32[]{:S(2)}, u32[]{:S(2)}) collective-permute-start(bf16[4,256,128]{2,1,0:T(8,128)(2,1)} %get-tuple-element.37), channel_id=1, source_target_pairs={{0,16},{1,17},{2,18},{3,19},{4,20},{5,21},{6,22},{7,23},{8,24},{9,... | collective-permute-start | bytes 786440 | tf_op jit(solution)/shard_map/ppermute | solution.py:374
  66.7 1.5 %collective-permute-start.2 = (bf16[4,256,128]{2,1,0:T(8,128)(2,1)}, bf16[4,256,128]{2,1,0:T(8,128)(2,1)S(1)}, u32[]{:S(2)}, u32[]{:S(2)}) collective-permute-start(bf16[4,256,128]{2,1,0:T(8,128)(2,1)} %get-tuple-element.36), channel_id=1, source_target_pairs={{0,2},{1,3},{2,0},{3,1},{4,6},{5,7},{6,4},{7,5},{8,10},{9,11},{10,... | collective-permute-start | bytes 786440 | tf_op jit(solution)/shard_map/ppermute | solution.py:374
  68.2 0.4 collective-permute-start.3
  68.6 0.1 copy.13.partners_ref
  68.7 16.9 %all-to-all-done.2.returned_ref = bf16[32,3,8,512]{3,2,1,0:T(8,128)(2,1)S(1)} async-done(((bf16[32,3,8,512]{3,2,1,0:T(8,128)(2,1)}), bf16[32,3,8,512]{3,2,1,0:T(8,128)(2,1)S(1)}, u32[]{:S(2)}, u32[]{:S(2)}) %all-to-all-start.2) | async-done | bytes 786464 | tf_op jit(solution)/shard_map/all_to_all | solution.py:25
  85.6 1.6 %shard_map.97 = bf16[32,8,512]{2,1,0:T(8,128)(2,1)} custom-call(s32[32,3]{1,0:T(8,128)S(1)} %copy.13.partners_ref, bf16[32,3,8,512]{3,2,1,0:T(8,128)(2,1)S(1)} %all-to-all-done.2.returned_ref), custom_call_target="tpu_custom_call" | custom-call | tf_op jit(solution)/shard_map/pallas_call | solution.py:401
  87.2 2.6 %all-to-all-start.3 = ((bf16[32,8,512]{2,1,0:T(8,128)(2,1)}), bf16[32,8,512]{2,1,0:T(8,128)(2,1)S(1)}, u32[]{:S(2)}, u32[]{:S(2)}) async-start(bf16[32,8,512]{2,1,0:T(8,128)(2,1)} %shard_map.97), calls=%async_computation.3 | async-start | bytes 524288 | tf_op jit(solution)/shard_map/all_to_all | solution.py:25
  89.8 0.0 collective-permute-done.1
  89.8 0.0 collective-permute-done.2
  89.8 0.0 collective-permute-done.3
  89.8 0.1 add_convert_fusion.6
  89.9 0.0 copy-start.2
  89.9 2.7 %collective-permute-start.4 = (bf16[1,256,128]{2,1,0:T(8,128)(2,1)S(1)}, bf16[1,256,128]{2,1,0:T(8,128)(2,1)S(1)}, u32[]{:S(2)}, u32[]{:S(2)}) collective-permute-start(bf16[1,256,128]{2,1,0:T(8,128)(2,1)S(1)} %get-tuple-element.38), channel_id=1, source_target_pairs={{0,8},{1,9},{2,10},{3,11},{4,12},{5,13},{6,14},{7,15},{8,0},{9,1},... | collective-permute-start | bytes 196616 | tf_op jit(solution)/shard_map/ppermute | solution.py:374
  92.7 1.5 %collective-permute-start.5 = (bf16[1,256,128]{2,1,0:T(8,128)(2,1)S(1)}, bf16[1,256,128]{2,1,0:T(8,128)(2,1)S(1)}, u32[]{:S(2)}, u32[]{:S(2)}) collective-permute-start(bf16[1,256,128]{2,1,0:T(8,128)(2,1)S(1)} %get-tuple-element.40), channel_id=1, source_target_pairs={{0,4},{1,5},{2,6},{3,7},{4,0},{5,1},{6,2},{7,3},{8,12},{9,13},{10,... | collective-permute-start | bytes 196616 | tf_op jit(solution)/shard_map/ppermute | solution.py:374
  94.2 0.2 collective-permute-start.6
  94.4 9.4 %collective-permute-done.4 = bf16[1,256,128]{2,1,0:T(8,128)(2,1)S(1)} collective-permute-done((bf16[1,256,128]{2,1,0:T(8,128)(2,1)S(1)}, bf16[1,256,128]{2,1,0:T(8,128)(2,1)S(1)}, u32[]{:S(2)}, u32[]{:S(2)}) %collective-permute-start.4) | collective-permute-done | bytes 65568 | tf_op jit(solution)/shard_map/ppermute | solution.py:374
  103.8 0.0 collective-permute-done.5
  103.8 0.0 collective-permute-done.6
  103.8 0.7 add_bitcast_fusion
  104.6 0.0 all-to-all-done.3
  104.6 0.0 copy-done.2
  104.6 0.8 fusion
  (2 shorter events, 0.0 us)
Async XLA Ops:
  0.6 7.3 %copy-start.3 = (s32[32,3]{0,1:T(4,128)S(1)}, s32[32,3]{0,1:T(4,128)}, u32[]{:S(2)}) copy-start(s32[32,3]{0,1:T(4,128)} %param.15) | copy-start | bytes 1156
  0.6 17.6 %all-to-all-start = ((bf16[32,8,512]{2,1,0:T(8,128)(2,1)}), bf16[32,8,512]{2,1,0:T(8,128)(2,1)S(1)}, u32[]{:S(2)}, u32[]{:S(2)}) async-start(bf16[32,8,512]{2,1,0:T(8,128)(2,1)} %bitcast.8), calls=%async_computation | async-start | bytes 524288 | tf_op jit(solution)/shard_map/all_to_all | solution.py:25
  19.8 24.1 %all-to-all-start.1 = ((bf16[32,3,8,512]{3,2,1,0:T(8,128)(2,1)}), bf16[32,3,8,512]{3,2,1,0:T(8,128)(2,1)S(1)}, u32[]{:S(2)}, u32[]{:S(2)}) async-start(bf16[32,3,8,512]{3,2,1,0:T(8,128)(2,1)} %bitcast.2), calls=%async_computation.1 | async-start | bytes 1572864 | tf_op jit(solution)/shard_map/all_to_all | solution.py:25
  43.9 0.9 copy-start.1
  61.1 2.9 %copy-start = (bf16[16,256,128]{2,1,0:T(8,128)(2,1)S(1)}, bf16[16,256,128]{2,1,0:T(8,128)(2,1)}, u32[]{:S(2)}) copy-start(bf16[16,256,128]{2,1,0:T(8,128)(2,1)} %get-tuple-element.32) | copy-start | bytes 3145732
  61.1 2.9 %collective-permute-start = (bf16[16,256,128]{2,1,0:T(8,128)(2,1)}, bf16[16,256,128]{2,1,0:T(8,128)(2,1)S(1)}, u32[]{:S(2)}, u32[]{:S(2)}) collective-permute-start(bf16[16,256,128]{2,1,0:T(8,128)(2,1)} %get-tuple-element.33), channel_id=1, source_target_pairs={{0,1},{1,0},{2,3},{3,2},{4,5},{5,4},{6,7},{7,6},{8,9},{9,8},{10,11... | collective-permute-start | bytes 3145736 | tf_op jit(solution)/shard_map/ppermute | solution.py:374
  61.2 24.4 %all-to-all-start.2 = ((bf16[32,3,8,512]{3,2,1,0:T(8,128)(2,1)}), bf16[32,3,8,512]{3,2,1,0:T(8,128)(2,1)S(1)}, u32[]{:S(2)}, u32[]{:S(2)}) async-start(bf16[32,3,8,512]{3,2,1,0:T(8,128)(2,1)} %get-tuple-element.31), calls=%async_computation.2 | async-start | bytes 1572864 | tf_op jit(solution)/shard_map/all_to_all | solution.py:25
  65.1 24.7 %collective-permute-start.1 = (bf16[4,256,128]{2,1,0:T(8,128)(2,1)}, bf16[4,256,128]{2,1,0:T(8,128)(2,1)S(1)}, u32[]{:S(2)}, u32[]{:S(2)}) collective-permute-start(bf16[4,256,128]{2,1,0:T(8,128)(2,1)} %get-tuple-element.37), channel_id=1, source_target_pairs={{0,16},{1,17},{2,18},{3,19},{4,20},{5,21},{6,22},{7,23},{8,24},{9,... | collective-permute-start | bytes 786440 | tf_op jit(solution)/shard_map/ppermute | solution.py:374
  66.7 23.1 %collective-permute-start.2 = (bf16[4,256,128]{2,1,0:T(8,128)(2,1)}, bf16[4,256,128]{2,1,0:T(8,128)(2,1)S(1)}, u32[]{:S(2)}, u32[]{:S(2)}) collective-permute-start(bf16[4,256,128]{2,1,0:T(8,128)(2,1)} %get-tuple-element.36), channel_id=1, source_target_pairs={{0,2},{1,3},{2,0},{3,1},{4,6},{5,7},{6,4},{7,5},{8,10},{9,11},{10,... | collective-permute-start | bytes 786440 | tf_op jit(solution)/shard_map/ppermute | solution.py:374
  68.2 21.6 %collective-permute-start.3 = (bf16[4,256,128]{2,1,0:T(8,128)(2,1)S(1)}, bf16[4,256,128]{2,1,0:T(8,128)(2,1)S(1)}, u32[]{:S(2)}, u32[]{:S(2)}) collective-permute-start(bf16[4,256,128]{2,1,0:T(8,128)(2,1)S(1)} %get-tuple-element.35), channel_id=1, source_target_pairs={{0,18},{1,19},{2,16},{3,17},{4,22},{5,23},{6,20},{7,21},{8,26},{9,... | collective-permute-start | bytes 786440 | tf_op jit(solution)/shard_map/ppermute | solution.py:374
  87.2 17.4 %all-to-all-start.3 = ((bf16[32,8,512]{2,1,0:T(8,128)(2,1)}), bf16[32,8,512]{2,1,0:T(8,128)(2,1)S(1)}, u32[]{:S(2)}, u32[]{:S(2)}) async-start(bf16[32,8,512]{2,1,0:T(8,128)(2,1)} %shard_map.97), calls=%async_computation.3 | async-start | bytes 524288 | tf_op jit(solution)/shard_map/all_to_all | solution.py:25
  89.9 14.6 %copy-start.2 = (f32[256,512]{1,0:T(8,128)S(1)}, f32[256,512]{1,0:T(8,128)}, u32[]{:S(2)}) copy-start(f32[256,512]{1,0:T(8,128)} %get-tuple-element.30) | copy-start | bytes 1572868
  89.9 13.9 %collective-permute-start.4 = (bf16[1,256,128]{2,1,0:T(8,128)(2,1)S(1)}, bf16[1,256,128]{2,1,0:T(8,128)(2,1)S(1)}, u32[]{:S(2)}, u32[]{:S(2)}) collective-permute-start(bf16[1,256,128]{2,1,0:T(8,128)(2,1)S(1)} %get-tuple-element.38), channel_id=1, source_target_pairs={{0,8},{1,9},{2,10},{3,11},{4,12},{5,13},{6,14},{7,15},{8,0},{9,1},... | collective-permute-start | bytes 196616 | tf_op jit(solution)/shard_map/ppermute | solution.py:374
  92.7 11.2 %collective-permute-start.5 = (bf16[1,256,128]{2,1,0:T(8,128)(2,1)S(1)}, bf16[1,256,128]{2,1,0:T(8,128)(2,1)S(1)}, u32[]{:S(2)}, u32[]{:S(2)}) collective-permute-start(bf16[1,256,128]{2,1,0:T(8,128)(2,1)S(1)} %get-tuple-element.40), channel_id=1, source_target_pairs={{0,4},{1,5},{2,6},{3,7},{4,0},{5,1},{6,2},{7,3},{8,12},{9,13},{10,... | collective-permute-start | bytes 196616 | tf_op jit(solution)/shard_map/ppermute | solution.py:374
  94.2 9.6 %collective-permute-start.6 = (bf16[1,256,128]{2,1,0:T(8,128)(2,1)S(1)}, bf16[1,256,128]{2,1,0:T(8,128)(2,1)S(1)}, u32[]{:S(2)}, u32[]{:S(2)}) collective-permute-start(bf16[1,256,128]{2,1,0:T(8,128)(2,1)S(1)} %get-tuple-element.39), channel_id=1, source_target_pairs={{0,12},{1,13},{2,14},{3,15},{4,8},{5,9},{6,10},{7,11},{8,4},{9,5},... | collective-permute-start | bytes 196616 | tf_op jit(solution)/shard_map/ppermute | solution.py:374

commit v4 on v3

--- a/solution.py
+++ b/solution.py
@@ -90,6 +90,7 @@
 def attention_kernel(
     head_size,
     group,
+    together,
     chunk,
     stages,
     n_inner,
@@ -191,55 +192,71 @@
         if match > 0:
             far_needs[match - 1].wait()
         far = arrived_ref[match].reshape(block, width)
-        key_ref[here] = dot_nt(far, w_both_t_ref[:width]).astype(LOW)
-        key_t_ref[:, here] = dot_nt(w_both_t_ref[:width], far).astype(LOW)
+        far_key = dot_nt(far, w_both_t_ref[:width]).astype(LOW)
+        key_ref[here] = far_key
+        key_t_ref[:, here] = far_key.T
         if match == 0:
             value_need.wait()
-        value_ref[here] = dot_nt(far, w_both_t_ref[width:]).astype(LOW)
-        value_t_ref[:, here] = dot_nt(w_both_t_ref[width:], far).astype(LOW)
+        far_value = dot_nt(far, w_both_t_ref[width:]).astype(LOW)
+        value_ref[here] = far_value
+        value_t_ref[:, here] = far_value.T
         feats_t_ref[:, here] = far.T
     for copy in head_needs:
         copy.wait()
     span = group * head_size
     row = lax.broadcasted_iota(jnp.int32, (span, block), 0) // head_size
     col = lax.broadcasted_iota(jnp.int32, (block, span), 1) // head_size
-    for first in range(0, heads, group):
-        cols = slice(first * head_size, first * head_size + span)
-        query_t = query_t_ref[cols, :]
-        d_out_t = d_out_t_ref[cols, :] * scaling
-        query = query_ref[:, cols]
-        d_out = d_out_ref[:, cols]
-        zero_t = jnp.zeros_like(query_t)
-        zero = jnp.zeros_like(query)
-        for inner in range(group):
-            head = first + inner
+    for batch in range(0, heads, together):
+        batch_heads = range(batch, batch + together)
+        deltas = {}
+
+        def places(head):
+            first = head - head % group
+            cols = slice(first * head_size, first * head_size + span)
             rows = slice(head * head_size, (head + 1) * head_size)
-            lanes = slice(inner * block, (inner + 1) * block)
+            lanes = slice((head - batch) * block, (head - batch + 1) * block)
+            return head % group, cols, rows, lanes
+
+        for head in batch_heads:
+            inner, cols, rows, lanes = places(head)
             shift = lse_ref[head : head + 1, :] * log2e
-            query_one = jnp.where(row == inner, query_t, zero_t)
+            query_t = query_t_ref[cols, :]
+            query_one = jnp.where(row == inner, query_t, jnp.zeros_like(query_t))
             for start in range(0, members, chunk):
                 here = slice(start, start + chunk)
                 score = dot(key_ref[here, cols], query_one)
                 prob = jnp.exp2(jnp.minimum(score * (scaling * log2e) - shift, 0.0))
                 prob_ref[here, lanes] = prob.astype(LOW)
+        for head in batch_heads:
+            inner, cols, rows, lanes = places(head)
             out_t = dot(value_t_ref[rows, :], prob_ref[:, lanes]).astype(LOW)
             out_t_ref[rows, :] = out_t
-            d_rows = d_out_t_ref[rows, :]
-            delta = jnp.sum(d_rows.astype(WIDE) * out_t.astype(WIDE), axis=0, keepdims=True) * scaling
-            d_out_one = jnp.where(row == inner, d_out_t, zero_t)
+            d_rows = d_out_t_ref[rows, :].astype(WIDE)
+            deltas[head] = jnp.sum(d_rows * out_t.astype(WIDE), axis=0, keepdims=True) * scaling
+        for head in batch_heads:
+            inner, cols, rows, lanes = places(head)
+            d_out_t = d_out_t_ref[cols, :] * scaling
+            d_out_one = jnp.where(row == inner, d_out_t, jnp.zeros_like(d_out_t))
             for start in range(0, members, chunk):
                 here = slice(start, start + chunk)
                 grad_prob = dot(value_ref[here, cols], d_out_one)
-                grad_score = prob_ref[here, lanes].astype(WIDE) * (grad_prob - delta)
+                grad_score = prob_ref[here, lanes].astype(WIDE) * (grad_prob - deltas[head])
                 grad_score_ref[here, lanes] = grad_score.astype(LOW)
+        for first in range(batch, batch + together, group):
+            _, cols, _, _ = places(first)
+            later = slice(width + cols.start, width + cols.stop)
+            lanes = slice((first - batch) * block, (first - batch + group) * block)
+            query, d_out = query_ref[:, cols], d_out_ref[:, cols]
+            queries = [jnp.where(col == inner, query, jnp.zeros_like(query)) for inner in range(group)]
+            d_outs = [jnp.where(col == inner, d_out, jnp.zeros_like(d_out)) for inner in range(group)]
+            queries, d_outs = jnp.concatenate(queries, axis=0), jnp.concatenate(d_outs, axis=0)
+            for start in range(0, members, chunk):
+                here = slice(start, start + chunk)
+                grad_both_ref[here, cols] = dot(grad_score_ref[here, lanes], queries).astype(LOW)
+                grad_both_ref[here, later] = dot(prob_ref[here, lanes], d_outs).astype(LOW)
+        for head in batch_heads:
+            inner, cols, rows, lanes = places(head)
             grad_query_t_ref[rows, :] = dot(key_t_ref[rows, :], grad_score_ref[:, lanes]).astype(LOW)
-        queries = jnp.concatenate([jnp.where(col == inner, query, zero) for inner in range(group)], axis=0)
-        d_outs = jnp.concatenate([jnp.where(col == inner, d_out, zero) for inner in range(group)], axis=0)
-        for start in range(0, members, chunk):
-            here = slice(start, start + chunk)
-            grad_both_ref[here, cols] = dot(grad_score_ref[here, :], queries).astype(LOW)
-            later = slice(width + cols.start, width + cols.stop)
-            grad_both_ref[here, later] = dot(prob_ref[here, :], d_outs).astype(LOW)
     for copy in last_needs:
         copy.wait()
 
@@ -295,6 +312,7 @@
     head_size = width // heads
     members = 4 * block
     group = max(1, 128 // head_size)
+    together = min(heads, group)
     devices, _, piece, _ = arrived.shape
     whole_tiles = piece % 8 == 0
     if not whole_tiles:
@@ -308,7 +326,7 @@
     )
     long, long_t = pltpu.VMEM((members, width), LOW), pltpu.VMEM((width, members), LOW)
     terms, own, keep, send = pl.pallas_call(
-        functools.partial(attention_kernel, head_size, group, 2 * block, stages, n_inner),
+        functools.partial(attention_kernel, head_size, group, together, 2 * block, stages, n_inner),
         out_shape=(shaped(arrived.shape), shaped((block, width), WIDE), shaped(half), shaped(half)),
         in_specs=[pl.BlockSpec(memory_space=pltpu.SMEM), VMEM] + [ANY] * 14,
         out_specs=(ANY,) * 4,
@@ -333,8 +351,8 @@
             pltpu.VMEM((members, 2 * width), LOW),
             pltpu.VMEM(half, LOW),
             pltpu.VMEM(half, LOW),
-            pltpu.VMEM((members, group * block), LOW),
-            pltpu.VMEM((members, group * block), LOW),
+            pltpu.VMEM((members, together * block), LOW),
+            pltpu.VMEM((members, together * block), LOW),
             pltpu.SemaphoreType.DMA((16,)),
             pltpu.SemaphoreType.DMA((6,)),
         ],

time: 106 us -> 103 us (0.972)
  Pallas kernels: 21.9 us -> 19.3 us
    pallas_call x1, Pallas kernels: 16.3 us -> 13.7 us  [attention(): pl.pallas_call(functools.partial(attention_kernel, head_size, group, toge...]
where the time goes in v4:
time: 103 us
  waiting for transfers between devices  54 us (52%)
  starting transfers between devices  23.3 us (23%)
  Pallas kernels  19.3 us (19%)
  local copies, waits for them, and re-layouts  2.7 us (3%)
  other arithmetic  2.7 us (3%)
    all_to_all x4, waiting for transfers between devices, exchange(): return lax.all_to_all(pieces, AXES, split_axis=0, concat_axis=0, tiled=True)  44.4 us
    all_to_all x4, starting transfers between devices, exchange(): return lax.all_to_all(pieces, AXES, split_axis=0, concat_axis=0, tiled=True)  15.3 us
    pallas_call x1, Pallas kernels, attention(): pl.pallas_call(functools.partial(attention_kernel, head_size, group, toge...  13.7 us
    ppermute x7, waiting for transfers between devices, swap(): lax.ppermute(value, AXES, [(device, device ^ mask) for device in range(de...  9.53 us
    ppermute x7, starting transfers between devices, swap(): lax.ppermute(value, AXES, [(device, device ^ mask) for device in range(de...  8.01 us
    pallas_call x1, Pallas kernels, project(): pl.pallas_call(project_kernel, out_shape=(plain, turned) * 4 + (square,)...  4 us
  transfers between devices with their start and end apart: 11, of which 5 were waited for; matrix products, arithmetic and copies ran while one was open for 2% of the time, Pallas kernels for 5%

profile of v4, /device:TPU:0, one launch (start us, length us, event | category | flops | bytes accessed | tf_op | source)
XLA Modules:
  0.0 102.7 jit_solution(10338704542544718314)
XLA Ops:
  0.6 0.0 copy-start.3
  0.6 7.3 %all-to-all-start = ((bf16[32,8,512]{2,1,0:T(8,128)(2,1)}), bf16[32,8,512]{2,1,0:T(8,128)(2,1)S(1)}, u32[]{:S(2)}, u32[]{:S(2)}) async-start(bf16[32,8,512]{2,1,0:T(8,128)(2,1)} %bitcast.8), calls=%async_computation | async-start | bytes 524288 | tf_op jit(solution)/shard_map/all_to_all | solution.py:25
  8.0 0.0 copy-done.3
  8.0 0.1 copy.12
  8.1 0.1 reshape.121
  8.2 10.1 %all-to-all-done = bf16[32,8,512]{2,1,0:T(8,128)(2,1)S(1)} async-done(((bf16[32,8,512]{2,1,0:T(8,128)(2,1)}), bf16[32,8,512]{2,1,0:T(8,128)(2,1)S(1)}, u32[]{:S(2)}, u32[]{:S(2)}) %all-to-all-start) | async-done | bytes 262176 | tf_op jit(solution)/shard_map/all_to_all | solution.py:25
  18.2 1.5 %gather_fusion = bf16[96,8,512]{2,1,0:T(8,128)(2,1)} fusion(bf16[32,8,512]{2,1,0:T(8,128)(2,1)S(1)} %all-to-all-done, s32[1024]{0:T(1024)S(1)} %pad_clamp_fusion), kind=kCustom, calls=%fused_computation | custom fusion | bytes 1573248 | tf_op jit(solution)/shard_map/gather | solution.py:437
  19.8 2.6 %all-to-all-start.1 = ((bf16[32,3,8,512]{3,2,1,0:T(8,128)(2,1)}), bf16[32,3,8,512]{3,2,1,0:T(8,128)(2,1)S(1)}, u32[]{:S(2)}, u32[]{:S(2)}) async-start(bf16[32,3,8,512]{3,2,1,0:T(8,128)(2,1)} %bitcast.2), calls=%async_computation.1 | async-start | bytes 1572864 | tf_op jit(solution)/shard_map/all_to_all | solution.py:25
  22.4 4.0 %shard_map.95 = (bf16[256,512]{1,0:T(8,128)(2,1)}, bf16[512,256]{1,0:T(8,128)(2,1)}, bf16[256,512]{1,0:T(8,128)(2,1)}, bf16[512,256]{1,0:T(8,128)(2,1)}, bf16[25...) custom-call(bf16[256,512]{1,0:T(8,128)(2,1)} %feats_ref.1, ...), custom_call_target="tpu_custom_call" | custom-call | flops 1073741824 | bytes 6291456 | tf_op jit(solution)/shard_map/pallas_call | solution.py:76
  26.4 17.5 %all-to-all-done.1.arrived_hbm = bf16[32,3,8,512]{3,2,1,0:T(8,128)(2,1)S(1)} async-done(((bf16[32,3,8,512]{3,2,1,0:T(8,128)(2,1)}), bf16[32,3,8,512]{3,2,1,0:T(8,128)(2,1)S(1)}, u32[]{:S(2)}, u32[]{:S(2)}) %all-to-all-start.1) | async-done | bytes 786464 | tf_op jit(solution)/shard_map/all_to_all | solution.py:25
  43.9 0.0 copy-start.1
  43.9 0.9 copy-done.1
  44.8 13.7 %shard_map.96 = (bf16[32,3,8,512]{3,2,1,0:T(8,128)(2,1)}, f32[256,512]{1,0:T(8,128)}, bf16[16,256,128]{2,1,0:T(8,128)(2,1)}, bf16[16,256,128]{2,1,0:T(8,128)(2,1)}) custom-call(s32[1]{0:T(128)} %bitcast.me_ref, f32[8,256]{1,0:T(8,128)} %lse_ref.1, bf16[32,3,8,512]{3,2,1,0:T(8,128)(2,1)} %copy-done.1, bf16[256,512]{1,0:T(8,128)(2,1)} %get-tuple-element.18.query_hbm, ...), custom_call_target="tpu_custom_call" | custom-call | flops 10200547328 | bytes 8388608 | tf_op jit(solution)/shard_map/pallas_call | solution.py:328
  58.5 0.0 copy-start
  58.5 0.1 collective-permute-start
  58.6 2.8 %all-to-all-start.2 = ((bf16[32,3,8,512]{3,2,1,0:T(8,128)(2,1)}), bf16[32,3,8,512]{3,2,1,0:T(8,128)(2,1)S(1)}, u32[]{:S(2)}, u32[]{:S(2)}) async-start(bf16[32,3,8,512]{3,2,1,0:T(8,128)(2,1)} %get-tuple-element.31), calls=%async_computation.2 | async-start | bytes 1572864 | tf_op jit(solution)/shard_map/all_to_all | solution.py:25
  61.4 0.1 collective-permute-done
  61.4 0.0 copy-done
  61.4 1.1 %add_convert_fusion.3 = (bf16[4,256,128]{2,1,0:T(8,128)(2,1)S(1)}, bf16[4,256,128]{2,1,0:T(8,128)(2,1)S(1)}, bf16[4,256,128]{2,1,0:T(8,128)(2,1)}, bf16[4,256,128]{2,1,0:T(8,128)(2,1)}) fusion(bf16[16,256,128]{2,1,0:T(8,128)(2,1)S(1)} %collective-permute-done, bf16[16,256,128]{2,1,0:T(8,128)(2,1)S(1)} %copy-done), kind=kLoop, calls=%fused_computation.6 | loop fusion | flops 2097152 | bytes 3145728 | tf_op jit(solution)/shard_map/convert_element_type | solution.py:448
  62.5 1.6 %collective-permute-start.1 = (bf16[4,256,128]{2,1,0:T(8,128)(2,1)}, bf16[4,256,128]{2,1,0:T(8,128)(2,1)S(1)}, u32[]{:S(2)}, u32[]{:S(2)}) collective-permute-start(bf16[4,256,128]{2,1,0:T(8,128)(2,1)} %get-tuple-element.37), channel_id=1, source_target_pairs={{0,16},{1,17},{2,18},{3,19},{4,20},{5,21},{6,22},{7,23},{8,24},{9,... | collective-permute-start | bytes 786440 | tf_op jit(solution)/shard_map/ppermute | solution.py:392
  64.1 1.5 %collective-permute-start.2 = (bf16[4,256,128]{2,1,0:T(8,128)(2,1)}, bf16[4,256,128]{2,1,0:T(8,128)(2,1)S(1)}, u32[]{:S(2)}, u32[]{:S(2)}) collective-permute-start(bf16[4,256,128]{2,1,0:T(8,128)(2,1)} %get-tuple-element.36), channel_id=1, source_target_pairs={{0,2},{1,3},{2,0},{3,1},{4,6},{5,7},{6,4},{7,5},{8,10},{9,11},{10,... | collective-permute-start | bytes 786440 | tf_op jit(solution)/shard_map/ppermute | solution.py:392
  65.6 0.4 collective-permute-start.3
  66.0 0.1 copy.13.partners_ref
  66.1 16.9 %all-to-all-done.2.returned_ref = bf16[32,3,8,512]{3,2,1,0:T(8,128)(2,1)S(1)} async-done(((bf16[32,3,8,512]{3,2,1,0:T(8,128)(2,1)}), bf16[32,3,8,512]{3,2,1,0:T(8,128)(2,1)S(1)}, u32[]{:S(2)}, u32[]{:S(2)}) %all-to-all-start.2) | async-done | bytes 786464 | tf_op jit(solution)/shard_map/all_to_all | solution.py:25
  83.0 1.6 %shard_map.97 = bf16[32,8,512]{2,1,0:T(8,128)(2,1)} custom-call(s32[32,3]{1,0:T(8,128)S(1)} %copy.13.partners_ref, bf16[32,3,8,512]{3,2,1,0:T(8,128)(2,1)S(1)} %all-to-all-done.2.returned_ref), custom_call_target="tpu_custom_call" | custom-call | tf_op jit(solution)/shard_map/pallas_call | solution.py:419
  84.6 2.6 %all-to-all-start.3 = ((bf16[32,8,512]{2,1,0:T(8,128)(2,1)}), bf16[32,8,512]{2,1,0:T(8,128)(2,1)S(1)}, u32[]{:S(2)}, u32[]{:S(2)}) async-start(bf16[32,8,512]{2,1,0:T(8,128)(2,1)} %shard_map.97), calls=%async_computation.3 | async-start | bytes 524288 | tf_op jit(solution)/shard_map/all_to_all | solution.py:25
  87.2 0.0 collective-permute-done.1
  87.2 0.0 collective-permute-done.2
  87.2 0.0 collective-permute-done.3
  87.2 0.1 add_convert_fusion.6
  87.3 0.0 copy-start.2
  87.3 2.7 %collective-permute-start.4 = (bf16[1,256,128]{2,1,0:T(8,128)(2,1)S(1)}, bf16[1,256,128]{2,1,0:T(8,128)(2,1)S(1)}, u32[]{:S(2)}, u32[]{:S(2)}) collective-permute-start(bf16[1,256,128]{2,1,0:T(8,128)(2,1)S(1)} %get-tuple-element.38), channel_id=1, source_target_pairs={{0,8},{1,9},{2,10},{3,11},{4,12},{5,13},{6,14},{7,15},{8,0},{9,1},... | collective-permute-start | bytes 196616 | tf_op jit(solution)/shard_map/ppermute | solution.py:392
  90.1 1.5 %collective-permute-start.5 = (bf16[1,256,128]{2,1,0:T(8,128)(2,1)S(1)}, bf16[1,256,128]{2,1,0:T(8,128)(2,1)S(1)}, u32[]{:S(2)}, u32[]{:S(2)}) collective-permute-start(bf16[1,256,128]{2,1,0:T(8,128)(2,1)S(1)} %get-tuple-element.40), channel_id=1, source_target_pairs={{0,4},{1,5},{2,6},{3,7},{4,0},{5,1},{6,2},{7,3},{8,12},{9,13},{10,... | collective-permute-start | bytes 196616 | tf_op jit(solution)/shard_map/ppermute | solution.py:392
  91.6 0.2 collective-permute-start.6
  91.8 9.4 %collective-permute-done.4 = bf16[1,256,128]{2,1,0:T(8,128)(2,1)S(1)} collective-permute-done((bf16[1,256,128]{2,1,0:T(8,128)(2,1)S(1)}, bf16[1,256,128]{2,1,0:T(8,128)(2,1)S(1)}, u32[]{:S(2)}, u32[]{:S(2)}) %collective-permute-start.4) | collective-permute-done | bytes 65568 | tf_op jit(solution)/shard_map/ppermute | solution.py:392
  101.2 0.0 collective-permute-done.5
  101.2 0.0 collective-permute-done.6
  101.2 0.7 add_bitcast_fusion
  102.0 0.0 all-to-all-done.3
  102.0 0.0 copy-done.2
  102.0 0.8 fusion
  (2 shorter events, 0.0 us)
Async XLA Ops:
  0.6 7.3 %copy-start.3 = (s32[32,3]{0,1:T(4,128)S(1)}, s32[32,3]{0,1:T(4,128)}, u32[]{:S(2)}) copy-start(s32[32,3]{0,1:T(4,128)} %param.15) | copy-start | bytes 1156
  0.6 17.6 %all-to-all-start = ((bf16[32,8,512]{2,1,0:T(8,128)(2,1)}), bf16[32,8,512]{2,1,0:T(8,128)(2,1)S(1)}, u32[]{:S(2)}, u32[]{:S(2)}) async-start(bf16[32,8,512]{2,1,0:T(8,128)(2,1)} %bitcast.8), calls=%async_computation | async-start | bytes 524288 | tf_op jit(solution)/shard_map/all_to_all | solution.py:25
  19.8 24.1 %all-to-all-start.1 = ((bf16[32,3,8,512]{3,2,1,0:T(8,128)(2,1)}), bf16[32,3,8,512]{3,2,1,0:T(8,128)(2,1)S(1)}, u32[]{:S(2)}, u32[]{:S(2)}) async-start(bf16[32,3,8,512]{3,2,1,0:T(8,128)(2,1)} %bitcast.2), calls=%async_computation.1 | async-start | bytes 1572864 | tf_op jit(solution)/shard_map/all_to_all | solution.py:25
  43.9 0.9 copy-start.1
  58.5 2.9 %copy-start = (bf16[16,256,128]{2,1,0:T(8,128)(2,1)S(1)}, bf16[16,256,128]{2,1,0:T(8,128)(2,1)}, u32[]{:S(2)}) copy-start(bf16[16,256,128]{2,1,0:T(8,128)(2,1)} %get-tuple-element.32) | copy-start | bytes 3145732
  58.5 2.9 %collective-permute-start = (bf16[16,256,128]{2,1,0:T(8,128)(2,1)}, bf16[16,256,128]{2,1,0:T(8,128)(2,1)S(1)}, u32[]{:S(2)}, u32[]{:S(2)}) collective-permute-start(bf16[16,256,128]{2,1,0:T(8,128)(2,1)} %get-tuple-element.33), channel_id=1, source_target_pairs={{0,1},{1,0},{2,3},{3,2},{4,5},{5,4},{6,7},{7,6},{8,9},{9,8},{10,11... | collective-permute-start | bytes 3145736 | tf_op jit(solution)/shard_map/ppermute | solution.py:392
  58.6 24.4 %all-to-all-start.2 = ((bf16[32,3,8,512]{3,2,1,0:T(8,128)(2,1)}), bf16[32,3,8,512]{3,2,1,0:T(8,128)(2,1)S(1)}, u32[]{:S(2)}, u32[]{:S(2)}) async-start(bf16[32,3,8,512]{3,2,1,0:T(8,128)(2,1)} %get-tuple-element.31), calls=%async_computation.2 | async-start | bytes 1572864 | tf_op jit(solution)/shard_map/all_to_all | solution.py:25
  62.5 24.7 %collective-permute-start.1 = (bf16[4,256,128]{2,1,0:T(8,128)(2,1)}, bf16[4,256,128]{2,1,0:T(8,128)(2,1)S(1)}, u32[]{:S(2)}, u32[]{:S(2)}) collective-permute-start(bf16[4,256,128]{2,1,0:T(8,128)(2,1)} %get-tuple-element.37), channel_id=1, source_target_pairs={{0,16},{1,17},{2,18},{3,19},{4,20},{5,21},{6,22},{7,23},{8,24},{9,... | collective-permute-start | bytes 786440 | tf_op jit(solution)/shard_map/ppermute | solution.py:392
  64.1 23.1 %collective-permute-start.2 = (bf16[4,256,128]{2,1,0:T(8,128)(2,1)}, bf16[4,256,128]{2,1,0:T(8,128)(2,1)S(1)}, u32[]{:S(2)}, u32[]{:S(2)}) collective-permute-start(bf16[4,256,128]{2,1,0:T(8,128)(2,1)} %get-tuple-element.36), channel_id=1, source_target_pairs={{0,2},{1,3},{2,0},{3,1},{4,6},{5,7},{6,4},{7,5},{8,10},{9,11},{10,... | collective-permute-start | bytes 786440 | tf_op jit(solution)/shard_map/ppermute | solution.py:392
  65.6 21.6 %collective-permute-start.3 = (bf16[4,256,128]{2,1,0:T(8,128)(2,1)S(1)}, bf16[4,256,128]{2,1,0:T(8,128)(2,1)S(1)}, u32[]{:S(2)}, u32[]{:S(2)}) collective-permute-start(bf16[4,256,128]{2,1,0:T(8,128)(2,1)S(1)} %get-tuple-element.35), channel_id=1, source_target_pairs={{0,18},{1,19},{2,16},{3,17},{4,22},{5,23},{6,20},{7,21},{8,26},{9,... | collective-permute-start | bytes 786440 | tf_op jit(solution)/shard_map/ppermute | solution.py:392
  84.6 17.4 %all-to-all-start.3 = ((bf16[32,8,512]{2,1,0:T(8,128)(2,1)}), bf16[32,8,512]{2,1,0:T(8,128)(2,1)S(1)}, u32[]{:S(2)}, u32[]{:S(2)}) async-start(bf16[32,8,512]{2,1,0:T(8,128)(2,1)} %shard_map.97), calls=%async_computation.3 | async-start | bytes 524288 | tf_op jit(solution)/shard_map/all_to_all | solution.py:25
  87.3 14.6 %copy-start.2 = (f32[256,512]{1,0:T(8,128)S(1)}, f32[256,512]{1,0:T(8,128)}, u32[]{:S(2)}) copy-start(f32[256,512]{1,0:T(8,128)} %get-tuple-element.30) | copy-start | bytes 1572868
  87.3 13.9 %collective-permute-start.4 = (bf16[1,256,128]{2,1,0:T(8,128)(2,1)S(1)}, bf16[1,256,128]{2,1,0:T(8,128)(2,1)S(1)}, u32[]{:S(2)}, u32[]{:S(2)}) collective-permute-start(bf16[1,256,128]{2,1,0:T(8,128)(2,1)S(1)} %get-tuple-element.38), channel_id=1, source_target_pairs={{0,8},{1,9},{2,10},{3,11},{4,12},{5,13},{6,14},{7,15},{8,0},{9,1},... | collective-permute-start | bytes 196616 | tf_op jit(solution)/shard_map/ppermute | solution.py:392
  90.1 11.2 %collective-permute-start.5 = (bf16[1,256,128]{2,1,0:T(8,128)(2,1)S(1)}, bf16[1,256,128]{2,1,0:T(8,128)(2,1)S(1)}, u32[]{:S(2)}, u32[]{:S(2)}) collective-permute-start(bf16[1,256,128]{2,1,0:T(8,128)(2,1)S(1)} %get-tuple-element.40), channel_id=1, source_target_pairs={{0,4},{1,5},{2,6},{3,7},{4,0},{5,1},{6,2},{7,3},{8,12},{9,13},{10,... | collective-permute-start | bytes 196616 | tf_op jit(solution)/shard_map/ppermute | solution.py:392
  91.6 9.6 %collective-permute-start.6 = (bf16[1,256,128]{2,1,0:T(8,128)(2,1)S(1)}, bf16[1,256,128]{2,1,0:T(8,128)(2,1)S(1)}, u32[]{:S(2)}, u32[]{:S(2)}) collective-permute-start(bf16[1,256,128]{2,1,0:T(8,128)(2,1)S(1)} %get-tuple-element.39), channel_id=1, source_target_pairs={{0,12},{1,13},{2,14},{3,15},{4,8},{5,9},{6,10},{7,11},{8,4},{9,5},... | collective-permute-start | bytes 196616 | tf_op jit(solution)/shard_map/ppermute | solution.py:392

commit v5 on v4

--- a/solution.py
+++ b/solution.py
@@ -28,6 +28,7 @@
 VMEM = pl.BlockSpec(memory_space=pltpu.VMEM)
 ANY = pl.BlockSpec(memory_space=pl.ANY)
 FULL_VMEM = 56 * 1024 * 1024
+MOST_VMEM = 50 * 1024 * 1024
 LITTLE_VMEM = 8 * 1024 * 1024
 
 
@@ -35,52 +36,55 @@
     return jax.ShapeDtypeStruct(shape, dtype)
 
 
+def packing(block, width):
+    rows, places = 0, {}
+    for name in ("w_key_t", "w_value_t", "w_query_t"):
+        places[name] = (pl.ds(rows, width), pl.ds(0, width))
+        rows += width
+    for name in ("query", "d_out", "key", "value", "grad_out"):
+        places[name] = (pl.ds(rows, block), pl.ds(0, width))
+        rows += block
+    for pair in (("query_t", "d_out_t"), ("key_t", "value_t"), ("feats_t",)):
+        for position, name in enumerate(pair):
+            places[name] = (pl.ds(rows, width), pl.ds(position * block, block))
+        rows += width
+    return rows, places
+
+
 def project_kernel(
-    feats_ref,
-    grad_out_ref,
-    w_query_ref,
-    w_key_ref,
-    w_value_ref,
-    w_output_ref,
-    query_ref,
-    query_t_ref,
-    d_out_ref,
-    d_out_t_ref,
-    key_ref,
-    key_t_ref,
-    value_ref,
-    value_t_ref,
-    w_query_t_ref,
-    w_key_t_ref,
-    w_value_t_ref,
-    feats_t_ref,
+    feats_ref, grad_out_ref, w_query_ref, w_key_ref, w_value_ref, w_output_ref, packed_ref
 ):
+    block, width = feats_ref.shape
+    _, places = packing(block, width)
+
+    def put(name, value):
+        packed_ref[places[name]] = value.astype(LOW)
+
     feats = feats_ref[...]
-    feats_t_ref[...] = feats.T
-    for w_ref, w_t_ref, plain_ref, turned_ref in (
-        (w_query_ref, w_query_t_ref, query_ref, query_t_ref),
-        (w_key_ref, w_key_t_ref, key_ref, key_t_ref),
-        (w_value_ref, w_value_t_ref, value_ref, value_t_ref),
-    ):
-        w_t = w_ref[...].T
-        w_t_ref[...] = w_t
-        plain_ref[...] = dot(feats, w_ref[...]).astype(LOW)
-        turned_ref[...] = dot_nt(w_t, feats).astype(LOW)
-    d_out_ref[...] = dot_nt(grad_out_ref[...], w_output_ref[...]).astype(LOW)
-    d_out_t_ref[...] = dot_nt(w_output_ref[...], grad_out_ref[...]).astype(LOW)
+    grad_out = grad_out_ref[...]
+    put("feats_t", feats.T)
+    put("grad_out", grad_out)
+    for name, w_ref in (("query", w_query_ref), ("key", w_key_ref), ("value", w_value_ref)):
+        put("w_" + name + "_t", w_ref[...].T)
+        projected = dot(feats, w_ref[...]).astype(LOW)
+        put(name, projected)
+        put(name + "_t", projected.T)
+    d_out = dot_nt(grad_out, w_output_ref[...]).astype(LOW)
+    put("d_out", d_out)
+    put("d_out_t", d_out.T)
 
 
 def project(node_feats, grad_out, *weights):
     block, width = node_feats.shape
-    plain, turned, square = shaped((block, width)), shaped((width, block)), shaped((width, width))
+    rows, _ = packing(block, width)
     return pl.pallas_call(
         project_kernel,
-        out_shape=(plain, turned) * 4 + (square,) * 3 + (turned,),
+        out_shape=shaped((rows, width)),
         in_specs=[VMEM] * 6,
-        out_specs=(VMEM,) * 12,
+        out_specs=VMEM,
         compiler_params=pltpu.CompilerParams(vmem_limit_bytes=FULL_VMEM),
         cost_estimate=pl.CostEstimate(
-            flops=16 * block * width * width,
+            flops=8 * block * width * width,
             bytes_accessed=2 * (10 * block * width + 7 * width * width),
             transcendentals=0,
         ),
@@ -95,26 +99,13 @@
     stages,
     n_inner,
     me_ref,
-    lse_ref,
-    arrived_hbm,
-    query_hbm,
-    query_t_hbm,
-    d_out_hbm,
-    d_out_t_hbm,
-    key_own_hbm,
-    key_own_t_hbm,
-    value_own_hbm,
-    value_own_t_hbm,
-    w_query_t_hbm,
-    w_key_t_hbm,
-    w_value_t_hbm,
-    feats_t_hbm,
-    grad_out_hbm,
+    lse_hbm,
+    arrived_ref,
+    packed_hbm,
     terms_hbm,
     own_hbm,
     keep_hbm,
     send_hbm,
-    arrived_ref,
     query_ref,
     query_t_ref,
     d_out_ref,
@@ -136,6 +127,7 @@
     send_ref,
     prob_ref,
     grad_score_ref,
+    lse_ref,
     in_sem,
     out_sem,
 ):
@@ -163,35 +155,38 @@
         copy.start()
         stores.append(copy)
 
+    _, places = packing(block, width)
+
+    def part(name):
+        return packed_hbm.at[places[name]]
+
+    def far_rows(match):
+        rows = arrived_ref[:, match] if len(arrived_ref.shape) == 4 else arrived_ref[match]
+        return rows.reshape(block, width)
+
     own = pl.ds(0, block)
-    first_needs = [
-        load(by_match(arrived_hbm, 0), arrived_ref.at[0]),
-        load(w_key_t_hbm, w_both_t_ref.at[pl.ds(0, width)]),
-    ]
-    far_needs = [load(by_match(arrived_hbm, match), arrived_ref.at[match]) for match in (1, 2)]
-    value_need = load(w_value_t_hbm, w_both_t_ref.at[pl.ds(width, width)])
+    key_need = load(part("w_key_t"), w_both_t_ref.at[pl.ds(0, width)])
+    value_need = load(part("w_value_t"), w_both_t_ref.at[pl.ds(width, width)])
     head_needs = [
-        load(key_own_hbm, key_ref.at[own]),
-        load(query_t_hbm, query_t_ref),
-        load(value_own_t_hbm, value_t_ref.at[:, own]),
-        load(value_own_hbm, value_ref.at[own]),
-        load(d_out_t_hbm, d_out_t_ref),
-        load(key_own_t_hbm, key_t_ref.at[:, own]),
-        load(query_hbm, query_ref),
-        load(d_out_hbm, d_out_ref),
+        load(lse_hbm, lse_ref),
+        load(part("key"), key_ref.at[own]),
+        load(part("query_t"), query_t_ref),
+        load(part("value_t"), value_t_ref.at[:, own]),
+        load(part("value"), value_ref.at[own]),
+        load(part("d_out_t"), d_out_t_ref),
+        load(part("key_t"), key_t_ref.at[:, own]),
+        load(part("query"), query_ref),
+        load(part("d_out"), d_out_ref),
     ]
     last_needs = [
-        load(feats_t_hbm, feats_t_ref.at[:, own]),
-        load(grad_out_hbm, grad_out_ref),
-        load(w_query_t_hbm, w_query_t_ref),
+        load(part("feats_t"), feats_t_ref.at[:, own]),
+        load(part("grad_out"), grad_out_ref),
+        load(part("w_query_t"), w_query_t_ref),
     ]
-    for copy in first_needs:
-        copy.wait()
+    key_need.wait()
     for match in range(3):
         here = slice((match + 1) * block, (match + 2) * block)
-        if match > 0:
-            far_needs[match - 1].wait()
-        far = arrived_ref[match].reshape(block, width)
+        far = far_rows(match)
         far_key = dot_nt(far, w_both_t_ref[:width]).astype(LOW)
         key_ref[here] = far_key
         key_t_ref[:, here] = far_key.T
@@ -305,9 +300,8 @@
         copy.wait()
 
 
-def attention(me, stages, arrived, projections, grad_out, log_sum_exp):
+def attention(me, stages, arrived, packed, block, width, log_sum_exp):
     n_outer, n_inner = lax.axis_size("gx"), lax.axis_size("gy")
-    block, width = grad_out.shape
     heads = log_sum_exp.shape[0]
     head_size = width // heads
     members = 4 * block
@@ -328,10 +322,9 @@
     terms, own, keep, send = pl.pallas_call(
         functools.partial(attention_kernel, head_size, group, together, 2 * block, stages, n_inner),
         out_shape=(shaped(arrived.shape), shaped((block, width), WIDE), shaped(half), shaped(half)),
-        in_specs=[pl.BlockSpec(memory_space=pltpu.SMEM), VMEM] + [ANY] * 14,
+        in_specs=[pl.BlockSpec(memory_space=pltpu.SMEM), ANY, VMEM, ANY],
         out_specs=(ANY,) * 4,
         scratch_shapes=[
-            pltpu.VMEM(staged, LOW),
             plain,
             turned,
             plain,
@@ -353,16 +346,17 @@
             pltpu.VMEM(half, LOW),
             pltpu.VMEM((members, together * block), LOW),
             pltpu.VMEM((members, together * block), LOW),
-            pltpu.SemaphoreType.DMA((16,)),
+            pltpu.VMEM((heads, block), WIDE),
+            pltpu.SemaphoreType.DMA((17,)),
             pltpu.SemaphoreType.DMA((6,)),
         ],
-        compiler_params=pltpu.CompilerParams(vmem_limit_bytes=FULL_VMEM),
+        compiler_params=pltpu.CompilerParams(vmem_limit_bytes=MOST_VMEM),
         cost_estimate=pl.CostEstimate(
             flops=12 * block * members * width + 32 * members * width * width,
             bytes_accessed=16 * members * width,
             transcendentals=heads * block * members,
         ),
-    )(me.reshape(1), log_sum_exp, arrived, *projections, grad_out)
+    )(me.reshape(1), log_sum_exp, arrived, packed)
     if not whole_tiles:
         terms = terms.reshape(3, devices, piece, width).transpose(1, 0, 2, 3)
     return terms, own, keep, send
@@ -435,8 +429,8 @@
 
     spread = exchange(node_feats.reshape(devices, piece, width))
     arrived = exchange(spread[partners])
-    projections = project(node_feats, grad_out, w_query, w_key, w_value, w_output)
-    terms, own, keep, send = attention(me, stages, arrived, projections, grad_out, log_sum_exp)
+    packed = project(node_feats, grad_out, w_query, w_key, w_value, w_output)
+    terms, own, keep, send = attention(me, stages, arrived, packed, block, width, log_sum_exp)
     returned = exchange(terms)
     got = [swap(send, 1, devices)]
     summed = None

time: 103 us -> 102 us (level)
  other arithmetic: 2.7 us -> 5.22 us
  waiting for transfers between devices: 54 us -> 51.7 us
    all_to_all x4, waiting for transfers between devices: 44.4 us -> 42.9 us  [exchange(): return lax.all_to_all(pieces, AXES, split_axis=0, concat_axis=0, tiled=True)]
  transfers between devices with their start and end apart: 11 -> 11, of which waited for: 5 -> 5; matrix products, arithmetic and copies ran while one was open for 2% -> 5% of each run, Pallas kernels for 5% -> 6%
where the time goes in v5:
time: 102 us
  waiting for transfers between devices  51.7 us (51%)
  starting transfers between devices  23.3 us (23%)
  Pallas kernels  19 us (19%)
  other arithmetic  5.22 us (5%)
  local copies, waits for them, and re-layouts  1.82 us (2%)
    all_to_all x4, waiting for transfers between devices, exchange(): return lax.all_to_all(pieces, AXES, split_axis=0, concat_axis=0, tiled=True)  42.9 us
    all_to_all x4, starting transfers between devices, exchange(): return lax.all_to_all(pieces, AXES, split_axis=0, concat_axis=0, tiled=True)  15.3 us
    pallas_call x1, Pallas kernels, attention(): pl.pallas_call(functools.partial(attention_kernel, head_size, group, toge...  12.7 us
    ppermute x7, waiting for transfers between devices, swap(): lax.ppermute(value, AXES, [(device, device ^ mask) for device in range(de...  8.77 us
    ppermute x7, starting transfers between devices, swap(): lax.ppermute(value, AXES, [(device, device ^ mask) for device in range(de...  8.01 us
    pallas_call x1, Pallas kernels, project(): pl.pallas_call(project_kernel, out_shape=shaped((rows, width)), in_specs=...  4.6 us
    convert_element_type x2, other arithmetic, on_device(): add_up(keep[index], *(each[index] for each in got)).astype(LOW)  2.2 us
  transfers between devices with their start and end apart: 11, of which 5 were waited for; matrix products, arithmetic and copies ran while one was open for 5% of the time, Pallas kernels for 6%

profile of v5, /device:TPU:0, one launch (start us, length us, event | category | flops | bytes accessed | tf_op | source)
XLA Modules:
  0.0 101.7 jit_solution(3621933101152263980)
XLA Ops:
  0.6 7.3 %all-to-all-start = ((bf16[32,8,512]{2,1,0:T(8,128)(2,1)}), bf16[32,8,512]{2,1,0:T(8,128)(2,1)S(1)}, u32[]{:S(2)}, u32[]{:S(2)}) async-start(bf16[32,8,512]{2,1,0:T(8,128)(2,1)} %bitcast.8), calls=%async_computation | async-start | bytes 524288 | tf_op jit(solution)/shard_map/all_to_all | solution.py:25
  7.9 0.7 compare_select_fusion
  8.6 0.1 copy.12
  8.7 0.1 reshape.121
  8.8 9.4 %all-to-all-done = bf16[32,8,512]{2,1,0:T(8,128)(2,1)S(1)} async-done(((bf16[32,8,512]{2,1,0:T(8,128)(2,1)}), bf16[32,8,512]{2,1,0:T(8,128)(2,1)S(1)}, u32[]{:S(2)}, u32[]{:S(2)}) %all-to-all-start) | async-done | bytes 262176 | tf_op jit(solution)/shard_map/all_to_all | solution.py:25
  18.2 1.5 %gather_fusion = bf16[96,8,512]{2,1,0:T(8,128)(2,1)} fusion(bf16[32,8,512]{2,1,0:T(8,128)(2,1)S(1)} %all-to-all-done, s32[1024]{0:T(1024)S(1)} %pad_clamp_fusion), kind=kCustom, calls=%fused_computation | custom fusion | bytes 1573248 | tf_op jit(solution)/shard_map/gather | solution.py:431
  19.8 0.0 copy-start
  19.8 2.8 %all-to-all-start.1 = ((bf16[32,3,8,512]{3,2,1,0:T(8,128)(2,1)}), bf16[32,3,8,512]{3,2,1,0:T(8,128)(2,1)S(1)}, u32[]{:S(2)}, u32[]{:S(2)}) async-start(bf16[32,3,8,512]{3,2,1,0:T(8,128)(2,1)} %bitcast.2), calls=%async_computation.1 | async-start | bytes 1572864 | tf_op jit(solution)/shard_map/all_to_all | solution.py:25
  22.5 4.6 %shard_map.95.packed_hbm = bf16[4352,512]{1,0:T(8,128)(2,1)} custom-call(bf16[256,512]{1,0:T(8,128)(2,1)} %feats_ref.1, bf16[256,512]{1,0:T(8,128)(2,1)} %grad_out_ref.1, bf16[512,512]{1,0:T(8,128)(2,1)} %w_query_ref.1, bf16[512,512]{1,0:T(8,128)(2,1)} %w_key_ref.1, bf16[512,512]{1,0:T(8,128)(2,1)} %w_value_ref.1, bf16[512,512]{1,0:T(8,128)(2,1)} %w_output_ref.1), custom_call_target="tpu_custom_call" | custom-call | flops 536870912 | bytes 6291456 | tf_op jit(solution)/shard_map/pallas_call | solution.py:80
  27.1 16.9 %all-to-all-done.1.arrived_ref = bf16[32,3,8,512]{3,2,1,0:T(8,128)(2,1)S(1)} async-done(((bf16[32,3,8,512]{3,2,1,0:T(8,128)(2,1)}), bf16[32,3,8,512]{3,2,1,0:T(8,128)(2,1)S(1)}, u32[]{:S(2)}, u32[]{:S(2)}) %all-to-all-start.1) | async-done | bytes 786464 | tf_op jit(solution)/shard_map/all_to_all | solution.py:25
  44.0 0.0 copy-done
  44.0 12.7 %shard_map.96 = (bf16[32,3,8,512]{3,2,1,0:T(8,128)(2,1)}, f32[256,512]{1,0:T(8,128)S(1)}, bf16[16,256,128]{2,1,0:T(8,128)(2,1)S(1)}, bf16[16,256,128]{2,1,0:T(8,128)(2,1)}) custom-call(s32[1]{0:T(128)} %bitcast.me_ref, f32[8,256]{1,0:T(8,128)S(1)} %copy-done, bf16[32,3,8,512]{3,2,1,0:T(8,128)(2,1)S(1)} %all-to-all-done.1.arrived_ref, ...), custom_call_target="tpu_custom_call" | custom-call | flops 10200547328 | bytes 8388608 | tf_op jit(solution)/shard_map/pallas_call | solution.py:322
  56.8 0.0 copy-start.1
  56.8 0.1 collective-permute-start
  56.9 2.6 %all-to-all-start.2 = ((bf16[32,3,8,512]{3,2,1,0:T(8,128)(2,1)}), bf16[32,3,8,512]{3,2,1,0:T(8,128)(2,1)S(1)}, u32[]{:S(2)}, u32[]{:S(2)}) async-start(bf16[32,3,8,512]{3,2,1,0:T(8,128)(2,1)} %get-tuple-element.7), calls=%async_computation.2 | async-start | bytes 1572864 | tf_op jit(solution)/shard_map/all_to_all | solution.py:25
  59.5 0.2 collective-permute-done
  59.7 1.2 %add_convert_fusion.3 = (bf16[4,256,128]{2,1,0:T(8,128)(2,1)}, bf16[4,256,128]{2,1,0:T(8,128)(2,1)}, bf16[4,256,128]{2,1,0:T(8,128)(2,1)}, bf16[4,256,128]{2,1,0:T(8,128)(2,1)}) fusion(bf16[16,256,128]{2,1,0:T(8,128)(2,1)S(1)} %collective-permute-done, bf16[16,256,128]{2,1,0:T(8,128)(2,1)S(1)} %get-tuple-element.8), kind=kLoop, calls=%fused_computation.6 | loop fusion | flops 2097152 | bytes 3145728 | tf_op jit(solution)/shard_map/convert_element_type | solution.py:442
  60.9 1.4 %collective-permute-start.1 = (bf16[4,256,128]{2,1,0:T(8,128)(2,1)}, bf16[4,256,128]{2,1,0:T(8,128)(2,1)S(1)}, u32[]{:S(2)}, u32[]{:S(2)}) collective-permute-start(bf16[4,256,128]{2,1,0:T(8,128)(2,1)} %get-tuple-element.13), channel_id=1, source_target_pairs={{0,16},{1,17},{2,18},{3,19},{4,20},{5,21},{6,22},{7,23},{8,24},{9,... | collective-permute-start | bytes 786440 | tf_op jit(solution)/shard_map/ppermute | solution.py:386
  62.4 1.5 %collective-permute-start.2 = (bf16[4,256,128]{2,1,0:T(8,128)(2,1)}, bf16[4,256,128]{2,1,0:T(8,128)(2,1)S(1)}, u32[]{:S(2)}, u32[]{:S(2)}) collective-permute-start(bf16[4,256,128]{2,1,0:T(8,128)(2,1)} %get-tuple-element.12), channel_id=1, source_target_pairs={{0,2},{1,3},{2,0},{3,1},{4,6},{5,7},{6,4},{7,5},{8,10},{9,11},{10,... | collective-permute-start | bytes 786440 | tf_op jit(solution)/shard_map/ppermute | solution.py:386
  63.9 0.6 collective-permute-start.3
  64.4 0.0 copy-done.1
  64.4 0.1 copy.13.partners_ref
  64.5 16.6 %all-to-all-done.2.returned_ref = bf16[32,3,8,512]{3,2,1,0:T(8,128)(2,1)S(1)} async-done(((bf16[32,3,8,512]{3,2,1,0:T(8,128)(2,1)}), bf16[32,3,8,512]{3,2,1,0:T(8,128)(2,1)S(1)}, u32[]{:S(2)}, u32[]{:S(2)}) %all-to-all-start.2) | async-done | bytes 786464 | tf_op jit(solution)/shard_map/all_to_all | solution.py:25
  81.1 1.6 %shard_map.97 = bf16[32,8,512]{2,1,0:T(8,128)(2,1)} custom-call(s32[32,3]{1,0:T(8,128)S(1)} %copy.13.partners_ref, bf16[32,3,8,512]{3,2,1,0:T(8,128)(2,1)S(1)} %all-to-all-done.2.returned_ref), custom_call_target="tpu_custom_call" | custom-call | tf_op jit(solution)/shard_map/pallas_call | solution.py:413
  82.8 2.6 %all-to-all-start.3 = ((bf16[32,8,512]{2,1,0:T(8,128)(2,1)}), bf16[32,8,512]{2,1,0:T(8,128)(2,1)S(1)}, u32[]{:S(2)}, u32[]{:S(2)}) async-start(bf16[32,8,512]{2,1,0:T(8,128)(2,1)} %shard_map.97), calls=%async_computation.3 | async-start | bytes 524288 | tf_op jit(solution)/shard_map/all_to_all | solution.py:25
  85.3 0.0 collective-permute-done.1
  85.4 0.0 collective-permute-done.2
  85.4 0.0 collective-permute-done.3
  85.4 1.0 add_convert_fusion.6
  86.4 2.7 %collective-permute-start.4 = (bf16[1,256,128]{2,1,0:T(8,128)(2,1)S(1)}, bf16[1,256,128]{2,1,0:T(8,128)(2,1)S(1)}, u32[]{:S(2)}, u32[]{:S(2)}) collective-permute-start(bf16[1,256,128]{2,1,0:T(8,128)(2,1)S(1)} %get-tuple-element.14), channel_id=1, source_target_pairs={{0,8},{1,9},{2,10},{3,11},{4,12},{5,13},{6,14},{7,15},{8,0},{9,1},... | collective-permute-start | bytes 196616 | tf_op jit(solution)/shard_map/ppermute | solution.py:386
  89.1 1.5 %collective-permute-start.5 = (bf16[1,256,128]{2,1,0:T(8,128)(2,1)S(1)}, bf16[1,256,128]{2,1,0:T(8,128)(2,1)S(1)}, u32[]{:S(2)}, u32[]{:S(2)}) collective-permute-start(bf16[1,256,128]{2,1,0:T(8,128)(2,1)S(1)} %get-tuple-element.16), channel_id=1, source_target_pairs={{0,4},{1,5},{2,6},{3,7},{4,0},{5,1},{6,2},{7,3},{8,12},{9,13},{10,... | collective-permute-start | bytes 196616 | tf_op jit(solution)/shard_map/ppermute | solution.py:386
  90.6 0.2 collective-permute-start.6
  90.8 8.5 %collective-permute-done.4 = bf16[1,256,128]{2,1,0:T(8,128)(2,1)S(1)} collective-permute-done((bf16[1,256,128]{2,1,0:T(8,128)(2,1)S(1)}, bf16[1,256,128]{2,1,0:T(8,128)(2,1)S(1)}, u32[]{:S(2)}, u32[]{:S(2)}) %collective-permute-start.4) | collective-permute-done | bytes 65568 | tf_op jit(solution)/shard_map/ppermute | solution.py:386
  99.4 0.0 collective-permute-done.5
  99.4 0.0 collective-permute-done.6
  99.4 1.6 %add_bitcast_fusion = f32[256,128]{1,0:T(8,128)} fusion(bf16[1,256,128]{2,1,0:T(8,128)(2,1)S(1)} %collective-permute-done.6, bf16[1,256,128]{2,1,0:T(8,128)(2,1)S(1)} %collective-permute-done.5, bf16[1,256,128]{2,1,0:T(8,128)(2,1)S(1)} %collective-permute-done.4, bf16[4,256,128]{2,1,0:T(8,128)(2,1)S(1)} %collective-permute-done.3, ...), kind=kLoop, calls=%fused_computation.7 | loop fusion | flops 491520 | bytes 589824 | tf_op jit(solution)/shard_map/squeeze | solution.py:449
  101.0 0.0 all-to-all-done.3
  101.0 0.8 fusion
  (1 shorter events, 0.0 us)
Async XLA Ops:
  0.6 17.6 %all-to-all-start = ((bf16[32,8,512]{2,1,0:T(8,128)(2,1)}), bf16[32,8,512]{2,1,0:T(8,128)(2,1)S(1)}, u32[]{:S(2)}, u32[]{:S(2)}) async-start(bf16[32,8,512]{2,1,0:T(8,128)(2,1)} %bitcast.8), calls=%async_computation | async-start | bytes 524288 | tf_op jit(solution)/shard_map/all_to_all | solution.py:25
  19.8 24.3 %copy-start = (f32[8,256]{1,0:T(8,128)S(1)}, f32[8,256]{1,0:T(8,128)}, u32[]{:S(2)}) copy-start(f32[8,256]{1,0:T(8,128)} %lse_hbm.1) | copy-start | bytes 24580
  19.8 24.3 %all-to-all-start.1 = ((bf16[32,3,8,512]{3,2,1,0:T(8,128)(2,1)}), bf16[32,3,8,512]{3,2,1,0:T(8,128)(2,1)S(1)}, u32[]{:S(2)}, u32[]{:S(2)}) async-start(bf16[32,3,8,512]{3,2,1,0:T(8,128)(2,1)} %bitcast.2), calls=%async_computation.1 | async-start | bytes 1572864 | tf_op jit(solution)/shard_map/all_to_all | solution.py:25
  56.8 7.6 %copy-start.1 = (s32[32,3]{0,1:T(4,128)S(1)}, s32[32,3]{0,1:T(4,128)}, u32[]{:S(2)}) copy-start(s32[32,3]{0,1:T(4,128)} %param.15) | copy-start | bytes 1156
  56.8 2.9 %collective-permute-start = (bf16[16,256,128]{2,1,0:T(8,128)(2,1)}, bf16[16,256,128]{2,1,0:T(8,128)(2,1)S(1)}, u32[]{:S(2)}, u32[]{:S(2)}) collective-permute-start(bf16[16,256,128]{2,1,0:T(8,128)(2,1)} %get-tuple-element.9), channel_id=1, source_target_pairs={{0,1},{1,0},{2,3},{3,2},{4,5},{5,4},{6,7},{7,6},{8,9},{9,8},{10,11... | collective-permute-start | bytes 3145736 | tf_op jit(solution)/shard_map/ppermute | solution.py:386
  56.9 24.3 %all-to-all-start.2 = ((bf16[32,3,8,512]{3,2,1,0:T(8,128)(2,1)}), bf16[32,3,8,512]{3,2,1,0:T(8,128)(2,1)S(1)}, u32[]{:S(2)}, u32[]{:S(2)}) async-start(bf16[32,3,8,512]{3,2,1,0:T(8,128)(2,1)} %get-tuple-element.7), calls=%async_computation.2 | async-start | bytes 1572864 | tf_op jit(solution)/shard_map/all_to_all | solution.py:25
  60.9 24.4 %collective-permute-start.1 = (bf16[4,256,128]{2,1,0:T(8,128)(2,1)}, bf16[4,256,128]{2,1,0:T(8,128)(2,1)S(1)}, u32[]{:S(2)}, u32[]{:S(2)}) collective-permute-start(bf16[4,256,128]{2,1,0:T(8,128)(2,1)} %get-tuple-element.13), channel_id=1, source_target_pairs={{0,16},{1,17},{2,18},{3,19},{4,20},{5,21},{6,22},{7,23},{8,24},{9,... | collective-permute-start | bytes 786440 | tf_op jit(solution)/shard_map/ppermute | solution.py:386
  62.4 23.0 %collective-permute-start.2 = (bf16[4,256,128]{2,1,0:T(8,128)(2,1)}, bf16[4,256,128]{2,1,0:T(8,128)(2,1)S(1)}, u32[]{:S(2)}, u32[]{:S(2)}) collective-permute-start(bf16[4,256,128]{2,1,0:T(8,128)(2,1)} %get-tuple-element.12), channel_id=1, source_target_pairs={{0,2},{1,3},{2,0},{3,1},{4,6},{5,7},{6,4},{7,5},{8,10},{9,11},{10,... | collective-permute-start | bytes 786440 | tf_op jit(solution)/shard_map/ppermute | solution.py:386
  63.9 21.5 %collective-permute-start.3 = (bf16[4,256,128]{2,1,0:T(8,128)(2,1)}, bf16[4,256,128]{2,1,0:T(8,128)(2,1)S(1)}, u32[]{:S(2)}, u32[]{:S(2)}) collective-permute-start(bf16[4,256,128]{2,1,0:T(8,128)(2,1)} %get-tuple-element.11), channel_id=1, source_target_pairs={{0,18},{1,19},{2,16},{3,17},{4,22},{5,23},{6,20},{7,21},{8,26},{9,... | collective-permute-start | bytes 786440 | tf_op jit(solution)/shard_map/ppermute | solution.py:386
  82.8 18.2 %all-to-all-start.3 = ((bf16[32,8,512]{2,1,0:T(8,128)(2,1)}), bf16[32,8,512]{2,1,0:T(8,128)(2,1)S(1)}, u32[]{:S(2)}, u32[]{:S(2)}) async-start(bf16[32,8,512]{2,1,0:T(8,128)(2,1)} %shard_map.97), calls=%async_computation.3 | async-start | bytes 524288 | tf_op jit(solution)/shard_map/all_to_all | solution.py:25
  86.4 13.0 %collective-permute-start.4 = (bf16[1,256,128]{2,1,0:T(8,128)(2,1)S(1)}, bf16[1,256,128]{2,1,0:T(8,128)(2,1)S(1)}, u32[]{:S(2)}, u32[]{:S(2)}) collective-permute-start(bf16[1,256,128]{2,1,0:T(8,128)(2,1)S(1)} %get-tuple-element.14), channel_id=1, source_target_pairs={{0,8},{1,9},{2,10},{3,11},{4,12},{5,13},{6,14},{7,15},{8,0},{9,1},... | collective-permute-start | bytes 196616 | tf_op jit(solution)/shard_map/ppermute | solution.py:386
  89.1 10.3 %collective-permute-start.5 = (bf16[1,256,128]{2,1,0:T(8,128)(2,1)S(1)}, bf16[1,256,128]{2,1,0:T(8,128)(2,1)S(1)}, u32[]{:S(2)}, u32[]{:S(2)}) collective-permute-start(bf16[1,256,128]{2,1,0:T(8,128)(2,1)S(1)} %get-tuple-element.16), channel_id=1, source_target_pairs={{0,4},{1,5},{2,6},{3,7},{4,0},{5,1},{6,2},{7,3},{8,12},{9,13},{10,... | collective-permute-start | bytes 196616 | tf_op jit(solution)/shard_map/ppermute | solution.py:386
  90.6 8.8 %collective-permute-start.6 = (bf16[1,256,128]{2,1,0:T(8,128)(2,1)S(1)}, bf16[1,256,128]{2,1,0:T(8,128)(2,1)S(1)}, u32[]{:S(2)}, u32[]{:S(2)}) collective-permute-start(bf16[1,256,128]{2,1,0:T(8,128)(2,1)S(1)} %get-tuple-element.15), channel_id=1, source_target_pairs={{0,12},{1,13},{2,14},{3,15},{4,8},{5,9},{6,10},{7,11},{8,4},{9,5},... | collective-permute-start | bytes 196616 | tf_op jit(solution)/shard_map/ppermute | solution.py:386

commit v6 on v5

--- a/solution.py
+++ b/solution.py
@@ -419,6 +419,24 @@
     )(partners, returned)
 
 
+def finish_kernel(own_ref, back_ref, keep_ref, *refs):
+    *got_refs, nodes_ref, weights_ref = refs
+    back = back_ref[...].reshape(own_ref.shape)
+    nodes_ref[...] = (own_ref[...] + back.astype(WIDE)).astype(LOW)
+    weights_ref[...] = add_up(keep_ref[0], *(each[0] for each in got_refs))
+
+
+def finish(own, back, keep, got):
+    _, tall, wide = keep.shape
+    return pl.pallas_call(
+        finish_kernel,
+        out_shape=(shaped(own.shape), shaped((tall, wide), WIDE)),
+        in_specs=[VMEM] * (3 + len(got)),
+        out_specs=(VMEM, VMEM),
+        compiler_params=pltpu.CompilerParams(vmem_limit_bytes=LITTLE_VMEM),
+    )(own, back, keep, *got)
+
+
 def on_device(node_feats, grad_out, log_sum_exp, w_query, w_key, w_value, w_output, partners):
     block, width = node_feats.shape
     n_outer, n_inner = lax.axis_size("gx"), lax.axis_size("gy")
@@ -433,20 +451,21 @@
     terms, own, keep, send = attention(me, stages, arrived, packed, block, width, log_sum_exp)
     returned = exchange(terms)
     got = [swap(send, 1, devices)]
-    summed = None
+    summed = collect_pieces(returned, partners)
     for number, masks in enumerate(stages):
         count = 2 ** len(masks)
+        if number == 1:
+            keep, _ = lax.optimization_barrier((keep, summed))
         keep = keep.reshape((count, -1) + keep.shape[1:])
         got = [each.reshape(keep.shape) for each in got]
         parts = [
             add_up(keep[index], *(each[index] for each in got)).astype(LOW) for index in range(count)
         ]
-        if number == len(stages) - 1:
-            summed = collect_pieces(returned, partners)
         keep, got = stage_sum(parts, masks, devices)
-    back = exchange(summed).reshape(block, width)
-    grad_nodes = (own + back.astype(WIDE)).astype(LOW)
-    weight_grads = add_up(keep, *got)[0]
+    back = exchange(summed)
+    if piece % 8:
+        back = back.reshape(block, width)
+    grad_nodes, weight_grads = finish(own, back, keep, got)
     return grad_nodes, weight_grads
 
 

time: 102 us -> 101 us (level)
  other arithmetic: 5.22 us -> 1.13 us
  waiting for transfers between devices: 51.7 us -> 53.2 us
    ppermute x7, waiting for transfers between devices: 8.77 us -> 12.2 us  [swap(): lax.ppermute(value, AXES, [(device, device ^ mask) for device in range(de...]
    all_to_all x4, waiting for transfers between devices: 42.9 us -> 41 us  [exchange(): return lax.all_to_all(pieces, AXES, split_axis=0, concat_axis=0, tiled=True)]
    convert_element_type x2, other arithmetic: 2.2 us -> 0.44 us  [on_device(): add_up(keep[index], *(each[index] for each in got)).astype(LOW)]
    squeeze x1 -> x0, other arithmetic: 1.56 us -> none  [on_device(): weight_grads = add_up(keep, *got)[0]]
  transfers between devices with their start and end apart: 11 -> 11, of which waited for: 5 -> 5; matrix products, arithmetic and copies ran while one was open for 5% -> 1% of each run, Pallas kernels for 6% -> 6%
where the time goes in v6:
time: 101 us; the launch traced here: 100 us
  waiting for transfers between devices  53.2 us (53%)
  starting transfers between devices  23.5 us (23%)
  Pallas kernels  19.8 us (20%)
  local copies, waits for them, and re-layouts  1.82 us (2%)
  other arithmetic  1.13 us (1%)
    all_to_all x4, waiting for transfers between devices, exchange(): return lax.all_to_all(pieces, AXES, split_axis=0, concat_axis=0, tiled=True)  41 us
    all_to_all x4, starting transfers between devices, exchange(): return lax.all_to_all(pieces, AXES, split_axis=0, concat_axis=0, tiled=True)  15.3 us
    pallas_call x1, Pallas kernels, attention(): pl.pallas_call(functools.partial(attention_kernel, head_size, group, toge...  12.8 us
    ppermute x7, waiting for transfers between devices, swap(): lax.ppermute(value, AXES, [(device, device ^ mask) for device in range(de...  12.2 us
    ppermute x7, starting transfers between devices, swap(): lax.ppermute(value, AXES, [(device, device ^ mask) for device in range(de...  8.18 us
    pallas_call x1, Pallas kernels, project(): pl.pallas_call(project_kernel, out_shape=shaped((rows, width)), in_specs=...  4.6 us
  transfers between devices with their start and end apart: 11, of which 5 were waited for; matrix products, arithmetic and copies ran while one was open for 1% of the time, Pallas kernels for 6%

profile of v6, /device:TPU:0, one launch (start us, length us, event | category | flops | bytes accessed | tf_op | source)
XLA Modules:
  0.0 100.1 jit_solution(6377094594319857079)
XLA Ops:
  0.6 7.3 %all-to-all-start = ((bf16[32,8,512]{2,1,0:T(8,128)(2,1)}), bf16[32,8,512]{2,1,0:T(8,128)(2,1)S(1)}, u32[]{:S(2)}, u32[]{:S(2)}) async-start(bf16[32,8,512]{2,1,0:T(8,128)(2,1)} %bitcast.3), calls=%async_computation | async-start | bytes 524288 | tf_op jit(solution)/shard_map/all_to_all | solution.py:25
  7.9 0.7 compare_select_fusion
  8.6 0.1 copy.12
  8.7 0.1 reshape.116
  8.8 9.4 %all-to-all-done = bf16[32,8,512]{2,1,0:T(8,128)(2,1)S(1)} async-done(((bf16[32,8,512]{2,1,0:T(8,128)(2,1)}), bf16[32,8,512]{2,1,0:T(8,128)(2,1)S(1)}, u32[]{:S(2)}, u32[]{:S(2)}) %all-to-all-start) | async-done | bytes 262176 | tf_op jit(solution)/shard_map/all_to_all | solution.py:25
  18.2 1.5 %gather_fusion = bf16[96,8,512]{2,1,0:T(8,128)(2,1)} fusion(bf16[32,8,512]{2,1,0:T(8,128)(2,1)S(1)} %all-to-all-done, s32[1024]{0:T(1024)S(1)} %pad_clamp_fusion), kind=kCustom, calls=%fused_computation | custom fusion | bytes 1573248 | tf_op jit(solution)/shard_map/gather | solution.py:449
  19.8 0.0 copy-start
  19.8 2.8 %all-to-all-start.1 = ((bf16[32,3,8,512]{3,2,1,0:T(8,128)(2,1)}), bf16[32,3,8,512]{3,2,1,0:T(8,128)(2,1)S(1)}, u32[]{:S(2)}, u32[]{:S(2)}) async-start(bf16[32,3,8,512]{3,2,1,0:T(8,128)(2,1)} %bitcast.2), calls=%async_computation.1 | async-start | bytes 1572864 | tf_op jit(solution)/shard_map/all_to_all | solution.py:25
  22.5 4.6 %shard_map.95.packed_hbm = bf16[4352,512]{1,0:T(8,128)(2,1)} custom-call(bf16[256,512]{1,0:T(8,128)(2,1)} %feats_ref.1, bf16[256,512]{1,0:T(8,128)(2,1)} %grad_out_ref.1, bf16[512,512]{1,0:T(8,128)(2,1)} %w_query_ref.1, bf16[512,512]{1,0:T(8,128)(2,1)} %w_key_ref.1, bf16[512,512]{1,0:T(8,128)(2,1)} %w_value_ref.1, bf16[512,512]{1,0:T(8,128)(2,1)} %w_output_ref.1), custom_call_target="tpu_custom_call" | custom-call | flops 536870912 | bytes 6291456 | tf_op jit(solution)/shard_map/pallas_call | solution.py:80
  27.1 16.9 %all-to-all-done.1.arrived_ref = bf16[32,3,8,512]{3,2,1,0:T(8,128)(2,1)S(1)} async-done(((bf16[32,3,8,512]{3,2,1,0:T(8,128)(2,1)}), bf16[32,3,8,512]{3,2,1,0:T(8,128)(2,1)S(1)}, u32[]{:S(2)}, u32[]{:S(2)}) %all-to-all-start.1) | async-done | bytes 786464 | tf_op jit(solution)/shard_map/all_to_all | solution.py:25
  44.0 0.0 copy-done
  44.0 12.8 %shard_map.96 = (bf16[32,3,8,512]{3,2,1,0:T(8,128)(2,1)}, f32[256,512]{1,0:T(8,128)S(1)}, bf16[16,256,128]{2,1,0:T(8,128)(2,1)S(1)}, bf16[16,256,128]{2,1,0:T(8,128)(2,1)}) custom-call(s32[1]{0:T(128)} %bitcast.me_ref, f32[8,256]{1,0:T(8,128)S(1)} %copy-done, bf16[32,3,8,512]{3,2,1,0:T(8,128)(2,1)S(1)} %all-to-all-done.1.arrived_ref, ...), custom_call_target="tpu_custom_call" | custom-call | flops 10200547328 | bytes 8388608 | tf_op jit(solution)/shard_map/pallas_call | solution.py:322
  56.8 0.0 copy-start.1
  56.8 2.6 %all-to-all-start.2 = ((bf16[32,3,8,512]{3,2,1,0:T(8,128)(2,1)}), bf16[32,3,8,512]{3,2,1,0:T(8,128)(2,1)S(1)}, u32[]{:S(2)}, u32[]{:S(2)}) async-start(bf16[32,3,8,512]{3,2,1,0:T(8,128)(2,1)} %get-tuple-element.8), calls=%async_computation.2 | async-start | bytes 1572864 | tf_op jit(solution)/shard_map/all_to_all | solution.py:25
  59.5 0.2 collective-permute-start
  59.6 2.8 %collective-permute-done = bf16[16,256,128]{2,1,0:T(8,128)(2,1)S(1)} collective-permute-done((bf16[16,256,128]{2,1,0:T(8,128)(2,1)}, bf16[16,256,128]{2,1,0:T(8,128)(2,1)S(1)}, u32[]{:S(2)}, u32[]{:S(2)}) %collective-permute-start) | collective-permute-done | bytes 1048608 | tf_op jit(solution)/shard_map/ppermute | solution.py:386
  62.4 0.3 add_convert_fusion.3
  62.7 1.7 %collective-permute-start.1 = (bf16[4,256,128]{2,1,0:T(8,128)(2,1)S(1)}, bf16[4,256,128]{2,1,0:T(8,128)(2,1)S(1)}, u32[]{:S(2)}, u32[]{:S(2)}) collective-permute-start(bf16[4,256,128]{2,1,0:T(8,128)(2,1)S(1)} %get-tuple-element.15), channel_id=1, source_target_pairs={{0,16},{1,17},{2,18},{3,19},{4,20},{5,21},{6,22},{7,23},{8,24},{9,... | collective-permute-start | bytes 786440 | tf_op jit(solution)/shard_map/ppermute | solution.py:386
  64.4 1.5 %collective-permute-start.2 = (bf16[4,256,128]{2,1,0:T(8,128)(2,1)S(1)}, bf16[4,256,128]{2,1,0:T(8,128)(2,1)S(1)}, u32[]{:S(2)}, u32[]{:S(2)}) collective-permute-start(bf16[4,256,128]{2,1,0:T(8,128)(2,1)S(1)} %get-tuple-element.14), channel_id=1, source_target_pairs={{0,2},{1,3},{2,0},{3,1},{4,6},{5,7},{6,4},{7,5},{8,10},{9,11},{10,... | collective-permute-start | bytes 786440 | tf_op jit(solution)/shard_map/ppermute | solution.py:386
  65.9 0.4 collective-permute-start.3
  66.3 0.0 copy-done.1
  66.3 0.1 copy.13.partners_ref
  66.3 14.7 %all-to-all-done.2.returned_ref = bf16[32,3,8,512]{3,2,1,0:T(8,128)(2,1)S(1)} async-done(((bf16[32,3,8,512]{3,2,1,0:T(8,128)(2,1)}), bf16[32,3,8,512]{3,2,1,0:T(8,128)(2,1)S(1)}, u32[]{:S(2)}, u32[]{:S(2)}) %all-to-all-start.2) | async-done | bytes 786464 | tf_op jit(solution)/shard_map/all_to_all | solution.py:25
  81.1 1.6 %shard_map.97 = bf16[32,8,512]{2,1,0:T(8,128)(2,1)} custom-call(s32[32,3]{1,0:T(8,128)S(1)} %copy.13.partners_ref, bf16[32,3,8,512]{3,2,1,0:T(8,128)(2,1)S(1)} %all-to-all-done.2.returned_ref), custom_call_target="tpu_custom_call" | custom-call | tf_op jit(solution)/shard_map/pallas_call | solution.py:413
  82.7 2.6 %all-to-all-start.3 = ((bf16[32,8,512]{2,1,0:T(8,128)(2,1)}), bf16[32,8,512]{2,1,0:T(8,128)(2,1)S(1)}, u32[]{:S(2)}, u32[]{:S(2)}) async-start(bf16[32,8,512]{2,1,0:T(8,128)(2,1)} %shard_map.97), calls=%async_computation.3 | async-start | bytes 524288 | tf_op jit(solution)/shard_map/all_to_all | solution.py:25
  85.3 0.0 collective-permute-done.1
  85.3 0.0 collective-permute-done.2
  85.3 0.0 collective-permute-done.3
  85.3 0.1 add_convert_fusion.4
  85.5 2.7 %collective-permute-start.4 = (bf16[1,256,128]{2,1,0:T(8,128)(2,1)S(1)}, bf16[1,256,128]{2,1,0:T(8,128)(2,1)S(1)}, u32[]{:S(2)}, u32[]{:S(2)}) collective-permute-start(bf16[1,256,128]{2,1,0:T(8,128)(2,1)S(1)} %get-tuple-element.18), channel_id=1, source_target_pairs={{0,8},{1,9},{2,10},{3,11},{4,12},{5,13},{6,14},{7,15},{8,0},{9,1},... | collective-permute-start | bytes 196616 | tf_op jit(solution)/shard_map/ppermute | solution.py:386
  88.2 1.5 %collective-permute-start.5 = (bf16[1,256,128]{2,1,0:T(8,128)(2,1)S(1)}, bf16[1,256,128]{2,1,0:T(8,128)(2,1)S(1)}, u32[]{:S(2)}, u32[]{:S(2)}) collective-permute-start(bf16[1,256,128]{2,1,0:T(8,128)(2,1)S(1)} %get-tuple-element.17), channel_id=1, source_target_pairs={{0,4},{1,5},{2,6},{3,7},{4,0},{5,1},{6,2},{7,3},{8,12},{9,13},{10,... | collective-permute-start | bytes 196616 | tf_op jit(solution)/shard_map/ppermute | solution.py:386
  89.7 0.2 collective-permute-start.6
  89.9 9.4 %collective-permute-done.4.refs_0_ = bf16[1,256,128]{2,1,0:T(8,128)(2,1)S(1)} collective-permute-done((bf16[1,256,128]{2,1,0:T(8,128)(2,1)S(1)}, bf16[1,256,128]{2,1,0:T(8,128)(2,1)S(1)}, u32[]{:S(2)}, u32[]{:S(2)}) %collective-permute-start.4) | collective-permute-done | bytes 65568 | tf_op jit(solution)/shard_map/ppermute | solution.py:386
  99.3 0.0 collective-permute-done.5.refs_1_
  99.3 0.0 collective-permute-done.6.refs_2_
  99.3 0.0 all-to-all-done.3.back_ref
  99.3 0.8 shard_map.98
  (1 shorter events, 0.0 us)
Async XLA Ops:
  0.6 17.6 %all-to-all-start = ((bf16[32,8,512]{2,1,0:T(8,128)(2,1)}), bf16[32,8,512]{2,1,0:T(8,128)(2,1)S(1)}, u32[]{:S(2)}, u32[]{:S(2)}) async-start(bf16[32,8,512]{2,1,0:T(8,128)(2,1)} %bitcast.3), calls=%async_computation | async-start | bytes 524288 | tf_op jit(solution)/shard_map/all_to_all | solution.py:25
  19.8 24.3 %copy-start = (f32[8,256]{1,0:T(8,128)S(1)}, f32[8,256]{1,0:T(8,128)}, u32[]{:S(2)}) copy-start(f32[8,256]{1,0:T(8,128)} %lse_hbm.1) | copy-start | bytes 24580
  19.8 24.3 %all-to-all-start.1 = ((bf16[32,3,8,512]{3,2,1,0:T(8,128)(2,1)}), bf16[32,3,8,512]{3,2,1,0:T(8,128)(2,1)S(1)}, u32[]{:S(2)}, u32[]{:S(2)}) async-start(bf16[32,3,8,512]{3,2,1,0:T(8,128)(2,1)} %bitcast.2), calls=%async_computation.1 | async-start | bytes 1572864 | tf_op jit(solution)/shard_map/all_to_all | solution.py:25
  56.8 9.5 %copy-start.1 = (s32[32,3]{0,1:T(4,128)S(1)}, s32[32,3]{0,1:T(4,128)}, u32[]{:S(2)}) copy-start(s32[32,3]{0,1:T(4,128)} %param.15) | copy-start | bytes 1156
  56.8 24.3 %all-to-all-start.2 = ((bf16[32,3,8,512]{3,2,1,0:T(8,128)(2,1)}), bf16[32,3,8,512]{3,2,1,0:T(8,128)(2,1)S(1)}, u32[]{:S(2)}, u32[]{:S(2)}) async-start(bf16[32,3,8,512]{3,2,1,0:T(8,128)(2,1)} %get-tuple-element.8), calls=%async_computation.2 | async-start | bytes 1572864 | tf_op jit(solution)/shard_map/all_to_all | solution.py:25
  59.5 2.9 %collective-permute-start = (bf16[16,256,128]{2,1,0:T(8,128)(2,1)}, bf16[16,256,128]{2,1,0:T(8,128)(2,1)S(1)}, u32[]{:S(2)}, u32[]{:S(2)}) collective-permute-start(bf16[16,256,128]{2,1,0:T(8,128)(2,1)} %get-tuple-element.10), channel_id=1, source_target_pairs={{0,1},{1,0},{2,3},{3,2},{4,5},{5,4},{6,7},{7,6},{8,9},{9,8},{10,11... | collective-permute-start | bytes 3145736 | tf_op jit(solution)/shard_map/ppermute | solution.py:386
  62.7 22.6 %collective-permute-start.1 = (bf16[4,256,128]{2,1,0:T(8,128)(2,1)S(1)}, bf16[4,256,128]{2,1,0:T(8,128)(2,1)S(1)}, u32[]{:S(2)}, u32[]{:S(2)}) collective-permute-start(bf16[4,256,128]{2,1,0:T(8,128)(2,1)S(1)} %get-tuple-element.15), channel_id=1, source_target_pairs={{0,16},{1,17},{2,18},{3,19},{4,20},{5,21},{6,22},{7,23},{8,24},{9,... | collective-permute-start | bytes 786440 | tf_op jit(solution)/shard_map/ppermute | solution.py:386
  64.4 20.9 %collective-permute-start.2 = (bf16[4,256,128]{2,1,0:T(8,128)(2,1)S(1)}, bf16[4,256,128]{2,1,0:T(8,128)(2,1)S(1)}, u32[]{:S(2)}, u32[]{:S(2)}) collective-permute-start(bf16[4,256,128]{2,1,0:T(8,128)(2,1)S(1)} %get-tuple-element.14), channel_id=1, source_target_pairs={{0,2},{1,3},{2,0},{3,1},{4,6},{5,7},{6,4},{7,5},{8,10},{9,11},{10,... | collective-permute-start | bytes 786440 | tf_op jit(solution)/shard_map/ppermute | solution.py:386
  65.9 19.4 %collective-permute-start.3 = (bf16[4,256,128]{2,1,0:T(8,128)(2,1)S(1)}, bf16[4,256,128]{2,1,0:T(8,128)(2,1)S(1)}, u32[]{:S(2)}, u32[]{:S(2)}) collective-permute-start(bf16[4,256,128]{2,1,0:T(8,128)(2,1)S(1)} %get-tuple-element.13), channel_id=1, source_target_pairs={{0,18},{1,19},{2,16},{3,17},{4,22},{5,23},{6,20},{7,21},{8,26},{9,... | collective-permute-start | bytes 786440 | tf_op jit(solution)/shard_map/ppermute | solution.py:386
  82.7 16.7 %all-to-all-start.3 = ((bf16[32,8,512]{2,1,0:T(8,128)(2,1)}), bf16[32,8,512]{2,1,0:T(8,128)(2,1)S(1)}, u32[]{:S(2)}, u32[]{:S(2)}) async-start(bf16[32,8,512]{2,1,0:T(8,128)(2,1)} %shard_map.97), calls=%async_computation.3 | async-start | bytes 524288 | tf_op jit(solution)/shard_map/all_to_all | solution.py:25
  85.5 13.9 %collective-permute-start.4 = (bf16[1,256,128]{2,1,0:T(8,128)(2,1)S(1)}, bf16[1,256,128]{2,1,0:T(8,128)(2,1)S(1)}, u32[]{:S(2)}, u32[]{:S(2)}) collective-permute-start(bf16[1,256,128]{2,1,0:T(8,128)(2,1)S(1)} %get-tuple-element.18), channel_id=1, source_target_pairs={{0,8},{1,9},{2,10},{3,11},{4,12},{5,13},{6,14},{7,15},{8,0},{9,1},... | collective-permute-start | bytes 196616 | tf_op jit(solution)/shard_map/ppermute | solution.py:386
  88.2 11.2 %collective-permute-start.5 = (bf16[1,256,128]{2,1,0:T(8,128)(2,1)S(1)}, bf16[1,256,128]{2,1,0:T(8,128)(2,1)S(1)}, u32[]{:S(2)}, u32[]{:S(2)}) collective-permute-start(bf16[1,256,128]{2,1,0:T(8,128)(2,1)S(1)} %get-tuple-element.17), channel_id=1, source_target_pairs={{0,4},{1,5},{2,6},{3,7},{4,0},{5,1},{6,2},{7,3},{8,12},{9,13},{10,... | collective-permute-start | bytes 196616 | tf_op jit(solution)/shard_map/ppermute | solution.py:386
  89.7 9.6 %collective-permute-start.6 = (bf16[1,256,128]{2,1,0:T(8,128)(2,1)S(1)}, bf16[1,256,128]{2,1,0:T(8,128)(2,1)S(1)}, u32[]{:S(2)}, u32[]{:S(2)}) collective-permute-start(bf16[1,256,128]{2,1,0:T(8,128)(2,1)S(1)} %get-tuple-element.16), channel_id=1, source_target_pairs={{0,12},{1,13},{2,14},{3,15},{4,8},{5,9},{6,10},{7,11},{8,4},{9,5},... | collective-permute-start | bytes 196616 | tf_op jit(solution)/shard_map/ppermute | solution.py:386

commit v7 on v6

--- a/solution.py
+++ b/solution.py
@@ -103,14 +103,14 @@
     arrived_ref,
     packed_hbm,
     terms_hbm,
-    own_hbm,
+    own_both_hbm,
+    grad_query_t_hbm,
     keep_hbm,
     send_hbm,
     query_ref,
     query_t_ref,
     d_out_ref,
     d_out_t_ref,
-    w_query_t_ref,
     w_both_t_ref,
     feats_t_ref,
     grad_out_ref,
@@ -119,7 +119,6 @@
     key_t_ref,
     value_t_ref,
     terms_ref,
-    own_ref,
     grad_query_t_ref,
     out_t_ref,
     grad_both_ref,
@@ -181,7 +180,6 @@
     last_needs = [
         load(part("feats_t"), feats_t_ref.at[:, own]),
         load(part("grad_out"), grad_out_ref),
-        load(part("w_query_t"), w_query_t_ref),
     ]
     key_need.wait()
     for match in range(3):
@@ -278,24 +276,17 @@
 
     place(3 * width, dot(out_t_ref[...], grad_out_ref[...]))
     place(0, dot_nt(feats_t_ref[:, :block], grad_query_t_ref[...]))
-    for start in range(0, 2 * width, block):
-        place(width + start, dot(feats_t_ref[...], grad_both_ref[:, start : start + block]))
+    for start in range(0, 2 * width, 2 * block):
+        place(width + start, dot(feats_t_ref[...], grad_both_ref[:, start : start + 2 * block]))
     store(send_ref, send_hbm)
     store(keep_ref, keep_hbm)
-    for member in range(4):
-        here = slice(member * block, (member + 1) * block)
+    store(grad_both_ref.at[own], own_both_hbm)
+    store(grad_query_t_ref, grad_query_t_hbm)
+    for match in range(3):
+        here = slice((match + 1) * block, (match + 2) * block)
         total = dot(grad_both_ref[here], w_both_t_ref[...])
-        if member == 0:
-            own_ref[...] = total + lax.dot_general(
-                grad_query_t_ref[...],
-                w_query_t_ref[...],
-                (((0,), (0,)), ((), ())),
-                preferred_element_type=WIDE,
-            )
-            store(own_ref, own_hbm)
-        else:
-            terms_ref[member - 1] = total.astype(LOW).reshape(terms_ref.shape[1:])
-            store(terms_ref.at[member - 1], by_match(terms_hbm, member - 1))
+        terms_ref[match] = total.astype(LOW).reshape(terms_ref.shape[1:])
+        store(terms_ref.at[match], by_match(terms_hbm, match))
     for copy in stores:
         copy.wait()
 
@@ -313,23 +304,27 @@
         arrived = arrived.transpose(1, 0, 2, 3).reshape(3, block, width)
     staged = (3, devices, piece, width) if whole_tiles else (3, block, width)
     half = (devices // 2, width // n_outer, 4 * width // n_inner)
-    plain, turned, square = (
+    plain, turned = (
         pltpu.VMEM((block, width), LOW),
         pltpu.VMEM((width, block), LOW),
-        pltpu.VMEM((width, width), LOW),
     )
     long, long_t = pltpu.VMEM((members, width), LOW), pltpu.VMEM((width, members), LOW)
-    terms, own, keep, send = pl.pallas_call(
+    terms, own_both, grad_query_t, keep, send = pl.pallas_call(
         functools.partial(attention_kernel, head_size, group, together, 2 * block, stages, n_inner),
-        out_shape=(shaped(arrived.shape), shaped((block, width), WIDE), shaped(half), shaped(half)),
+        out_shape=(
+            shaped(arrived.shape),
+            shaped((block, 2 * width)),
+            shaped((width, block)),
+            shaped(half),
+            shaped(half),
+        ),
         in_specs=[pl.BlockSpec(memory_space=pltpu.SMEM), ANY, VMEM, ANY],
-        out_specs=(ANY,) * 4,
+        out_specs=(ANY,) * 5,
         scratch_shapes=[
             plain,
             turned,
             plain,
             turned,
-            square,
             pltpu.VMEM((2 * width, width), LOW),
             long_t,
             plain,
@@ -338,7 +333,6 @@
             long_t,
             long_t,
             pltpu.VMEM(staged, LOW),
-            pltpu.VMEM((block, width), WIDE),
             turned,
             turned,
             pltpu.VMEM((members, 2 * width), LOW),
@@ -348,7 +342,7 @@
             pltpu.VMEM((members, together * block), LOW),
             pltpu.VMEM((heads, block), WIDE),
             pltpu.SemaphoreType.DMA((17,)),
-            pltpu.SemaphoreType.DMA((6,)),
+            pltpu.SemaphoreType.DMA((8,)),
         ],
         compiler_params=pltpu.CompilerParams(vmem_limit_bytes=MOST_VMEM),
         cost_estimate=pl.CostEstimate(
@@ -359,7 +353,38 @@
     )(me.reshape(1), log_sum_exp, arrived, packed)
     if not whole_tiles:
         terms = terms.reshape(3, devices, piece, width).transpose(1, 0, 2, 3)
-    return terms, own, keep, send
+    return terms, own_both, grad_query_t, keep, send
+
+
+def own_kernel(both_ref, grad_query_t_ref, packed_hbm, own_ref, weights_ref, sem):
+    width, block = grad_query_t_ref.shape
+    _, places = packing(block, width)
+    copies = []
+    for number, name in enumerate(("w_key_t", "w_value_t", "w_query_t")):
+        target = weights_ref.at[pl.ds(number * width, width)]
+        copies.append(pltpu.make_async_copy(packed_hbm.at[places[name]], target, sem.at[number]))
+        copies[-1].start()
+    for copy in copies:
+        copy.wait()
+    total = dot(both_ref[...], weights_ref[: 2 * width])
+    own_ref[...] = total + dot(grad_query_t_ref[...].T, weights_ref[2 * width :])
+
+
+def own_terms(own_both, grad_query_t, packed):
+    width, block = grad_query_t.shape
+    return pl.pallas_call(
+        own_kernel,
+        out_shape=shaped((block, width), WIDE),
+        in_specs=[VMEM, VMEM, ANY],
+        out_specs=VMEM,
+        scratch_shapes=[pltpu.VMEM((3 * width, width), LOW), pltpu.SemaphoreType.DMA((3,))],
+        compiler_params=pltpu.CompilerParams(vmem_limit_bytes=MOST_VMEM),
+        cost_estimate=pl.CostEstimate(
+            flops=6 * block * width * width,
+            bytes_accessed=2 * (5 * block * width + 3 * width * width),
+            transcendentals=0,
+        ),
+    )(own_both, grad_query_t, packed)
 
 
 def bits_of(count):
@@ -448,7 +473,10 @@
     spread = exchange(node_feats.reshape(devices, piece, width))
     arrived = exchange(spread[partners])
     packed = project(node_feats, grad_out, w_query, w_key, w_value, w_output)
-    terms, own, keep, send = attention(me, stages, arrived, packed, block, width, log_sum_exp)
+    terms, own_both, grad_query_t, keep, send = attention(
+        me, stages, arrived, packed, block, width, log_sum_exp
+    )
+    own = own_terms(own_both, grad_query_t, packed)
     returned = exchange(terms)
     got = [swap(send, 1, devices)]
     summed = collect_pieces(returned, partners)

time: 101 us -> 100 us (0.990)
  waiting for transfers between devices: 53.2 us -> 50.6 us
  Pallas kernels: 19.8 us -> 21.2 us
    ppermute x7, waiting for transfers between devices: 12.2 us -> 10.2 us  [swap(): lax.ppermute(value, AXES, [(device, device ^ mask) for device in range(de...]
    pallas_call x0 -> x1, Pallas kernels: none -> 1.97 us  [own_terms(): pl.pallas_call(own_kernel, out_shape=shaped((block, width), WIDE), in_spe...]
  transfers between devices with their start and end apart: 11 -> 11, of which waited for: 5 -> 5; matrix products, arithmetic and copies ran while one was open for 1% -> 2% of each run, Pallas kernels for 6% -> 8%
where the time goes in v7:
time: 100 us; the launch traced here: 99.6 us
  waiting for transfers between devices  50.6 us (51%)
  starting transfers between devices  23.4 us (23%)
  Pallas kernels  21.2 us (21%)
  other arithmetic  1.82 us (2%)
  local copies, waits for them, and re-layouts  1.82 us (2%)
    all_to_all x4, waiting for transfers between devices, exchange(): return lax.all_to_all(pieces, AXES, split_axis=0, concat_axis=0, tiled=True)  40.4 us
    all_to_all x4, starting transfers between devices, exchange(): return lax.all_to_all(pieces, AXES, split_axis=0, concat_axis=0, tiled=True)  15.3 us
    pallas_call x1, Pallas kernels, attention(): pl.pallas_call(functools.partial(attention_kernel, head_size, group, toge...  12.2 us
    ppermute x7, waiting for transfers between devices, swap(): lax.ppermute(value, AXES, [(device, device ^ mask) for device in range(de...  10.2 us
    ppermute x7, starting transfers between devices, swap(): lax.ppermute(value, AXES, [(device, device ^ mask) for device in range(de...  8.12 us
    pallas_call x1, Pallas kernels, project(): pl.pallas_call(project_kernel, out_shape=shaped((rows, width)), in_specs=...  4.6 us
  transfers between devices with their start and end apart: 11, of which 5 were waited for; matrix products, arithmetic and copies ran while one was open for 2% of the time, Pallas kernels for 8%

profile of v7, /device:TPU:0, one launch (start us, length us, event | category | flops | bytes accessed | tf_op | source)
XLA Modules:
  0.0 99.6 jit_solution(5392518887666585126)
XLA Ops:
  0.6 7.3 %all-to-all-start = ((bf16[32,8,512]{2,1,0:T(8,128)(2,1)}), bf16[32,8,512]{2,1,0:T(8,128)(2,1)S(1)}, u32[]{:S(2)}, u32[]{:S(2)}) async-start(bf16[32,8,512]{2,1,0:T(8,128)(2,1)} %bitcast.3), calls=%async_computation | async-start | bytes 524288 | tf_op jit(solution)/shard_map/all_to_all | solution.py:25
  7.9 0.7 compare_select_fusion
  8.6 0.1 copy.12
  8.7 0.1 reshape.116
  8.8 9.4 %all-to-all-done = bf16[32,8,512]{2,1,0:T(8,128)(2,1)S(1)} async-done(((bf16[32,8,512]{2,1,0:T(8,128)(2,1)}), bf16[32,8,512]{2,1,0:T(8,128)(2,1)S(1)}, u32[]{:S(2)}, u32[]{:S(2)}) %all-to-all-start) | async-done | bytes 262176 | tf_op jit(solution)/shard_map/all_to_all | solution.py:25
  18.2 1.5 %gather_fusion = bf16[96,8,512]{2,1,0:T(8,128)(2,1)} fusion(bf16[32,8,512]{2,1,0:T(8,128)(2,1)S(1)} %all-to-all-done, s32[1024]{0:T(1024)S(1)} %pad_clamp_fusion), kind=kCustom, calls=%fused_computation | custom fusion | bytes 1573248 | tf_op jit(solution)/shard_map/gather | solution.py:474
  19.8 0.0 copy-start
  19.8 2.8 %all-to-all-start.1 = ((bf16[32,3,8,512]{3,2,1,0:T(8,128)(2,1)}), bf16[32,3,8,512]{3,2,1,0:T(8,128)(2,1)S(1)}, u32[]{:S(2)}, u32[]{:S(2)}) async-start(bf16[32,3,8,512]{3,2,1,0:T(8,128)(2,1)} %bitcast.2), calls=%async_computation.1 | async-start | bytes 1572864 | tf_op jit(solution)/shard_map/all_to_all | solution.py:25
  22.5 4.6 %shard_map.95.packed_hbm = bf16[4352,512]{1,0:T(8,128)(2,1)} custom-call(bf16[256,512]{1,0:T(8,128)(2,1)} %feats_ref.1, bf16[256,512]{1,0:T(8,128)(2,1)} %grad_out_ref.1, bf16[512,512]{1,0:T(8,128)(2,1)} %w_query_ref.1, bf16[512,512]{1,0:T(8,128)(2,1)} %w_key_ref.1, bf16[512,512]{1,0:T(8,128)(2,1)} %w_value_ref.1, bf16[512,512]{1,0:T(8,128)(2,1)} %w_output_ref.1), custom_call_target="tpu_custom_call" | custom-call | flops 536870912 | bytes 6291456 | tf_op jit(solution)/shard_map/pallas_call | solution.py:80
  27.1 16.9 %all-to-all-done.1.arrived_ref = bf16[32,3,8,512]{3,2,1,0:T(8,128)(2,1)S(1)} async-done(((bf16[32,3,8,512]{3,2,1,0:T(8,128)(2,1)}), bf16[32,3,8,512]{3,2,1,0:T(8,128)(2,1)S(1)}, u32[]{:S(2)}, u32[]{:S(2)}) %all-to-all-start.1) | async-done | bytes 786464 | tf_op jit(solution)/shard_map/all_to_all | solution.py:25
  44.0 0.0 copy-done
  44.0 12.2 %shard_map.96 = (bf16[32,3,8,512]{3,2,1,0:T(8,128)(2,1)}, bf16[256,1024]{1,0:T(8,128)(2,1)S(1)}, bf16[512,256]{1,0:T(8,128)(2,1)S(1)}, bf16[16,256,128]{2,1,0:T(8,128)(2,1)S(1)}, bf16[16,256,128]{2,1,0:T(8,128)(2,1)}) custom-call(s32[1]{0:T(128)} %bitcast.me_ref, f32[8,256]{1,0:T(8,128)S(1)} %copy-done, ...), custom_call_target="tpu_custom_call" | custom-call | flops 10200547328 | bytes 8388608 | tf_op jit(solution)/shard_map/pallas_call | solution.py:312
  56.2 0.0 copy-start.1
  56.2 2.6 %all-to-all-start.2 = ((bf16[32,3,8,512]{3,2,1,0:T(8,128)(2,1)}), bf16[32,3,8,512]{3,2,1,0:T(8,128)(2,1)S(1)}, u32[]{:S(2)}, u32[]{:S(2)}) async-start(bf16[32,3,8,512]{3,2,1,0:T(8,128)(2,1)} %get-tuple-element.10), calls=%async_computation.2 | async-start | bytes 1572864 | tf_op jit(solution)/shard_map/all_to_all | solution.py:25
  58.9 0.2 collective-permute-start
  59.1 2.8 %collective-permute-done = bf16[16,256,128]{2,1,0:T(8,128)(2,1)S(1)} collective-permute-done((bf16[16,256,128]{2,1,0:T(8,128)(2,1)}, bf16[16,256,128]{2,1,0:T(8,128)(2,1)S(1)}, u32[]{:S(2)}, u32[]{:S(2)}) %collective-permute-start) | collective-permute-done | bytes 1048608 | tf_op jit(solution)/shard_map/ppermute | solution.py:411
  61.8 1.0 add_convert_fusion.3
  62.8 2.6 %collective-permute-start.3 = (bf16[4,256,128]{2,1,0:T(8,128)(2,1)}, bf16[4,256,128]{2,1,0:T(8,128)(2,1)S(1)}, u32[]{:S(2)}, u32[]{:S(2)}) collective-permute-start(bf16[4,256,128]{2,1,0:T(8,128)(2,1)} %get-tuple-element.15), channel_id=1, source_target_pairs={{0,18},{1,19},{2,16},{3,17},{4,22},{5,23},{6,20},{7,21},{8,26},{9,... | collective-permute-start | bytes 786440 | tf_op jit(solution)/shard_map/ppermute | solution.py:411
  65.4 0.5 collective-permute-start.2
  65.9 0.4 collective-permute-start.1
  66.3 0.0 copy-done.1
  66.3 0.1 copy.13.partners_ref
  66.4 14.1 %all-to-all-done.2.returned_ref = bf16[32,3,8,512]{3,2,1,0:T(8,128)(2,1)S(1)} async-done(((bf16[32,3,8,512]{3,2,1,0:T(8,128)(2,1)}), bf16[32,3,8,512]{3,2,1,0:T(8,128)(2,1)S(1)}, u32[]{:S(2)}, u32[]{:S(2)}) %all-to-all-start.2) | async-done | bytes 786464 | tf_op jit(solution)/shard_map/all_to_all | solution.py:25
  80.5 1.6 %shard_map.98 = bf16[32,8,512]{2,1,0:T(8,128)(2,1)} custom-call(s32[32,3]{1,0:T(8,128)S(1)} %copy.13.partners_ref, bf16[32,3,8,512]{3,2,1,0:T(8,128)(2,1)S(1)} %all-to-all-done.2.returned_ref), custom_call_target="tpu_custom_call" | custom-call | tf_op jit(solution)/shard_map/pallas_call | solution.py:438
  82.1 2.6 %all-to-all-start.3 = ((bf16[32,8,512]{2,1,0:T(8,128)(2,1)}), bf16[32,8,512]{2,1,0:T(8,128)(2,1)S(1)}, u32[]{:S(2)}, u32[]{:S(2)}) async-start(bf16[32,8,512]{2,1,0:T(8,128)(2,1)} %shard_map.98), calls=%async_computation.3 | async-start | bytes 524288 | tf_op jit(solution)/shard_map/all_to_all | solution.py:25
  84.7 0.0 collective-permute-done.3
  84.7 0.0 collective-permute-done.2
  84.7 0.0 collective-permute-done.1
  84.7 0.1 add_convert_fusion.4
  84.9 2.7 %collective-permute-start.4 = (bf16[1,256,128]{2,1,0:T(8,128)(2,1)S(1)}, bf16[1,256,128]{2,1,0:T(8,128)(2,1)S(1)}, u32[]{:S(2)}, u32[]{:S(2)}) collective-permute-start(bf16[1,256,128]{2,1,0:T(8,128)(2,1)S(1)} %get-tuple-element.20), channel_id=1, source_target_pairs={{0,8},{1,9},{2,10},{3,11},{4,12},{5,13},{6,14},{7,15},{8,0},{9,1},... | collective-permute-start | bytes 196616 | tf_op jit(solution)/shard_map/ppermute | solution.py:411
  87.6 1.5 %collective-permute-start.5 = (bf16[1,256,128]{2,1,0:T(8,128)(2,1)S(1)}, bf16[1,256,128]{2,1,0:T(8,128)(2,1)S(1)}, u32[]{:S(2)}, u32[]{:S(2)}) collective-permute-start(bf16[1,256,128]{2,1,0:T(8,128)(2,1)S(1)} %get-tuple-element.19), channel_id=1, source_target_pairs={{0,4},{1,5},{2,6},{3,7},{4,0},{5,1},{6,2},{7,3},{8,12},{9,13},{10,... | collective-permute-start | bytes 196616 | tf_op jit(solution)/shard_map/ppermute | solution.py:411
  89.1 0.2 collective-permute-start.6
  89.4 2.0 %shard_map.97.own_ref = f32[256,512]{1,0:T(8,128)S(1)} custom-call(bf16[256,1024]{1,0:T(8,128)(2,1)S(1)} %get-tuple-element.8.both_ref, bf16[512,256]{1,0:T(8,128)(2,1)S(1)} %get-tuple-element.9.grad_query_t_ref, bf16[4352,512]{1,0:T(8,128)(2,1)} %shard_map.95.packed_hbm), custom_call_target="tpu_custom_call" | custom-call | flops 402653184 | bytes 2883584 | tf_op jit(solution)/shard_map/pallas_call | solution.py:375
  91.3 7.4 %collective-permute-done.4.refs_0_ = bf16[1,256,128]{2,1,0:T(8,128)(2,1)S(1)} collective-permute-done((bf16[1,256,128]{2,1,0:T(8,128)(2,1)S(1)}, bf16[1,256,128]{2,1,0:T(8,128)(2,1)S(1)}, u32[]{:S(2)}, u32[]{:S(2)}) %collective-permute-start.4) | collective-permute-done | bytes 65568 | tf_op jit(solution)/shard_map/ppermute | solution.py:411
  98.8 0.0 collective-permute-done.5.refs_1_
  98.8 0.0 collective-permute-done.6.refs_2_
  98.8 0.0 all-to-all-done.3.back_ref
  98.8 0.8 shard_map.99
  (1 shorter events, 0.0 us)
Async XLA Ops:
  0.6 17.6 %all-to-all-start = ((bf16[32,8,512]{2,1,0:T(8,128)(2,1)}), bf16[32,8,512]{2,1,0:T(8,128)(2,1)S(1)}, u32[]{:S(2)}, u32[]{:S(2)}) async-start(bf16[32,8,512]{2,1,0:T(8,128)(2,1)} %bitcast.3), calls=%async_computation | async-start | bytes 524288 | tf_op jit(solution)/shard_map/all_to_all | solution.py:25
  19.8 24.3 %copy-start = (f32[8,256]{1,0:T(8,128)S(1)}, f32[8,256]{1,0:T(8,128)}, u32[]{:S(2)}) copy-start(f32[8,256]{1,0:T(8,128)} %lse_hbm.1) | copy-start | bytes 24580
  19.8 24.3 %all-to-all-start.1 = ((bf16[32,3,8,512]{3,2,1,0:T(8,128)(2,1)}), bf16[32,3,8,512]{3,2,1,0:T(8,128)(2,1)S(1)}, u32[]{:S(2)}, u32[]{:S(2)}) async-start(bf16[32,3,8,512]{3,2,1,0:T(8,128)(2,1)} %bitcast.2), calls=%async_computation.1 | async-start | bytes 1572864 | tf_op jit(solution)/shard_map/all_to_all | solution.py:25
  56.2 10.1 %copy-start.1 = (s32[32,3]{0,1:T(4,128)S(1)}, s32[32,3]{0,1:T(4,128)}, u32[]{:S(2)}) copy-start(s32[32,3]{0,1:T(4,128)} %param.15) | copy-start | bytes 1156
  56.2 24.3 %all-to-all-start.2 = ((bf16[32,3,8,512]{3,2,1,0:T(8,128)(2,1)}), bf16[32,3,8,512]{3,2,1,0:T(8,128)(2,1)S(1)}, u32[]{:S(2)}, u32[]{:S(2)}) async-start(bf16[32,3,8,512]{3,2,1,0:T(8,128)(2,1)} %get-tuple-element.10), calls=%async_computation.2 | async-start | bytes 1572864 | tf_op jit(solution)/shard_map/all_to_all | solution.py:25
  58.9 2.9 %collective-permute-start = (bf16[16,256,128]{2,1,0:T(8,128)(2,1)}, bf16[16,256,128]{2,1,0:T(8,128)(2,1)S(1)}, u32[]{:S(2)}, u32[]{:S(2)}) collective-permute-start(bf16[16,256,128]{2,1,0:T(8,128)(2,1)} %get-tuple-element.12), channel_id=1, source_target_pairs={{0,1},{1,0},{2,3},{3,2},{4,5},{5,4},{6,7},{7,6},{8,9},{9,8},{10,11... | collective-permute-start | bytes 3145736 | tf_op jit(solution)/shard_map/ppermute | solution.py:411
  62.8 21.9 %collective-permute-start.3 = (bf16[4,256,128]{2,1,0:T(8,128)(2,1)}, bf16[4,256,128]{2,1,0:T(8,128)(2,1)S(1)}, u32[]{:S(2)}, u32[]{:S(2)}) collective-permute-start(bf16[4,256,128]{2,1,0:T(8,128)(2,1)} %get-tuple-element.15), channel_id=1, source_target_pairs={{0,18},{1,19},{2,16},{3,17},{4,22},{5,23},{6,20},{7,21},{8,26},{9,... | collective-permute-start | bytes 786440 | tf_op jit(solution)/shard_map/ppermute | solution.py:411
  65.4 19.3 %collective-permute-start.2 = (bf16[4,256,128]{2,1,0:T(8,128)(2,1)S(1)}, bf16[4,256,128]{2,1,0:T(8,128)(2,1)S(1)}, u32[]{:S(2)}, u32[]{:S(2)}) collective-permute-start(bf16[4,256,128]{2,1,0:T(8,128)(2,1)S(1)} %get-tuple-element.16), channel_id=1, source_target_pairs={{0,2},{1,3},{2,0},{3,1},{4,6},{5,7},{6,4},{7,5},{8,10},{9,11},{10,... | collective-permute-start | bytes 786440 | tf_op jit(solution)/shard_map/ppermute | solution.py:411
  65.9 18.8 %collective-permute-start.1 = (bf16[4,256,128]{2,1,0:T(8,128)(2,1)S(1)}, bf16[4,256,128]{2,1,0:T(8,128)(2,1)S(1)}, u32[]{:S(2)}, u32[]{:S(2)}) collective-permute-start(bf16[4,256,128]{2,1,0:T(8,128)(2,1)S(1)} %get-tuple-element.17), channel_id=1, source_target_pairs={{0,16},{1,17},{2,18},{3,19},{4,20},{5,21},{6,22},{7,23},{8,24},{9,... | collective-permute-start | bytes 786440 | tf_op jit(solution)/shard_map/ppermute | solution.py:411
  82.1 16.7 %all-to-all-start.3 = ((bf16[32,8,512]{2,1,0:T(8,128)(2,1)}), bf16[32,8,512]{2,1,0:T(8,128)(2,1)S(1)}, u32[]{:S(2)}, u32[]{:S(2)}) async-start(bf16[32,8,512]{2,1,0:T(8,128)(2,1)} %shard_map.98), calls=%async_computation.3 | async-start | bytes 524288 | tf_op jit(solution)/shard_map/all_to_all | solution.py:25
  84.9 13.9 %collective-permute-start.4 = (bf16[1,256,128]{2,1,0:T(8,128)(2,1)S(1)}, bf16[1,256,128]{2,1,0:T(8,128)(2,1)S(1)}, u32[]{:S(2)}, u32[]{:S(2)}) collective-permute-start(bf16[1,256,128]{2,1,0:T(8,128)(2,1)S(1)} %get-tuple-element.20), channel_id=1, source_target_pairs={{0,8},{1,9},{2,10},{3,11},{4,12},{5,13},{6,14},{7,15},{8,0},{9,1},... | collective-permute-start | bytes 196616 | tf_op jit(solution)/shard_map/ppermute | solution.py:411
  87.6 11.2 %collective-permute-start.5 = (bf16[1,256,128]{2,1,0:T(8,128)(2,1)S(1)}, bf16[1,256,128]{2,1,0:T(8,128)(2,1)S(1)}, u32[]{:S(2)}, u32[]{:S(2)}) collective-permute-start(bf16[1,256,128]{2,1,0:T(8,128)(2,1)S(1)} %get-tuple-element.19), channel_id=1, source_target_pairs={{0,4},{1,5},{2,6},{3,7},{4,0},{5,1},{6,2},{7,3},{8,12},{9,13},{10,... | collective-permute-start | bytes 196616 | tf_op jit(solution)/shard_map/ppermute | solution.py:411
  89.1 9.6 %collective-permute-start.6 = (bf16[1,256,128]{2,1,0:T(8,128)(2,1)S(1)}, bf16[1,256,128]{2,1,0:T(8,128)(2,1)S(1)}, u32[]{:S(2)}, u32[]{:S(2)}) collective-permute-start(bf16[1,256,128]{2,1,0:T(8,128)(2,1)S(1)} %get-tuple-element.18), channel_id=1, source_target_pairs={{0,12},{1,13},{2,14},{3,15},{4,8},{5,9},{6,10},{7,11},{8,4},{9,5},... | collective-permute-start | bytes 196616 | tf_op jit(solution)/shard_map/ppermute | solution.py:411

commit v8 on v7

--- a/solution.py
+++ b/solution.py
@@ -181,6 +181,8 @@
         load(part("feats_t"), feats_t_ref.at[:, own]),
         load(part("grad_out"), grad_out_ref),
     ]
+    for match in range(3):
+        feats_t_ref[:, (match + 1) * block : (match + 2) * block] = far_rows(match).T
     key_need.wait()
     for match in range(3):
         here = slice((match + 1) * block, (match + 2) * block)
@@ -193,7 +195,6 @@
         far_value = dot_nt(far, w_both_t_ref[width:]).astype(LOW)
         value_ref[here] = far_value
         value_t_ref[:, here] = far_value.T
-        feats_t_ref[:, here] = far.T
     for copy in head_needs:
         copy.wait()
     span = group * head_size
@@ -250,6 +251,8 @@
         for head in batch_heads:
             inner, cols, rows, lanes = places(head)
             grad_query_t_ref[rows, :] = dot(key_t_ref[rows, :], grad_score_ref[:, lanes]).astype(LOW)
+    store(grad_both_ref.at[own], own_both_hbm)
+    store(grad_query_t_ref, grad_query_t_hbm)
     for copy in last_needs:
         copy.wait()
 
@@ -280,8 +283,6 @@
         place(width + start, dot(feats_t_ref[...], grad_both_ref[:, start : start + 2 * block]))
     store(send_ref, send_hbm)
     store(keep_ref, keep_hbm)
-    store(grad_both_ref.at[own], own_both_hbm)
-    store(grad_query_t_ref, grad_query_t_hbm)
     for match in range(3):
         here = slice((match + 1) * block, (match + 2) * block)
         total = dot(grad_both_ref[here], w_both_t_ref[...])

time: 100 us -> 100 us (level)
  no operation moved by 1% of the time
where the time goes in v8:
time: 100 us; the launch traced here: 99.5 us
  waiting for transfers between devices  50.6 us (51%)
  starting transfers between devices  23.4 us (23%)
  Pallas kernels  21.1 us (21%)
  other arithmetic  1.82 us (2%)
  local copies, waits for them, and re-layouts  1.82 us (2%)
    all_to_all x4, waiting for transfers between devices, exchange(): return lax.all_to_all(pieces, AXES, split_axis=0, concat_axis=0, tiled=True)  40.4 us
    all_to_all x4, starting transfers between devices, exchange(): return lax.all_to_all(pieces, AXES, split_axis=0, concat_axis=0, tiled=True)  15.3 us
    pallas_call x1, Pallas kernels, attention(): pl.pallas_call(functools.partial(attention_kernel, head_size, group, toge...  12.1 us
    ppermute x7, waiting for transfers between devices, swap(): lax.ppermute(value, AXES, [(device, device ^ mask) for device in range(de...  10.2 us
    ppermute x7, starting transfers between devices, swap(): lax.ppermute(value, AXES, [(device, device ^ mask) for device in range(de...  8.12 us
    pallas_call x1, Pallas kernels, project(): pl.pallas_call(project_kernel, out_shape=shaped((rows, width)), in_specs=...  4.6 us
  transfers between devices with their start and end apart: 11, of which 5 were waited for; matrix products, arithmetic and copies ran while one was open for 2% of the time, Pallas kernels for 8%

profile of v8, /device:TPU:0, one launch (start us, length us, event | category | flops | bytes accessed | tf_op | source)
XLA Modules:
  0.0 99.5 jit_solution(16827532687131677514)
XLA Ops:
  0.6 7.3 %all-to-all-start = ((bf16[32,8,512]{2,1,0:T(8,128)(2,1)}), bf16[32,8,512]{2,1,0:T(8,128)(2,1)S(1)}, u32[]{:S(2)}, u32[]{:S(2)}) async-start(bf16[32,8,512]{2,1,0:T(8,128)(2,1)} %bitcast.3), calls=%async_computation | async-start | bytes 524288 | tf_op jit(solution)/shard_map/all_to_all | solution.py:25
  7.9 0.7 compare_select_fusion
  8.6 0.1 copy.12
  8.7 0.1 reshape.116
  8.8 9.4 %all-to-all-done = bf16[32,8,512]{2,1,0:T(8,128)(2,1)S(1)} async-done(((bf16[32,8,512]{2,1,0:T(8,128)(2,1)}), bf16[32,8,512]{2,1,0:T(8,128)(2,1)S(1)}, u32[]{:S(2)}, u32[]{:S(2)}) %all-to-all-start) | async-done | bytes 262176 | tf_op jit(solution)/shard_map/all_to_all | solution.py:25
  18.2 1.5 %gather_fusion = bf16[96,8,512]{2,1,0:T(8,128)(2,1)} fusion(bf16[32,8,512]{2,1,0:T(8,128)(2,1)S(1)} %all-to-all-done, s32[1024]{0:T(1024)S(1)} %pad_clamp_fusion), kind=kCustom, calls=%fused_computation | custom fusion | bytes 1573248 | tf_op jit(solution)/shard_map/gather | solution.py:475
  19.8 0.0 copy-start
  19.8 2.8 %all-to-all-start.1 = ((bf16[32,3,8,512]{3,2,1,0:T(8,128)(2,1)}), bf16[32,3,8,512]{3,2,1,0:T(8,128)(2,1)S(1)}, u32[]{:S(2)}, u32[]{:S(2)}) async-start(bf16[32,3,8,512]{3,2,1,0:T(8,128)(2,1)} %bitcast.2), calls=%async_computation.1 | async-start | bytes 1572864 | tf_op jit(solution)/shard_map/all_to_all | solution.py:25
  22.5 4.6 %shard_map.95.packed_hbm = bf16[4352,512]{1,0:T(8,128)(2,1)} custom-call(bf16[256,512]{1,0:T(8,128)(2,1)} %feats_ref.1, bf16[256,512]{1,0:T(8,128)(2,1)} %grad_out_ref.1, bf16[512,512]{1,0:T(8,128)(2,1)} %w_query_ref.1, bf16[512,512]{1,0:T(8,128)(2,1)} %w_key_ref.1, bf16[512,512]{1,0:T(8,128)(2,1)} %w_value_ref.1, bf16[512,512]{1,0:T(8,128)(2,1)} %w_output_ref.1), custom_call_target="tpu_custom_call" | custom-call | flops 536870912 | bytes 6291456 | tf_op jit(solution)/shard_map/pallas_call | solution.py:80
  27.1 16.9 %all-to-all-done.1.arrived_ref = bf16[32,3,8,512]{3,2,1,0:T(8,128)(2,1)S(1)} async-done(((bf16[32,3,8,512]{3,2,1,0:T(8,128)(2,1)}), bf16[32,3,8,512]{3,2,1,0:T(8,128)(2,1)S(1)}, u32[]{:S(2)}, u32[]{:S(2)}) %all-to-all-start.1) | async-done | bytes 786464 | tf_op jit(solution)/shard_map/all_to_all | solution.py:25
  44.0 0.0 copy-done
  44.0 12.1 %shard_map.96 = (bf16[32,3,8,512]{3,2,1,0:T(8,128)(2,1)}, bf16[256,1024]{1,0:T(8,128)(2,1)S(1)}, bf16[512,256]{1,0:T(8,128)(2,1)S(1)}, bf16[16,256,128]{2,1,0:T(8,128)(2,1)S(1)}, bf16[16,256,128]{2,1,0:T(8,128)(2,1)}) custom-call(s32[1]{0:T(128)} %bitcast.me_ref, f32[8,256]{1,0:T(8,128)S(1)} %copy-done, ...), custom_call_target="tpu_custom_call" | custom-call | flops 10200547328 | bytes 8388608 | tf_op jit(solution)/shard_map/pallas_call | solution.py:313
  56.2 0.0 copy-start.1
  56.2 2.6 %all-to-all-start.2 = ((bf16[32,3,8,512]{3,2,1,0:T(8,128)(2,1)}), bf16[32,3,8,512]{3,2,1,0:T(8,128)(2,1)S(1)}, u32[]{:S(2)}, u32[]{:S(2)}) async-start(bf16[32,3,8,512]{3,2,1,0:T(8,128)(2,1)} %get-tuple-element.10), calls=%async_computation.2 | async-start | bytes 1572864 | tf_op jit(solution)/shard_map/all_to_all | solution.py:25
  58.8 0.2 collective-permute-start
  59.0 2.8 %collective-permute-done = bf16[16,256,128]{2,1,0:T(8,128)(2,1)S(1)} collective-permute-done((bf16[16,256,128]{2,1,0:T(8,128)(2,1)}, bf16[16,256,128]{2,1,0:T(8,128)(2,1)S(1)}, u32[]{:S(2)}, u32[]{:S(2)}) %collective-permute-start) | collective-permute-done | bytes 1048608 | tf_op jit(solution)/shard_map/ppermute | solution.py:412
  61.8 1.0 add_convert_fusion.3
  62.7 2.6 %collective-permute-start.3 = (bf16[4,256,128]{2,1,0:T(8,128)(2,1)}, bf16[4,256,128]{2,1,0:T(8,128)(2,1)S(1)}, u32[]{:S(2)}, u32[]{:S(2)}) collective-permute-start(bf16[4,256,128]{2,1,0:T(8,128)(2,1)} %get-tuple-element.15), channel_id=1, source_target_pairs={{0,18},{1,19},{2,16},{3,17},{4,22},{5,23},{6,20},{7,21},{8,26},{9,... | collective-permute-start | bytes 786440 | tf_op jit(solution)/shard_map/ppermute | solution.py:412
  65.3 0.5 collective-permute-start.2
  65.8 0.4 collective-permute-start.1
  66.2 0.0 copy-done.1
  66.2 0.1 copy.13.partners_ref
  66.3 14.1 %all-to-all-done.2.returned_ref = bf16[32,3,8,512]{3,2,1,0:T(8,128)(2,1)S(1)} async-done(((bf16[32,3,8,512]{3,2,1,0:T(8,128)(2,1)}), bf16[32,3,8,512]{3,2,1,0:T(8,128)(2,1)S(1)}, u32[]{:S(2)}, u32[]{:S(2)}) %all-to-all-start.2) | async-done | bytes 786464 | tf_op jit(solution)/shard_map/all_to_all | solution.py:25
  80.4 1.6 %shard_map.98 = bf16[32,8,512]{2,1,0:T(8,128)(2,1)} custom-call(s32[32,3]{1,0:T(8,128)S(1)} %copy.13.partners_ref, bf16[32,3,8,512]{3,2,1,0:T(8,128)(2,1)S(1)} %all-to-all-done.2.returned_ref), custom_call_target="tpu_custom_call" | custom-call | tf_op jit(solution)/shard_map/pallas_call | solution.py:439
  82.0 2.6 %all-to-all-start.3 = ((bf16[32,8,512]{2,1,0:T(8,128)(2,1)}), bf16[32,8,512]{2,1,0:T(8,128)(2,1)S(1)}, u32[]{:S(2)}, u32[]{:S(2)}) async-start(bf16[32,8,512]{2,1,0:T(8,128)(2,1)} %shard_map.98), calls=%async_computation.3 | async-start | bytes 524288 | tf_op jit(solution)/shard_map/all_to_all | solution.py:25
  84.6 0.0 collective-permute-done.3
  84.7 0.0 collective-permute-done.2
  84.7 0.0 collective-permute-done.1
  84.7 0.1 add_convert_fusion.4
  84.8 2.7 %collective-permute-start.4 = (bf16[1,256,128]{2,1,0:T(8,128)(2,1)S(1)}, bf16[1,256,128]{2,1,0:T(8,128)(2,1)S(1)}, u32[]{:S(2)}, u32[]{:S(2)}) collective-permute-start(bf16[1,256,128]{2,1,0:T(8,128)(2,1)S(1)} %get-tuple-element.20), channel_id=1, source_target_pairs={{0,8},{1,9},{2,10},{3,11},{4,12},{5,13},{6,14},{7,15},{8,0},{9,1},... | collective-permute-start | bytes 196616 | tf_op jit(solution)/shard_map/ppermute | solution.py:412
  87.5 1.5 %collective-permute-start.5 = (bf16[1,256,128]{2,1,0:T(8,128)(2,1)S(1)}, bf16[1,256,128]{2,1,0:T(8,128)(2,1)S(1)}, u32[]{:S(2)}, u32[]{:S(2)}) collective-permute-start(bf16[1,256,128]{2,1,0:T(8,128)(2,1)S(1)} %get-tuple-element.19), channel_id=1, source_target_pairs={{0,4},{1,5},{2,6},{3,7},{4,0},{5,1},{6,2},{7,3},{8,12},{9,13},{10,... | collective-permute-start | bytes 196616 | tf_op jit(solution)/shard_map/ppermute | solution.py:412
  89.1 0.2 collective-permute-start.6
  89.3 2.0 %shard_map.97.own_ref = f32[256,512]{1,0:T(8,128)S(1)} custom-call(bf16[256,1024]{1,0:T(8,128)(2,1)S(1)} %get-tuple-element.8.both_ref, bf16[512,256]{1,0:T(8,128)(2,1)S(1)} %get-tuple-element.9.grad_query_t_ref, bf16[4352,512]{1,0:T(8,128)(2,1)} %shard_map.95.packed_hbm), custom_call_target="tpu_custom_call" | custom-call | flops 402653184 | bytes 2883584 | tf_op jit(solution)/shard_map/pallas_call | solution.py:376
  91.3 7.4 %collective-permute-done.4.refs_0_ = bf16[1,256,128]{2,1,0:T(8,128)(2,1)S(1)} collective-permute-done((bf16[1,256,128]{2,1,0:T(8,128)(2,1)S(1)}, bf16[1,256,128]{2,1,0:T(8,128)(2,1)S(1)}, u32[]{:S(2)}, u32[]{:S(2)}) %collective-permute-start.4) | collective-permute-done | bytes 65568 | tf_op jit(solution)/shard_map/ppermute | solution.py:412
  98.7 0.0 collective-permute-done.5.refs_1_
  98.7 0.0 collective-permute-done.6.refs_2_
  98.7 0.0 all-to-all-done.3.back_ref
  98.7 0.8 shard_map.99
  (1 shorter events, 0.0 us)
Async XLA Ops:
  0.6 17.6 %all-to-all-start = ((bf16[32,8,512]{2,1,0:T(8,128)(2,1)}), bf16[32,8,512]{2,1,0:T(8,128)(2,1)S(1)}, u32[]{:S(2)}, u32[]{:S(2)}) async-start(bf16[32,8,512]{2,1,0:T(8,128)(2,1)} %bitcast.3), calls=%async_computation | async-start | bytes 524288 | tf_op jit(solution)/shard_map/all_to_all | solution.py:25
  19.8 24.3 %copy-start = (f32[8,256]{1,0:T(8,128)S(1)}, f32[8,256]{1,0:T(8,128)}, u32[]{:S(2)}) copy-start(f32[8,256]{1,0:T(8,128)} %lse_hbm.1) | copy-start | bytes 24580
  19.8 24.3 %all-to-all-start.1 = ((bf16[32,3,8,512]{3,2,1,0:T(8,128)(2,1)}), bf16[32,3,8,512]{3,2,1,0:T(8,128)(2,1)S(1)}, u32[]{:S(2)}, u32[]{:S(2)}) async-start(bf16[32,3,8,512]{3,2,1,0:T(8,128)(2,1)} %bitcast.2), calls=%async_computation.1 | async-start | bytes 1572864 | tf_op jit(solution)/shard_map/all_to_all | solution.py:25
  56.2 10.1 %copy-start.1 = (s32[32,3]{0,1:T(4,128)S(1)}, s32[32,3]{0,1:T(4,128)}, u32[]{:S(2)}) copy-start(s32[32,3]{0,1:T(4,128)} %param.15) | copy-start | bytes 1156
  56.2 24.3 %all-to-all-start.2 = ((bf16[32,3,8,512]{3,2,1,0:T(8,128)(2,1)}), bf16[32,3,8,512]{3,2,1,0:T(8,128)(2,1)S(1)}, u32[]{:S(2)}, u32[]{:S(2)}) async-start(bf16[32,3,8,512]{3,2,1,0:T(8,128)(2,1)} %get-tuple-element.10), calls=%async_computation.2 | async-start | bytes 1572864 | tf_op jit(solution)/shard_map/all_to_all | solution.py:25
  58.8 2.9 %collective-permute-start = (bf16[16,256,128]{2,1,0:T(8,128)(2,1)}, bf16[16,256,128]{2,1,0:T(8,128)(2,1)S(1)}, u32[]{:S(2)}, u32[]{:S(2)}) collective-permute-start(bf16[16,256,128]{2,1,0:T(8,128)(2,1)} %get-tuple-element.12), channel_id=1, source_target_pairs={{0,1},{1,0},{2,3},{3,2},{4,5},{5,4},{6,7},{7,6},{8,9},{9,8},{10,11... | collective-permute-start | bytes 3145736 | tf_op jit(solution)/shard_map/ppermute | solution.py:412
  62.7 21.9 %collective-permute-start.3 = (bf16[4,256,128]{2,1,0:T(8,128)(2,1)}, bf16[4,256,128]{2,1,0:T(8,128)(2,1)S(1)}, u32[]{:S(2)}, u32[]{:S(2)}) collective-permute-start(bf16[4,256,128]{2,1,0:T(8,128)(2,1)} %get-tuple-element.15), channel_id=1, source_target_pairs={{0,18},{1,19},{2,16},{3,17},{4,22},{5,23},{6,20},{7,21},{8,26},{9,... | collective-permute-start | bytes 786440 | tf_op jit(solution)/shard_map/ppermute | solution.py:412
  65.3 19.3 %collective-permute-start.2 = (bf16[4,256,128]{2,1,0:T(8,128)(2,1)S(1)}, bf16[4,256,128]{2,1,0:T(8,128)(2,1)S(1)}, u32[]{:S(2)}, u32[]{:S(2)}) collective-permute-start(bf16[4,256,128]{2,1,0:T(8,128)(2,1)S(1)} %get-tuple-element.16), channel_id=1, source_target_pairs={{0,2},{1,3},{2,0},{3,1},{4,6},{5,7},{6,4},{7,5},{8,10},{9,11},{10,... | collective-permute-start | bytes 786440 | tf_op jit(solution)/shard_map/ppermute | solution.py:412
  65.8 18.8 %collective-permute-start.1 = (bf16[4,256,128]{2,1,0:T(8,128)(2,1)S(1)}, bf16[4,256,128]{2,1,0:T(8,128)(2,1)S(1)}, u32[]{:S(2)}, u32[]{:S(2)}) collective-permute-start(bf16[4,256,128]{2,1,0:T(8,128)(2,1)S(1)} %get-tuple-element.17), channel_id=1, source_target_pairs={{0,16},{1,17},{2,18},{3,19},{4,20},{5,21},{6,22},{7,23},{8,24},{9,... | collective-permute-start | bytes 786440 | tf_op jit(solution)/shard_map/ppermute | solution.py:412
  82.0 16.7 %all-to-all-start.3 = ((bf16[32,8,512]{2,1,0:T(8,128)(2,1)}), bf16[32,8,512]{2,1,0:T(8,128)(2,1)S(1)}, u32[]{:S(2)}, u32[]{:S(2)}) async-start(bf16[32,8,512]{2,1,0:T(8,128)(2,1)} %shard_map.98), calls=%async_computation.3 | async-start | bytes 524288 | tf_op jit(solution)/shard_map/all_to_all | solution.py:25
  84.8 13.9 %collective-permute-start.4 = (bf16[1,256,128]{2,1,0:T(8,128)(2,1)S(1)}, bf16[1,256,128]{2,1,0:T(8,128)(2,1)S(1)}, u32[]{:S(2)}, u32[]{:S(2)}) collective-permute-start(bf16[1,256,128]{2,1,0:T(8,128)(2,1)S(1)} %get-tuple-element.20), channel_id=1, source_target_pairs={{0,8},{1,9},{2,10},{3,11},{4,12},{5,13},{6,14},{7,15},{8,0},{9,1},... | collective-permute-start | bytes 196616 | tf_op jit(solution)/shard_map/ppermute | solution.py:412
  87.5 11.2 %collective-permute-start.5 = (bf16[1,256,128]{2,1,0:T(8,128)(2,1)S(1)}, bf16[1,256,128]{2,1,0:T(8,128)(2,1)S(1)}, u32[]{:S(2)}, u32[]{:S(2)}) collective-permute-start(bf16[1,256,128]{2,1,0:T(8,128)(2,1)S(1)} %get-tuple-element.19), channel_id=1, source_target_pairs={{0,4},{1,5},{2,6},{3,7},{4,0},{5,1},{6,2},{7,3},{8,12},{9,13},{10,... | collective-permute-start | bytes 196616 | tf_op jit(solution)/shard_map/ppermute | solution.py:412
  89.1 9.6 %collective-permute-start.6 = (bf16[1,256,128]{2,1,0:T(8,128)(2,1)S(1)}, bf16[1,256,128]{2,1,0:T(8,128)(2,1)S(1)}, u32[]{:S(2)}, u32[]{:S(2)}) collective-permute-start(bf16[1,256,128]{2,1,0:T(8,128)(2,1)S(1)} %get-tuple-element.18), channel_id=1, source_target_pairs={{0,12},{1,13},{2,14},{3,15},{4,8},{5,9},{6,10},{7,11},{8,4},{9,5},... | collective-permute-start | bytes 196616 | tf_op jit(solution)/shard_map/ppermute | solution.py:412

commit v9 on v8

--- a/solution.py
+++ b/solution.py
@@ -311,7 +311,7 @@
     )
     long, long_t = pltpu.VMEM((members, width), LOW), pltpu.VMEM((width, members), LOW)
     terms, own_both, grad_query_t, keep, send = pl.pallas_call(
-        functools.partial(attention_kernel, head_size, group, together, 2 * block, stages, n_inner),
+        functools.partial(attention_kernel, head_size, group, together, block, stages, n_inner),
         out_shape=(
             shaped(arrived.shape),
             shaped((block, 2 * width)),

time: 100 us -> 100 us (level)
  no operation moved by 1% of the time
where the time goes in v9:
time: 100 us; the launch traced here: 99.5 us
  waiting for transfers between devices  50.6 us (51%)
  starting transfers between devices  23.4 us (23%)
  Pallas kernels  21.1 us (21%)
  other arithmetic  1.82 us (2%)
  local copies, waits for them, and re-layouts  1.82 us (2%)
    all_to_all x4, waiting for transfers between devices, exchange(): return lax.all_to_all(pieces, AXES, split_axis=0, concat_axis=0, tiled=True)  40.4 us
    all_to_all x4, starting transfers between devices, exchange(): return lax.all_to_all(pieces, AXES, split_axis=0, concat_axis=0, tiled=True)  15.3 us
    pallas_call x1, Pallas kernels, attention(): pl.pallas_call(functools.partial(attention_kernel, head_size, group, toge...  12.1 us
    ppermute x7, waiting for transfers between devices, swap(): lax.ppermute(value, AXES, [(device, device ^ mask) for device in range(de...  10.2 us
    ppermute x7, starting transfers between devices, swap(): lax.ppermute(value, AXES, [(device, device ^ mask) for device in range(de...  8.12 us
    pallas_call x1, Pallas kernels, project(): pl.pallas_call(project_kernel, out_shape=shaped((rows, width)), in_specs=...  4.6 us
  transfers between devices with their start and end apart: 11, of which 5 were waited for; matrix products, arithmetic and copies ran while one was open for 2% of the time, Pallas kernels for 8%

profile of v9, /device:TPU:0, one launch (start us, length us, event | category | flops | bytes accessed | tf_op | source)
XLA Modules:
  0.0 99.5 jit_solution(9516648896515464421)
XLA Ops:
  0.6 7.3 %all-to-all-start = ((bf16[32,8,512]{2,1,0:T(8,128)(2,1)}), bf16[32,8,512]{2,1,0:T(8,128)(2,1)S(1)}, u32[]{:S(2)}, u32[]{:S(2)}) async-start(bf16[32,8,512]{2,1,0:T(8,128)(2,1)} %bitcast.3), calls=%async_computation | async-start | bytes 524288 | tf_op jit(solution)/shard_map/all_to_all | solution.py:25
  7.9 0.7 compare_select_fusion
  8.6 0.1 copy.12
  8.7 0.1 reshape.116
  8.8 9.4 %all-to-all-done = bf16[32,8,512]{2,1,0:T(8,128)(2,1)S(1)} async-done(((bf16[32,8,512]{2,1,0:T(8,128)(2,1)}), bf16[32,8,512]{2,1,0:T(8,128)(2,1)S(1)}, u32[]{:S(2)}, u32[]{:S(2)}) %all-to-all-start) | async-done | bytes 262176 | tf_op jit(solution)/shard_map/all_to_all | solution.py:25
  18.2 1.5 %gather_fusion = bf16[96,8,512]{2,1,0:T(8,128)(2,1)} fusion(bf16[32,8,512]{2,1,0:T(8,128)(2,1)S(1)} %all-to-all-done, s32[1024]{0:T(1024)S(1)} %pad_clamp_fusion), kind=kCustom, calls=%fused_computation | custom fusion | bytes 1573248 | tf_op jit(solution)/shard_map/gather | solution.py:475
  19.8 0.0 copy-start
  19.8 2.8 %all-to-all-start.1 = ((bf16[32,3,8,512]{3,2,1,0:T(8,128)(2,1)}), bf16[32,3,8,512]{3,2,1,0:T(8,128)(2,1)S(1)}, u32[]{:S(2)}, u32[]{:S(2)}) async-start(bf16[32,3,8,512]{3,2,1,0:T(8,128)(2,1)} %bitcast.2), calls=%async_computation.1 | async-start | bytes 1572864 | tf_op jit(solution)/shard_map/all_to_all | solution.py:25
  22.5 4.6 %shard_map.95.packed_hbm = bf16[4352,512]{1,0:T(8,128)(2,1)} custom-call(bf16[256,512]{1,0:T(8,128)(2,1)} %feats_ref.1, bf16[256,512]{1,0:T(8,128)(2,1)} %grad_out_ref.1, bf16[512,512]{1,0:T(8,128)(2,1)} %w_query_ref.1, bf16[512,512]{1,0:T(8,128)(2,1)} %w_key_ref.1, bf16[512,512]{1,0:T(8,128)(2,1)} %w_value_ref.1, bf16[512,512]{1,0:T(8,128)(2,1)} %w_output_ref.1), custom_call_target="tpu_custom_call" | custom-call | flops 536870912 | bytes 6291456 | tf_op jit(solution)/shard_map/pallas_call | solution.py:80
  27.1 16.9 %all-to-all-done.1.arrived_ref = bf16[32,3,8,512]{3,2,1,0:T(8,128)(2,1)S(1)} async-done(((bf16[32,3,8,512]{3,2,1,0:T(8,128)(2,1)}), bf16[32,3,8,512]{3,2,1,0:T(8,128)(2,1)S(1)}, u32[]{:S(2)}, u32[]{:S(2)}) %all-to-all-start.1) | async-done | bytes 786464 | tf_op jit(solution)/shard_map/all_to_all | solution.py:25
  44.0 0.0 copy-done
  44.0 12.1 %shard_map.96 = (bf16[32,3,8,512]{3,2,1,0:T(8,128)(2,1)}, bf16[256,1024]{1,0:T(8,128)(2,1)S(1)}, bf16[512,256]{1,0:T(8,128)(2,1)S(1)}, bf16[16,256,128]{2,1,0:T(8,128)(2,1)S(1)}, bf16[16,256,128]{2,1,0:T(8,128)(2,1)}) custom-call(s32[1]{0:T(128)} %bitcast.me_ref, f32[8,256]{1,0:T(8,128)S(1)} %copy-done, ...), custom_call_target="tpu_custom_call" | custom-call | flops 10200547328 | bytes 8388608 | tf_op jit(solution)/shard_map/pallas_call | solution.py:313
  56.2 0.0 copy-start.1
  56.2 2.6 %all-to-all-start.2 = ((bf16[32,3,8,512]{3,2,1,0:T(8,128)(2,1)}), bf16[32,3,8,512]{3,2,1,0:T(8,128)(2,1)S(1)}, u32[]{:S(2)}, u32[]{:S(2)}) async-start(bf16[32,3,8,512]{3,2,1,0:T(8,128)(2,1)} %get-tuple-element.10), calls=%async_computation.2 | async-start | bytes 1572864 | tf_op jit(solution)/shard_map/all_to_all | solution.py:25
  58.9 0.2 collective-permute-start
  59.0 2.8 %collective-permute-done = bf16[16,256,128]{2,1,0:T(8,128)(2,1)S(1)} collective-permute-done((bf16[16,256,128]{2,1,0:T(8,128)(2,1)}, bf16[16,256,128]{2,1,0:T(8,128)(2,1)S(1)}, u32[]{:S(2)}, u32[]{:S(2)}) %collective-permute-start) | collective-permute-done | bytes 1048608 | tf_op jit(solution)/shard_map/ppermute | solution.py:412
  61.8 1.0 add_convert_fusion.3
  62.8 2.6 %collective-permute-start.3 = (bf16[4,256,128]{2,1,0:T(8,128)(2,1)}, bf16[4,256,128]{2,1,0:T(8,128)(2,1)S(1)}, u32[]{:S(2)}, u32[]{:S(2)}) collective-permute-start(bf16[4,256,128]{2,1,0:T(8,128)(2,1)} %get-tuple-element.15), channel_id=1, source_target_pairs={{0,18},{1,19},{2,16},{3,17},{4,22},{5,23},{6,20},{7,21},{8,26},{9,... | collective-permute-start | bytes 786440 | tf_op jit(solution)/shard_map/ppermute | solution.py:412
  65.3 0.5 collective-permute-start.2
  65.9 0.4 collective-permute-start.1
  66.3 0.0 copy-done.1
  66.3 0.1 copy.13.partners_ref
  66.4 14.1 %all-to-all-done.2.returned_ref = bf16[32,3,8,512]{3,2,1,0:T(8,128)(2,1)S(1)} async-done(((bf16[32,3,8,512]{3,2,1,0:T(8,128)(2,1)}), bf16[32,3,8,512]{3,2,1,0:T(8,128)(2,1)S(1)}, u32[]{:S(2)}, u32[]{:S(2)}) %all-to-all-start.2) | async-done | bytes 786464 | tf_op jit(solution)/shard_map/all_to_all | solution.py:25
  80.5 1.6 %shard_map.98 = bf16[32,8,512]{2,1,0:T(8,128)(2,1)} custom-call(s32[32,3]{1,0:T(8,128)S(1)} %copy.13.partners_ref, bf16[32,3,8,512]{3,2,1,0:T(8,128)(2,1)S(1)} %all-to-all-done.2.returned_ref), custom_call_target="tpu_custom_call" | custom-call | tf_op jit(solution)/shard_map/pallas_call | solution.py:439
  82.1 2.6 %all-to-all-start.3 = ((bf16[32,8,512]{2,1,0:T(8,128)(2,1)}), bf16[32,8,512]{2,1,0:T(8,128)(2,1)S(1)}, u32[]{:S(2)}, u32[]{:S(2)}) async-start(bf16[32,8,512]{2,1,0:T(8,128)(2,1)} %shard_map.98), calls=%async_computation.3 | async-start | bytes 524288 | tf_op jit(solution)/shard_map/all_to_all | solution.py:25
  84.7 0.0 collective-permute-done.3
  84.7 0.0 collective-permute-done.2
  84.7 0.0 collective-permute-done.1
  84.7 0.1 add_convert_fusion.4
  84.9 2.7 %collective-permute-start.4 = (bf16[1,256,128]{2,1,0:T(8,128)(2,1)S(1)}, bf16[1,256,128]{2,1,0:T(8,128)(2,1)S(1)}, u32[]{:S(2)}, u32[]{:S(2)}) collective-permute-start(bf16[1,256,128]{2,1,0:T(8,128)(2,1)S(1)} %get-tuple-element.20), channel_id=1, source_target_pairs={{0,8},{1,9},{2,10},{3,11},{4,12},{5,13},{6,14},{7,15},{8,0},{9,1},... | collective-permute-start | bytes 196616 | tf_op jit(solution)/shard_map/ppermute | solution.py:412
  87.6 1.5 %collective-permute-start.5 = (bf16[1,256,128]{2,1,0:T(8,128)(2,1)S(1)}, bf16[1,256,128]{2,1,0:T(8,128)(2,1)S(1)}, u32[]{:S(2)}, u32[]{:S(2)}) collective-permute-start(bf16[1,256,128]{2,1,0:T(8,128)(2,1)S(1)} %get-tuple-element.19), channel_id=1, source_target_pairs={{0,4},{1,5},{2,6},{3,7},{4,0},{5,1},{6,2},{7,3},{8,12},{9,13},{10,... | collective-permute-start | bytes 196616 | tf_op jit(solution)/shard_map/ppermute | solution.py:412
  89.1 0.2 collective-permute-start.6
  89.3 2.0 %shard_map.97.own_ref = f32[256,512]{1,0:T(8,128)S(1)} custom-call(bf16[256,1024]{1,0:T(8,128)(2,1)S(1)} %get-tuple-element.8.both_ref, bf16[512,256]{1,0:T(8,128)(2,1)S(1)} %get-tuple-element.9.grad_query_t_ref, bf16[4352,512]{1,0:T(8,128)(2,1)} %shard_map.95.packed_hbm), custom_call_target="tpu_custom_call" | custom-call | flops 402653184 | bytes 2883584 | tf_op jit(solution)/shard_map/pallas_call | solution.py:376
  91.3 7.4 %collective-permute-done.4.refs_0_ = bf16[1,256,128]{2,1,0:T(8,128)(2,1)S(1)} collective-permute-done((bf16[1,256,128]{2,1,0:T(8,128)(2,1)S(1)}, bf16[1,256,128]{2,1,0:T(8,128)(2,1)S(1)}, u32[]{:S(2)}, u32[]{:S(2)}) %collective-permute-start.4) | collective-permute-done | bytes 65568 | tf_op jit(solution)/shard_map/ppermute | solution.py:412
  98.7 0.0 collective-permute-done.5.refs_1_
  98.7 0.0 collective-permute-done.6.refs_2_
  98.7 0.0 all-to-all-done.3.back_ref
  98.7 0.8 shard_map.99
  (1 shorter events, 0.0 us)
Async XLA Ops:
  0.6 17.6 %all-to-all-start = ((bf16[32,8,512]{2,1,0:T(8,128)(2,1)}), bf16[32,8,512]{2,1,0:T(8,128)(2,1)S(1)}, u32[]{:S(2)}, u32[]{:S(2)}) async-start(bf16[32,8,512]{2,1,0:T(8,128)(2,1)} %bitcast.3), calls=%async_computation | async-start | bytes 524288 | tf_op jit(solution)/shard_map/all_to_all | solution.py:25
  19.8 24.3 %copy-start = (f32[8,256]{1,0:T(8,128)S(1)}, f32[8,256]{1,0:T(8,128)}, u32[]{:S(2)}) copy-start(f32[8,256]{1,0:T(8,128)} %lse_hbm.1) | copy-start | bytes 24580
  19.8 24.3 %all-to-all-start.1 = ((bf16[32,3,8,512]{3,2,1,0:T(8,128)(2,1)}), bf16[32,3,8,512]{3,2,1,0:T(8,128)(2,1)S(1)}, u32[]{:S(2)}, u32[]{:S(2)}) async-start(bf16[32,3,8,512]{3,2,1,0:T(8,128)(2,1)} %bitcast.2), calls=%async_computation.1 | async-start | bytes 1572864 | tf_op jit(solution)/shard_map/all_to_all | solution.py:25
  56.2 10.1 %copy-start.1 = (s32[32,3]{0,1:T(4,128)S(1)}, s32[32,3]{0,1:T(4,128)}, u32[]{:S(2)}) copy-start(s32[32,3]{0,1:T(4,128)} %param.15) | copy-start | bytes 1156
  56.2 24.3 %all-to-all-start.2 = ((bf16[32,3,8,512]{3,2,1,0:T(8,128)(2,1)}), bf16[32,3,8,512]{3,2,1,0:T(8,128)(2,1)S(1)}, u32[]{:S(2)}, u32[]{:S(2)}) async-start(bf16[32,3,8,512]{3,2,1,0:T(8,128)(2,1)} %get-tuple-element.10), calls=%async_computation.2 | async-start | bytes 1572864 | tf_op jit(solution)/shard_map/all_to_all | solution.py:25
  58.9 2.9 %collective-permute-start = (bf16[16,256,128]{2,1,0:T(8,128)(2,1)}, bf16[16,256,128]{2,1,0:T(8,128)(2,1)S(1)}, u32[]{:S(2)}, u32[]{:S(2)}) collective-permute-start(bf16[16,256,128]{2,1,0:T(8,128)(2,1)} %get-tuple-element.12), channel_id=1, source_target_pairs={{0,1},{1,0},{2,3},{3,2},{4,5},{5,4},{6,7},{7,6},{8,9},{9,8},{10,11... | collective-permute-start | bytes 3145736 | tf_op jit(solution)/shard_map/ppermute | solution.py:412
  62.8 21.9 %collective-permute-start.3 = (bf16[4,256,128]{2,1,0:T(8,128)(2,1)}, bf16[4,256,128]{2,1,0:T(8,128)(2,1)S(1)}, u32[]{:S(2)}, u32[]{:S(2)}) collective-permute-start(bf16[4,256,128]{2,1,0:T(8,128)(2,1)} %get-tuple-element.15), channel_id=1, source_target_pairs={{0,18},{1,19},{2,16},{3,17},{4,22},{5,23},{6,20},{7,21},{8,26},{9,... | collective-permute-start | bytes 786440 | tf_op jit(solution)/shard_map/ppermute | solution.py:412
  65.3 19.3 %collective-permute-start.2 = (bf16[4,256,128]{2,1,0:T(8,128)(2,1)S(1)}, bf16[4,256,128]{2,1,0:T(8,128)(2,1)S(1)}, u32[]{:S(2)}, u32[]{:S(2)}) collective-permute-start(bf16[4,256,128]{2,1,0:T(8,128)(2,1)S(1)} %get-tuple-element.16), channel_id=1, source_target_pairs={{0,2},{1,3},{2,0},{3,1},{4,6},{5,7},{6,4},{7,5},{8,10},{9,11},{10,... | collective-permute-start | bytes 786440 | tf_op jit(solution)/shard_map/ppermute | solution.py:412
  65.9 18.8 %collective-permute-start.1 = (bf16[4,256,128]{2,1,0:T(8,128)(2,1)S(1)}, bf16[4,256,128]{2,1,0:T(8,128)(2,1)S(1)}, u32[]{:S(2)}, u32[]{:S(2)}) collective-permute-start(bf16[4,256,128]{2,1,0:T(8,128)(2,1)S(1)} %get-tuple-element.17), channel_id=1, source_target_pairs={{0,16},{1,17},{2,18},{3,19},{4,20},{5,21},{6,22},{7,23},{8,24},{9,... | collective-permute-start | bytes 786440 | tf_op jit(solution)/shard_map/ppermute | solution.py:412
  82.1 16.7 %all-to-all-start.3 = ((bf16[32,8,512]{2,1,0:T(8,128)(2,1)}), bf16[32,8,512]{2,1,0:T(8,128)(2,1)S(1)}, u32[]{:S(2)}, u32[]{:S(2)}) async-start(bf16[32,8,512]{2,1,0:T(8,128)(2,1)} %shard_map.98), calls=%async_computation.3 | async-start | bytes 524288 | tf_op jit(solution)/shard_map/all_to_all | solution.py:25
  84.9 13.9 %collective-permute-start.4 = (bf16[1,256,128]{2,1,0:T(8,128)(2,1)S(1)}, bf16[1,256,128]{2,1,0:T(8,128)(2,1)S(1)}, u32[]{:S(2)}, u32[]{:S(2)}) collective-permute-start(bf16[1,256,128]{2,1,0:T(8,128)(2,1)S(1)} %get-tuple-element.20), channel_id=1, source_target_pairs={{0,8},{1,9},{2,10},{3,11},{4,12},{5,13},{6,14},{7,15},{8,0},{9,1},... | collective-permute-start | bytes 196616 | tf_op jit(solution)/shard_map/ppermute | solution.py:412
  87.6 11.2 %collective-permute-start.5 = (bf16[1,256,128]{2,1,0:T(8,128)(2,1)S(1)}, bf16[1,256,128]{2,1,0:T(8,128)(2,1)S(1)}, u32[]{:S(2)}, u32[]{:S(2)}) collective-permute-start(bf16[1,256,128]{2,1,0:T(8,128)(2,1)S(1)} %get-tuple-element.19), channel_id=1, source_target_pairs={{0,4},{1,5},{2,6},{3,7},{4,0},{5,1},{6,2},{7,3},{8,12},{9,13},{10,... | collective-permute-start | bytes 196616 | tf_op jit(solution)/shard_map/ppermute | solution.py:412
  89.1 9.6 %collective-permute-start.6 = (bf16[1,256,128]{2,1,0:T(8,128)(2,1)S(1)}, bf16[1,256,128]{2,1,0:T(8,128)(2,1)S(1)}, u32[]{:S(2)}, u32[]{:S(2)}) collective-permute-start(bf16[1,256,128]{2,1,0:T(8,128)(2,1)S(1)} %get-tuple-element.18), channel_id=1, source_target_pairs={{0,12},{1,13},{2,14},{3,15},{4,8},{5,9},{6,10},{7,11},{8,4},{9,5},... | collective-permute-start | bytes 196616 | tf_op jit(solution)/shard_map/ppermute | solution.py:412
